TPU v7x, 32 devices: a whole 2x2x4 slice. The times are simulated.
32 devices in a mesh: dp: 4 (over y, core), seq: 8 (over z, x).
Axes of the slice: x: 2, y: 2, z: 4, core: 2. Of those that a mesh axis runs over, the one named last changes fastest.
Arguments:
- tokens: bfloat16 [8, 512, 2048], P('dp', 'seq'), may hold values from -6 to 6
- cotangent: bfloat16 [8, 512, 2048], P('dp', 'seq'), may hold values from -6 to 6
- segment_ids: int32 [8, 512], P('dp', 'seq'), may hold values from 0 to 7, as said below
- doc_positions: int32 [8, 512], P('dp', 'seq'), may hold values from 0 to 504, as said below
- in_weight: float32 [2048, 17408], P(('dp', 'seq')), may hold values from -0.125 to 0.125
- in_first: float32 [2048, 17408], P(('dp', 'seq'))
- in_second: float32 [2048, 17408], P(('dp', 'seq'))
- in_average: float32 [2048, 17408], P(('dp', 'seq')), may hold values from -0.125 to 0.125
- out_weight: float32 [7680, 2048], P(('dp', 'seq'))
- out_first: float32 [7680, 2048], P(('dp', 'seq'))
- out_second: float32 [7680, 2048], P(('dp', 'seq'))
- out_average: float32 [7680, 2048], P(('dp', 'seq'))
- small_params: float32 [2048, 5], P(('dp', 'seq'))
- small_first: float32 [2048, 5], P(('dp', 'seq'))
- small_second: float32 [2048, 5], P(('dp', 'seq'))
- small_average: float32 [2048, 5], P(('dp', 'seq'))
Outputs:
- output: bfloat16 [8, 512, 2048], P('dp', 'seq')
- input_grad: float32 [8, 512, 2048], P('dp', 'seq')
- new_in_weight: float32 [2048, 17408], P(('dp', 'seq'))
- new_in_second: float32 [2048, 17408], P(('dp', 'seq'))
- new_in_average: float32 [2048, 17408], P(('dp', 'seq'))
- new_out_weight: float32 [7680, 2048], P(('dp', 'seq'))
- new_out_second: float32 [7680, 2048], P(('dp', 'seq'))
- new_out_average: float32 [7680, 2048], P(('dp', 'seq'))
- new_small_params: float32 [2048, 5], P(('dp', 'seq'))
- new_small_second: float32 [2048, 5], P(('dp', 'seq'))
- new_small_average: float32 [2048, 5], P(('dp', 'seq'))
- small_grad: float32 [2048, 5], P(('dp', 'seq'))
- in_grad: float32 [2048, 17408], P(('dp', 'seq'))
- out_grad: float32 [7680, 2048], P(('dp', 'seq'))
Inputs may be any that keep to these rules, and one draw needn't show every extreme that they name: `segment_ids`: within each row the ids never fall, start at 0 and take every value up to 7. `doc_positions`: 0 at a document's first token of a row, rising by one along the document; row 0's longest document reaches position 504.
All inputs are finite; a program needn't handle non-finite values.
Results may differ from a plain program's by a relative error of at most 0.025.
Values may be sent and summed in bfloat16 or wider, within the bound.
A program may use at most 448 MiB of HBM per device.

v0:
```python
import jax
import jax.numpy as jnp
from jax import lax
from jax.sharding import PartitionSpec as P

HEADS = 32
ROT = 16
STEP = 2


beta_one = 0.9
adam_eps = 1e-08
matrix_rate = 0.001
small_rate = 0.01
weight_decay = 0.1
norm_eps = 1e-05
rope_base = 10000.0
neg_large = -1e30


def rope_tables(positions, rot_dims):
    half_rot = rot_dims // 2
    inv_freq = rope_base ** (-2.0 * jnp.arange(half_rot, dtype=jnp.float32) / rot_dims)
    angles = positions.astype(jnp.float32)[..., None] * inv_freq
    return (jnp.cos(angles)[..., None, :], jnp.sin(angles)[..., None, :])


def apply_rope(field_in, cosine_tab, sine_tab, rot_dims):
    half_rot = rot_dims // 2
    low_half = field_in[..., :half_rot]
    high_half = field_in[..., half_rot:rot_dims]
    return jnp.concatenate(
        [
            low_half * cosine_tab - high_half * sine_tab,
            high_half * cosine_tab + low_half * sine_tab,
            field_in[..., rot_dims:],
        ],
        axis=-1,
    )


def undo_rope(grad_in, cosine_tab, sine_tab, rot_dims):
    half_rot = rot_dims // 2
    low_half = grad_in[..., :half_rot]
    high_half = grad_in[..., half_rot:rot_dims]
    return jnp.concatenate(
        [
            low_half * cosine_tab + high_half * sine_tab,
            high_half * cosine_tab - low_half * sine_tab,
            grad_in[..., rot_dims:],
        ],
        axis=-1,
    )


def visible(query_seg, key_seg, query_pos, key_pos):
    same_doc = query_seg[:, :, None] == key_seg[:, None, :]
    causal = key_pos[None, :] <= query_pos[:, None]
    return (same_doc & causal[None])[:, None]


def to_tokens(head_major):
    return jnp.transpose(head_major, (0, 2, 1, 3))


def adam_update(weight, first, second, average, gradient, rate, decay_rate):
    beta_two = 1.0 - STEP ** (-0.8)
    average_keep = min(0.999, (1.0 + STEP) / (10.0 + STEP))
    first_new = beta_one * first + (1.0 - beta_one) * gradient
    second_new = beta_two * second + (1.0 - beta_two) * gradient * gradient
    moment_hat = beta_one * first_new / (1.0 - beta_one ** (STEP + 1)) + (
        1.0 - beta_one
    ) * gradient / (1.0 - beta_one**STEP)
    weight_new = weight - rate * (
        moment_hat / (jnp.sqrt(second_new) + adam_eps) + decay_rate * weight
    )
    average_new = average_keep * average + (1.0 - average_keep) * weight_new
    return (weight_new, second_new, average_new)


def per_device(
    tokens,
    cotangent,
    segment_ids,
    doc_positions,
    in_weight,
    in_first,
    in_second,
    in_average,
    out_weight,
    out_first,
    out_second,
    out_average,
    small_params,
    small_first,
    small_second,
    small_average,
):
    rows_here, row_tokens, model_width = tokens.shape
    head_count = HEADS
    head_size = model_width // head_count
    score_scale = head_size ** (-0.5)
    all_tokens = rows_here * row_tokens
    wide_in = in_weight.shape[1]
    ffn_width = (wide_in - 3 * model_width) // 2
    shape_heads = (rows_here, row_tokens, head_count, head_size)
    own_places = lax.axis_index("seq") * row_tokens + jnp.arange(row_tokens)
    flat_in = tokens.astype(jnp.float32).reshape(all_tokens, model_width)
    centered = flat_in - jnp.mean(flat_in, axis=-1, keepdims=True)
    inv_std = lax.rsqrt(jnp.mean(centered * centered, axis=-1, keepdims=True) + norm_eps)
    normed = centered * inv_std
    in_low = in_weight.astype(jnp.bfloat16)
    out_low = out_weight.astype(jnp.bfloat16)
    small_low = small_params.astype(jnp.bfloat16)
    w_piece = lax.all_gather(in_low, ("dp", "seq"), axis=0, tiled=True)
    s_piece = lax.all_gather(small_low, ("dp", "seq"), axis=0, tiled=True)
    columns = normed
    s_float = s_piece.astype(jnp.float32)
    h_piece = (columns * s_float[:, 0] + s_float[:, 1]).astype(jnp.bfloat16)
    proj_acc = jnp.dot(h_piece, w_piece, preferred_element_type=jnp.float32)
    norm_gain = s_float[:, 0]
    qkv_bias = s_float[:, 2:5].T.reshape(3 * model_width)
    qkv_full = proj_acc[:, : 3 * model_width] + qkv_bias
    gate_pre = proj_acc[:, 3 * model_width : 3 * model_width + ffn_width]
    up_pre = proj_acc[:, 3 * model_width + ffn_width :]
    cosine_tab, sine_tab = rope_tables(doc_positions, ROT)
    query_low = apply_rope(
        qkv_full[:, :model_width].reshape(shape_heads), cosine_tab, sine_tab, ROT
    ).astype(jnp.bfloat16)
    key_low = apply_rope(
        qkv_full[:, model_width : 2 * model_width].reshape(shape_heads), cosine_tab, sine_tab, ROT
    ).astype(jnp.bfloat16)
    value_low = qkv_full[:, 2 * model_width :].reshape(shape_heads).astype(jnp.bfloat16)
    seg_low = segment_ids.astype(jnp.bfloat16)
    seg_own = segment_ids.astype(jnp.float32)
    key_flat = key_low.reshape(rows_here, row_tokens, model_width)
    value_flat = value_low.reshape(rows_here, row_tokens, model_width)
    attend_init = (
        jnp.full((rows_here, head_count, row_tokens), neg_large, jnp.float32),
        jnp.zeros((rows_here, head_count, row_tokens), jnp.float32),
        jnp.zeros((rows_here, head_count, row_tokens, head_size), jnp.float32),
    )
    key_piece = lax.all_gather(key_flat, "seq", axis=1, tiled=True)
    value_piece = lax.all_gather(value_flat, "seq", axis=1, tiled=True)
    seg_piece = lax.all_gather(seg_low, "seq", axis=1, tiled=True)
    turn_count = key_piece.shape[1] // row_tokens

    def attend_one_turn(turn_index, inner_state):
        offset = turn_index * row_tokens
        key_blk = lax.dynamic_slice_in_dim(key_piece, offset, row_tokens, 1).reshape(shape_heads)
        value_blk = lax.dynamic_slice_in_dim(value_piece, offset, row_tokens, 1).reshape(
            shape_heads
        )
        seg_blk = lax.dynamic_slice_in_dim(seg_piece, offset, row_tokens, 1).astype(jnp.float32)
        key_mask = visible(seg_own, seg_blk, own_places, offset + jnp.arange(row_tokens))
        running_top, running_sum, weighted = inner_state
        scores = (
            jnp.einsum("rqhe,rkhe->rhqk", query_low, key_blk, preferred_element_type=jnp.float32)
            * score_scale
        )
        scores = jnp.where(key_mask, scores, neg_large)
        new_top = jnp.maximum(running_top, jnp.max(scores, axis=-1))
        weights = jnp.where(key_mask, jnp.exp(scores - new_top[..., None]), 0.0)
        factor = jnp.exp(running_top - new_top)
        running_sum = running_sum * factor + jnp.sum(weights, axis=-1)
        weighted = weighted * factor[..., None] + jnp.einsum(
            "rhqk,rkhe->rhqe",
            weights.astype(jnp.bfloat16),
            value_blk,
            preferred_element_type=jnp.float32,
        )
        return (new_top, running_sum, weighted)

    running_top, running_sum, weighted = lax.fori_loop(0, turn_count, attend_one_turn, attend_init)
    attended = weighted / running_sum[..., None]
    log_total = running_top + jnp.log(running_sum)
    attended_low = to_tokens(attended).reshape(all_tokens, model_width).astype(jnp.bfloat16)
    gate_sig = jax.nn.sigmoid(gate_pre)
    activated = gate_pre * gate_sig * up_pre
    joined = jnp.concatenate([attended_low, activated.astype(jnp.bfloat16)], axis=1)
    columns = joined
    branch_sum = jnp.dot(
        columns,
        lax.all_gather(out_low, ("dp", "seq"), axis=0, tiled=True),
        preferred_element_type=jnp.float32,
    )
    output = (flat_in + branch_sum).astype(jnp.bfloat16).reshape(rows_here, row_tokens, model_width)
    grad_out = cotangent.reshape(all_tokens, model_width)
    d_joined = lax.dot_general(
        grad_out,
        lax.all_gather(out_low, ("dp", "seq"), axis=0, tiled=True),
        (((1,), (1,)), ((), ())),
        preferred_element_type=jnp.float32,
    )
    d_joined = d_joined.astype(jnp.bfloat16)
    columns = joined
    out_grad = lax.psum_scatter(
        lax.dot_general(
            columns, grad_out, (((0,), (0,)), ((), ())), preferred_element_type=jnp.float32
        ),
        ("dp", "seq"),
        scatter_dimension=0,
        tiled=True,
    )
    d_attended = d_joined[:, :model_width].reshape(shape_heads)
    d_act = d_joined[:, model_width:].astype(jnp.float32)
    d_gate = d_act * up_pre * gate_sig * (1.0 + gate_pre * (1.0 - gate_sig))
    d_up = d_act * gate_pre * gate_sig
    out_dot = jnp.einsum("rqhe,rhqe->rhq", d_attended.astype(jnp.float32), attended)
    grad_zero = jnp.zeros((rows_here, head_count, row_tokens, head_size), jnp.float32)
    query_key_piece = lax.all_gather(key_flat, "seq", axis=1, tiled=True)
    query_value_piece = lax.all_gather(value_flat, "seq", axis=1, tiled=True)
    query_seg_piece = lax.all_gather(seg_low, "seq", axis=1, tiled=True)
    turn_count = query_key_piece.shape[1] // row_tokens

    def query_one_turn(turn_index, inner_state):
        offset = turn_index * row_tokens
        key_blk = lax.dynamic_slice_in_dim(query_key_piece, offset, row_tokens, 1).reshape(
            shape_heads
        )
        value_blk = lax.dynamic_slice_in_dim(query_value_piece, offset, row_tokens, 1).reshape(
            shape_heads
        )
        seg_blk = lax.dynamic_slice_in_dim(query_seg_piece, offset, row_tokens, 1).astype(
            jnp.float32
        )
        key_mask = visible(seg_own, seg_blk, own_places, offset + jnp.arange(row_tokens))
        scores = (
            jnp.einsum("rqhe,rkhe->rhqk", query_low, key_blk, preferred_element_type=jnp.float32)
            * score_scale
        )
        weights = jnp.where(key_mask, jnp.exp(scores - log_total[..., None]), 0.0)
        d_prob = jnp.einsum(
            "rqhe,rkhe->rhqk", d_attended, value_blk, preferred_element_type=jnp.float32
        )
        d_score = (weights * (d_prob - out_dot[..., None])).astype(jnp.bfloat16)
        return (
            inner_state
            + jnp.einsum("rhqk,rkhe->rhqe", d_score, key_blk, preferred_element_type=jnp.float32)
            * score_scale
        )

    d_query = lax.fori_loop(0, turn_count, query_one_turn, grad_zero)
    row_stats = jnp.concatenate(
        [jnp.transpose(log_total, (0, 2, 1)), jnp.transpose(out_dot, (0, 2, 1))], axis=2
    )
    stat_high = row_stats.astype(jnp.bfloat16)
    stat_low = (row_stats - stat_high.astype(jnp.float32)).astype(jnp.bfloat16)
    query_flat = query_low.reshape(rows_here, row_tokens, model_width)
    d_att_flat = d_attended.reshape(rows_here, row_tokens, model_width)
    query_piece = lax.all_gather(query_flat, "seq", axis=1, tiled=True)
    dout_piece = lax.all_gather(d_att_flat, "seq", axis=1, tiled=True)
    high_piece = lax.all_gather(stat_high, "seq", axis=1, tiled=True)
    low_piece = lax.all_gather(stat_low, "seq", axis=1, tiled=True)
    key_seg_piece = lax.all_gather(seg_low, "seq", axis=1, tiled=True)
    turn_count = query_piece.shape[1] // row_tokens

    def key_one_turn(turn_index, inner_state):
        offset = turn_index * row_tokens
        query_blk = lax.dynamic_slice_in_dim(query_piece, offset, row_tokens, 1).reshape(
            shape_heads
        )
        dout_blk = lax.dynamic_slice_in_dim(dout_piece, offset, row_tokens, 1).reshape(shape_heads)
        stat_blk = lax.dynamic_slice_in_dim(high_piece, offset, row_tokens, 1).astype(
            jnp.float32
        ) + lax.dynamic_slice_in_dim(low_piece, offset, row_tokens, 1).astype(jnp.float32)
        lse_blk = jnp.transpose(stat_blk[..., :head_count], (0, 2, 1))
        dot_blk = jnp.transpose(stat_blk[..., head_count:], (0, 2, 1))
        seg_blk = lax.dynamic_slice_in_dim(key_seg_piece, offset, row_tokens, 1).astype(jnp.float32)
        key_mask = visible(seg_blk, seg_own, offset + jnp.arange(row_tokens), own_places)
        d_key, d_value = inner_state
        scores = (
            jnp.einsum("rqhe,rkhe->rhqk", query_blk, key_low, preferred_element_type=jnp.float32)
            * score_scale
        )
        weights = jnp.where(key_mask, jnp.exp(scores - lse_blk[..., None]), 0.0)
        d_value = d_value + jnp.einsum(
            "rhqk,rqhe->rhke",
            weights.astype(jnp.bfloat16),
            dout_blk,
            preferred_element_type=jnp.float32,
        )
        d_prob = jnp.einsum(
            "rqhe,rkhe->rhqk", dout_blk, value_low, preferred_element_type=jnp.float32
        )
        d_score = (weights * (d_prob - dot_blk[..., None])).astype(jnp.bfloat16)
        d_key = (
            d_key
            + jnp.einsum("rhqk,rqhe->rhke", d_score, query_blk, preferred_element_type=jnp.float32)
            * score_scale
        )
        return (d_key, d_value)

    d_key, d_value = lax.fori_loop(0, turn_count, key_one_turn, (grad_zero, grad_zero))
    d_query_tok = undo_rope(to_tokens(d_query), cosine_tab, sine_tab, ROT).reshape(
        all_tokens, model_width
    )
    d_key_tok = undo_rope(to_tokens(d_key), cosine_tab, sine_tab, ROT).reshape(
        all_tokens, model_width
    )
    d_value_tok = to_tokens(d_value).reshape(all_tokens, model_width)
    d_proj = jnp.concatenate([d_query_tok, d_key_tok, d_value_tok, d_gate, d_up], axis=1).astype(
        jnp.bfloat16
    )
    d_hidden = lax.dot_general(
        d_proj,
        lax.all_gather(in_low, ("dp", "seq"), axis=0, tiled=True),
        (((1,), (1,)), ((), ())),
        preferred_element_type=jnp.float32,
    )
    columns = h_piece
    in_grad = lax.psum_scatter(
        lax.dot_general(
            columns, d_proj, (((0,), (0,)), ((), ())), preferred_element_type=jnp.float32
        ),
        ("dp", "seq"),
        scatter_dimension=0,
        tiled=True,
    )
    gain_grad = jnp.sum(d_hidden * normed, axis=0)
    shift_grad = jnp.sum(d_hidden, axis=0)
    bias_grad = (
        jnp.sum(d_proj[:, : 3 * model_width].astype(jnp.float32), axis=0).reshape(3, model_width).T
    )
    small_term = jnp.concatenate([gain_grad[:, None], shift_grad[:, None], bias_grad], axis=1)
    small_grad = lax.psum_scatter(small_term, ("dp", "seq"), scatter_dimension=0, tiled=True)
    d_normed = d_hidden * norm_gain
    input_grad = grad_out.astype(jnp.float32) + inv_std * (
        d_normed
        - jnp.mean(d_normed, axis=-1, keepdims=True)
        - normed * jnp.mean(d_normed * normed, axis=-1, keepdims=True)
    )
    input_grad = input_grad.reshape(rows_here, row_tokens, model_width)
    in_new = adam_update(
        in_weight, in_first, in_second, in_average, in_grad, matrix_rate, weight_decay
    )
    out_new = adam_update(
        out_weight, out_first, out_second, out_average, out_grad, matrix_rate, weight_decay
    )
    small_new = adam_update(
        small_params, small_first, small_second, small_average, small_grad, small_rate, 0.0
    )
    return (
        output,
        input_grad,
        in_new[0],
        in_new[1],
        in_new[2],
        out_new[0],
        out_new[1],
        out_new[2],
        small_new[0],
        small_new[1],
        small_new[2],
        small_grad,
        in_grad,
        out_grad,
    )


def solution(mesh):
    return jax.shard_map(
        per_device,
        mesh=mesh,
        in_specs=(
            P("dp", "seq", None),
            P("dp", "seq", None),
            P("dp", "seq"),
            P("dp", "seq"),
            P(("dp", "seq"), None),
            P(("dp", "seq"), None),
            P(("dp", "seq"), None),
            P(("dp", "seq"), None),
            P(("dp", "seq"), None),
            P(("dp", "seq"), None),
            P(("dp", "seq"), None),
            P(("dp", "seq"), None),
            P(("dp", "seq"), None),
            P(("dp", "seq"), None),
            P(("dp", "seq"), None),
            P(("dp", "seq"), None),
        ),
        out_specs=(
            P("dp", "seq", None),
            P("dp", "seq", None),
            P(("dp", "seq"), None),
            P(("dp", "seq"), None),
            P(("dp", "seq"), None),
            P(("dp", "seq"), None),
            P(("dp", "seq"), None),
            P(("dp", "seq"), None),
            P(("dp", "seq"), None),
            P(("dp", "seq"), None),
            P(("dp", "seq"), None),
            P(("dp", "seq"), None),
            P(("dp", "seq"), None),
            P(("dp", "seq"), None),
        ),
        check_vma=False,
    )
```

profile of v0, /device:TPU:11, one launch (start us, length us, event | category | flops | bytes accessed | tf_op | source)
XLA Modules:
  0.0 4852.1 jit_solution(3374781583388868953)
XLA Ops:
  7.2 3.8 convert_element_type.158
  13.8 61.1 %all-gather.1 = bf16[32,64,5]{1,2,0:T(8,128)(2,1)S(1)} all-gather(bf16[1,64,5]{1,2,0:T(8,128)(2,1)S(1)} %convert_bitcast_fusion.2), channel_id=1, replica_groups=mesh['dp'=4,'seq'=8] {'dp','seq'}, dimensions={0}, use_global_device_ids=true | all-gather | bytes 21120 | tf_op jit(solution)/shard_map/all_gather | solution.py:116
  76.5 311.4 %all-gather.9.cloned.1.call-done = bf16[2048,17408]{1,0:T(8,128)(2,1)} async-done(((bf16[64,17408]{1,0:T(8,128)(2,1)}), bf16[2048,17408]{1,0:T(8,128)(2,1)}) %all-gather.9.cloned.1.call-update) | async-done | bytes 71303184 | tf_op jit(solution)/shard_map/all_gather | solution.py:115
  387.9 28.8 fusion.69
  425.7 3.7 fusion.66
  429.4 6.9 multiply_subtract_fusion.1
  439.9 2.8 convert_element_type.161
  445.0 129.5 %all-gather.15.cloned.1.call-done = bf16[7680,2048]{1,0:T(8,128)(2,1)} async-done(((bf16[240,2048]{1,0:T(8,128)(2,1)}), bf16[7680,2048]{1,0:T(8,128)(2,1)}) %all-gather.15.cloned.1.call-update) | async-done | bytes 31457296 | tf_op jit(solution)/shard_map/all_gather | solution.py:184
  574.5 15.5 convolution_convert_fusion
  592.3 13.0 all-gather
  622.4 4.6 multiply_convert_fusion.1
  627.1 20.1 all-gather.11.cloned.1.call-done
  647.2 73.7 %all-gather.13.cloned.1.call-done = bf16[2,512,2048]{2,1,0:T(8,128)(2,1)} async-done(((bf16[2,64,2048]{2,1,0:T(8,128)(2,1)}), bf16[2,512,2048]{2,1,0:T(8,128)(2,1)}) %all-gather.13.cloned.1.call-update) | async-done | bytes 4194320 | tf_op jit(solution)/shard_map/all_gather | solution.py:144
  720.9 94.3 %while.48 = (s32[]{:T(128)}, f32[2,32,64]{2,1,0:T(8,128)S(1)}, f32[2,32,64]{2,1,0:T(8,128)S(1)}, f32[2,32,64,64]{3,2,1,0:T(8,128)}, f32[2,64]{1,0:T(2,128)S(1)},...) while((s32[]{:T(128)}, f32[2,32,64]{2,1,0:T(8,128)S(1)}, ...), condition=%wide.region_5.6_spmd.clone, body=%wide.region_2.5_spmd.clone.sunk | while | flops 71344384 | bytes 11316183 | solution.py:174
  740.3 3.6 fusion.116
  752.2 3.6 fusion.116
  764.1 3.6 fusion.116
  776.0 3.6 fusion.116
  787.9 3.6 fusion.116
  799.7 3.6 fusion.116
  811.6 3.6 fusion.116
  815.5 4.6 multiply_reduce_fusion
  820.1 104.4 %while.49 = (s32[]{:T(128)}, f32[2,32,64,64]{3,2,1,0:T(8,128)}, f32[2,64]{1,0:T(2,128)S(1)}, bf16[2,512]{1,0:T(2,128)(2,1)S(1)}, bf16[2,512,2048]{2,1,0:T(8,128)...) while((s32[]{:T(128)}, f32[2,32,64,64]{3,2,1,0:T(8,128)}, ...), condition=%wide.region_7.8_spmd.clone, body=%wide.region_6.7_spmd.clone.sunk | while | flops 103043328 | bytes 11070429 | solution.py:243
  828.2 4.3 select_add_fusion.6
  840.7 5.0 select_add_fusion.6
  850.8 2.8 reshape.324
  853.8 5.0 select_add_fusion.6
  867.0 5.0 select_add_fusion.6
  880.1 5.0 select_add_fusion.6
  893.2 5.0 select_add_fusion.6
  906.3 5.0 select_add_fusion.6
  919.4 5.0 select_add_fusion.6
  924.6 3.0 slice.167
  927.6 23.7 all_gather.43
  951.5 25.2 all_gather.44
  976.7 144.5 %while.50 = (s32[]{:T(128)}, f32[2,32,64,64]{3,2,1,0:T(8,128)}, f32[2,32,64,64]{3,2,1,0:T(8,128)}, bf16[2,512]{1,0:T(2,128)(2,1)S(1)}, f32[2,64]{1,0:T(2,128)}, ...) while((s32[]{:T(128)}, f32[2,32,64,64]{3,2,1,0:T(8,128)}, ...), condition=%wide.region_9.10_spmd.clone, body=%wide.region_8.9_spmd.clone.sunk | while | flops 137408768 | bytes 17116220 | solution.py:294
  986.5 4.3 select_add_fusion.7
  1002.5 5.0 select_add_fusion.7
  1007.5 3.7 select_add_fusion.8
  1020.8 5.0 select_add_fusion.7
  1025.8 3.7 select_add_fusion.8
  1039.1 5.0 select_add_fusion.7
  1044.2 3.7 select_add_fusion.8
  1057.5 5.0 select_add_fusion.7
  1062.5 3.7 select_add_fusion.8
  1075.8 5.0 select_add_fusion.7
  1080.8 3.7 select_add_fusion.8
  1094.1 5.0 select_add_fusion.7
  1099.1 3.7 select_add_fusion.8
  1112.4 5.0 select_add_fusion.7
  1117.5 3.7 select_add_fusion.8
  1121.2 6.4 add_convert_fusion
  1132.7 2.8 pad_maximum_fusion.3
  1150.5 4.9 fusion.55
  1155.4 3.7 fusion.54
  1159.2 32.1 multiply_reduce_fusion.1
  1193.2 22.5 fusion.56
  1216.7 48.7 %fusion.70 = f32[2048,17408]{1,0:T(8,128)} fusion(bf16[128,2048]{1,0:T(8,128)(2,1)S(1)} %copy-done.12, bf16[128,17408]{1,0:T(8,128)(2,1)} %fusion.54), kind=kOutput, calls=%fused_computation.163 | convolution fusion | flops 9126805504 | bytes 147587072 | tf_op jit(solution)/shard_map/dot_general | solution.py:313
  1268.8 15.1 fusion.52
  1283.9 49.8 %reduce-scatter.10.cloned.1.call-done = f32[64,5]{1,0:T(8,128)} async-done(((f32[2048,5]{1,0:T(8,128)}), f32[64,5]{1,0:T(8,128)}) %reduce-scatter.10.cloned.1.call-update) | async-done | bytes 1296
  1335.3 524.7 %reduce-scatter.8.cloned.1.call-done = f32[240,2048]{1,0:T(8,128)} async-done(((f32[7680,2048]{1,0:T(8,128)}), f32[240,2048]{1,0:T(8,128)}) %reduce-scatter.8.cloned.1.call-update) | async-done | bytes 1966096 | tf_op jit(solution)/shard_map/reduce_scatter | solution.py:197
  1860.0 8.2 multiply_add_fusion.3
  1868.2 2964.3 %reduce-scatter.6.cloned.1.call-done = f32[64,17408]{1,0:T(8,128)} async-done(((f32[2048,17408]{1,0:T(8,128)}), f32[64,17408]{1,0:T(8,128)}) %reduce-scatter.6.cloned.1.call-update) | async-done | bytes 4456464 | tf_op jit(solution)/shard_map/reduce_scatter | solution.py:312
  4832.5 12.6 multiply_add_fusion
  (490 shorter events, 275.0 us)
Async XLA Ops:
  7.2 380.7 %all-gather.9.cloned.1.call-start = ((), (), s32[]{:S(2)}) async-start(), calls=%async_computation.3 | async-start | bytes 73531392 | tf_op jit(solution)/shard_map/all_gather | solution.py:115
  11.1 1.5 copy-start.10
  11.1 2.7 copy-start.30
  11.1 63.9 %copy-start.4 = (bf16[2,64,2048]{2,1,0:T(8,128)(2,1)S(1)}, bf16[2,64,2048]{2,1,0:T(8,128)(2,1)}, u32[]{:S(2)}) copy-start(bf16[2,64,2048]{2,1,0:T(8,128)(2,1)} %param.22) | copy-start | bytes 1572868
  11.1 64.6 %copy-start.39 = (s32[2,64]{1,0:T(2,128)S(1)}, s32[2,64]{1,0:T(2,128)}, u32[]{:S(2)}) copy-start(s32[2,64]{1,0:T(2,128)} %param.25) | copy-start | bytes 1540
  11.1 563.4 %all-gather.15.cloned.1.call-start = ((), (), s32[]{:S(2)}) async-start(), calls=%async_computation.6 | async-start | bytes 32440320 | tf_op jit(solution)/shard_map/all_gather | solution.py:184
  13.7 633.5 %all-gather.11.cloned.1.call-start = ((), (), s32[]{:S(2)}) async-start(), calls=%async_computation.4 | async-start | bytes 4718592 | tf_op jit(solution)/shard_map/all_gather | solution.py:143
  75.3 341.4 %copy-start.32 = (f32[128]{0:T(128)}, f32[128]{0:T(128)S(1)}, u32[]{:S(2)}) copy-start(f32[128]{0:T(128)S(1)} %div.76) | copy-start | bytes 1540
  75.7 341.0 %copy-start.34 = (f32[128]{0:T(128)}, f32[128]{0:T(128)S(1)}, u32[]{:S(2)}) copy-start(f32[128]{0:T(128)S(1)} %rsqrt.12) | copy-start | bytes 1540
  76.1 353.3 %copy-start.23 = (f32[2,64,8]{2,1,0:T(8,128)}, f32[2,64,8]{2,1,0:T(8,128)S(1)}, u32[]{:S(2)}) copy-start(f32[2,64,8]{2,1,0:T(8,128)S(1)} %get-tuple-element.903) | copy-start | bytes 12292
  76.1 340.6 %copy-start.25 = (f32[2048,1]{0,1:T(1,128)}, f32[2048,1]{0,1:T(1,128)S(1)}, u32[]{:S(2)}) copy-start(f32[2048,1]{0,1:T(1,128)S(1)} %get-tuple-element.900) | copy-start | bytes 24580
  76.5 340.2 %copy-start.11 = (bf16[128,2048]{1,0:T(8,128)(2,1)}, bf16[128,2048]{1,0:T(8,128)(2,1)S(1)}, u32[]{:S(2)}) copy-start(bf16[128,2048]{1,0:T(8,128)(2,1)S(1)} %add_convert_fusion.2) | copy-start | bytes 1572868
  418.9 2.0 copy-start.9
  423.1 1.7 copy-start.3
  429.4 6.9 copy-start.22
  439.9 134.6 %copy-start.13 = (bf16[2,64,2048]{2,1,0:T(8,128)(2,1)S(1)}, bf16[2,64,2048]{2,1,0:T(8,128)(2,1)}, u32[]{:S(2)}) copy-start(bf16[2,64,2048]{2,1,0:T(8,128)(2,1)} %param.23) | copy-start | bytes 1572868
  442.8 278.2 %all-gather.13.cloned.1.call-start = ((), (), s32[]{:S(2)}) async-start(), calls=%async_computation.5 | async-start | bytes 4718592 | tf_op jit(solution)/shard_map/all_gather | solution.py:144
  444.9 531.8 %all-gather.19.cloned.1.call-start = ((), (), s32[]{:S(2)}) async-start(), calls=%async_computation.8 | async-start | bytes 4718592 | tf_op jit(solution)/shard_map/all_gather | solution.py:252
  574.5 17.8 copy-start.40
  590.0 1.3 copy-start.6
  592.2 384.5 %all-gather.17.cloned.1.call-start = ((), (), s32[]{:S(2)}) async-start(), calls=%async_computation.7 | async-start | bytes 4718592 | tf_op jit(solution)/shard_map/all_gather | solution.py:251
  610.4 1.3 copy-start.16
  611.8 3.7 copy-start.17
  611.8 3.7 copy-start.18
  617.4 3.6 copy-start.19
  627.0 706.7 %reduce-scatter.10.cloned.1.call-start = ((), (), s32[]{:S(2)}) async-start(), calls=%async_computation.11 | async-start | bytes 1081344
  924.5 26.9 copy-start.24
  976.9 1.2 copy-start.27
  982.0 2.3 copy-start.1
  990.8 2.1 copy-start.28
  992.9 1.1 copy-start.27
  998.1 2.3 copy-start.1
  1007.5 3.7 copy-start.28
  1011.2 1.1 copy-start.27
  1016.4 2.3 copy-start.1
  1025.8 3.7 copy-start.28
  1034.7 2.3 copy-start.1
  1044.2 3.7 copy-start.28
  1053.0 2.3 copy-start.1
  1062.5 3.7 copy-start.28
  1071.4 2.3 copy-start.1
  1080.8 3.7 copy-start.28
  1089.7 2.3 copy-start.1
  1099.1 3.7 copy-start.28
  1108.0 2.3 copy-start.1
  1117.5 3.7 copy-start.28
  1121.2 6.4 copy-start
  1127.6 1.4 copy-start.21
  1142.4 4.4 copy-start.2
  1147.0 1.5 copy-start.15
  1148.5 1.9 copy-start.7
  1155.4 3.8 copy-start.5
  1155.4 3.8 copy-start.26
  1155.4 3.8 copy-start.33
  1155.4 3.8 copy-start.35
  1191.3 1.5 copy-start.8
  1191.3 1.9 copy-start.14
  1192.7 667.2 %reduce-scatter.8.cloned.1.call-start = ((), (), s32[]{:S(2)}) async-start(), calls=%async_computation.10 | async-start | bytes 64880640 | tf_op jit(solution)/shard_map/reduce_scatter | solution.py:197
  1215.7 3616.8 %reduce-scatter.6.cloned.1.call-start = ((), (), s32[]{:S(2)}) async-start(), calls=%async_computation.9 | async-start | bytes 147062784 | tf_op jit(solution)/shard_map/reduce_scatter | solution.py:312
  1268.8 65.8 %copy-start.31 = (f32[64,5]{0,1:T(8,128)S(1)}, f32[64,5]{0,1:T(8,128)}, u32[]{:S(2)}) copy-start(f32[64,5]{0,1:T(8,128)} %param.34) | copy-start | bytes 3844
  1268.8 65.8 %copy-start.36 = (f32[64,5]{0,1:T(8,128)S(1)}, f32[64,5]{0,1:T(8,128)}, u32[]{:S(2)}) copy-start(f32[64,5]{0,1:T(8,128)} %param.37) | copy-start | bytes 3844
  1268.8 65.8 %copy-start.37 = (f32[64,5]{0,1:T(8,128)S(1)}, f32[64,5]{0,1:T(8,128)}, u32[]{:S(2)}) copy-start(f32[64,5]{0,1:T(8,128)} %param.35) | copy-start | bytes 3844
  1268.8 65.8 %copy-start.38 = (f32[64,5]{0,1:T(8,128)S(1)}, f32[64,5]{0,1:T(8,128)}, u32[]{:S(2)}) copy-start(f32[64,5]{0,1:T(8,128)} %param.36) | copy-start | bytes 3844
  1334.6 533.6 %copy-start.29 = (f32[64,5]{0,1:T(8,128)}, f32[64,5]{0,1:T(8,128)S(1)}, u32[]{:S(2)}) copy-start(f32[64,5]{0,1:T(8,128)S(1)} %copy.186) | copy-start | bytes 3844
  (9 other events, 9.1 us)
Sparse Core Ops, SparseCore 0:
  11.4 376.4 all-gather.8
  391.5 182.9 all-gather.14
  576.7 70.4 all-gather.10
  649.3 71.6 all-gather.12
  723.5 71.6 all-gather.18
  797.3 71.6 all-gather.16
  1192.9 140.8 reduce-scatter.9
  1341.9 518.0 reduce-scatter.7
  1862.9 2969.5 reduce-scatter.5
where the time goes:
time: 4860 us; the launch traced here: 4850 us
  waiting for transfers between devices  4070 us (84%)
  matrix products  347 us (7%)
  local copies, waits for them, and re-layouts  200 us (4%)
  blocking collectives  123 us (3%)
  other arithmetic  91.1 us (2%)
    reduce_scatter x1, waiting for transfers between devices, per_device(): lax.psum_scatter(lax.dot_general(columns, d_proj, (((0,), (0,)), ((), ())...  2960 us
    reduce_scatter x1, waiting for transfers between devices, per_device(): lax.psum_scatter(lax.dot_general(columns, grad_out, (((0,), (0,)), ((), (...  525 us
    all_gather x1, waiting for transfers between devices, per_device(): w_piece = lax.all_gather(in_low, ('dp', 'seq'), axis=0, tiled=True)  311 us
    all_gather x1, waiting for transfers between devices, per_device(): lax.all_gather(out_low, ('dp', 'seq'), axis=0, tiled=True)  130 us
  transfers between devices with their start and end apart: 9, of which 7 were waited for; matrix products, arithmetic and copies ran while one was open for 8% of the time, Pallas kernels for 0%

commit v1 on v0

--- a/solution.py
+++ b/solution.py
@@ -1,6 +1,10 @@
+import functools
+
 import jax
 import jax.numpy as jnp
 from jax import lax
+from jax.experimental import pallas as pl
+from jax.experimental.pallas import tpu as pltpu
 from jax.sharding import PartitionSpec as P
 
 HEADS = 32
@@ -358,9 +362,303 @@
     )
 
 
+def heads_fit(n_dp, n_seq, own_rows, model_width, wide_in):
+    dp_rows = own_rows * n_seq
+    if n_dp != 4 or HEADS % (2 * n_seq) or not dp_rows < model_width < 2 * dp_rows:
+        return False
+    att_rows = model_width // n_seq
+    late_att = model_width - dp_rows
+    first_act = dp_rows - late_att
+    if first_act % n_seq:
+        return False
+    lead = att_rows - own_rows
+    return (
+        wide_in - 3 * model_width == 2 * (n_dp * dp_rows - model_width)
+        and lead == own_rows - first_act // n_seq
+        and lead * n_seq == late_att
+        and lead % 16 == 0
+    )
+
+
+def attention_kernel(
+    q_ref, k_ref, v_ref, bq_ref, bk_ref, bv_ref, da_ref, rope_ref, seg_q_ref, seg_k_ref,
+    o_ref, dq_ref, dk_ref, dv_ref, *, head_size, half_rot,
+):
+    cos, sin_low, sin_high = rope_ref[0], rope_ref[1], rope_ref[2]
+    tokens, lanes = cos.shape
+    scale = head_size ** (-0.5)
+
+    def turn(v, way):
+        return (
+            v * cos
+            + way * pltpu.roll(v, lanes - half_rot, 1) * sin_low
+            + way * pltpu.roll(v, half_rot, 1) * sin_high
+        )
+
+    query = (turn(q_ref[...] + bq_ref[...], 1.0)).astype(jnp.bfloat16) * scale
+    query = query.astype(jnp.bfloat16)
+    key = turn(k_ref[...] + bk_ref[...], 1.0).astype(jnp.bfloat16)
+    value = (v_ref[...] + bv_ref[...]).astype(jnp.bfloat16)
+    d_att = da_ref[...]
+    place_q = lax.broadcasted_iota(jnp.int32, (tokens, tokens), 0)
+    place_k = lax.broadcasted_iota(jnp.int32, (tokens, tokens), 1)
+    mask = (seg_q_ref[0] == seg_k_ref[0]) & (place_k <= place_q)
+    lane = lax.broadcasted_iota(jnp.int32, (tokens, lanes), 1)
+    nt = (((1,), (1,)), ((), ()))
+    tn = (((0,), (0,)), ((), ()))
+    dot = functools.partial(lax.dot_general, preferred_element_type=jnp.float32)
+    att = jnp.zeros((tokens, lanes), jnp.float32)
+    d_query = jnp.zeros((tokens, lanes), jnp.float32)
+    d_key = jnp.zeros((tokens, lanes), jnp.float32)
+    d_value = jnp.zeros((tokens, lanes), jnp.float32)
+    for head in range(lanes // head_size):
+        mine = (lane >= head * head_size) & (lane < (head + 1) * head_size)
+        q_h = jnp.where(mine, query, jnp.zeros_like(query))
+        da_h = jnp.where(mine, d_att, jnp.zeros_like(d_att))
+        scores = jnp.where(mask, dot(q_h, key, nt), neg_large)
+        top = jnp.max(scores, axis=1, keepdims=True)
+        weights = jnp.exp(scores - top)
+        probs = weights * (1.0 / jnp.sum(weights, axis=1, keepdims=True))
+        probs_low = probs.astype(jnp.bfloat16)
+        att_h = jnp.where(mine, dot(probs_low, value, (((1,), (0,)), ((), ()))), 0.0)
+        out_dot = jnp.sum(att_h * d_att.astype(jnp.float32), axis=1, keepdims=True)
+        d_prob = dot(da_h, value, nt)
+        d_score = (probs * (d_prob - out_dot)).astype(jnp.bfloat16)
+        att = att + att_h
+        d_query = d_query + jnp.where(mine, dot(d_score, key, (((1,), (0,)), ((), ()))), 0.0)
+        d_key = d_key + dot(d_score, q_h, tn)
+        d_value = d_value + dot(probs_low, da_h, tn)
+    o_ref[...] = att.astype(jnp.bfloat16)
+    dq_ref[...] = turn(d_query * scale, -1.0).astype(jnp.bfloat16)
+    dk_ref[...] = turn(d_key, -1.0).astype(jnp.bfloat16)
+    dv_ref[...] = d_value.astype(jnp.bfloat16)
+
+
+def attention_both(proj, bias, d_joined, rope, seg, rows, tokens, att_rows, head_size):
+    lanes = 2 * head_size
+    pairs = att_rows // lanes
+    block = lambda first: pl.BlockSpec((tokens, lanes), lambda r, h: (r, first + h))
+    row = lambda first: pl.BlockSpec((1, lanes), lambda r, h: (0, first + h))
+    out = jax.ShapeDtypeStruct((rows * tokens, att_rows), jnp.bfloat16)
+    return pl.pallas_call(
+        functools.partial(attention_kernel, head_size=head_size, half_rot=ROT // 2),
+        grid=(rows, pairs),
+        in_specs=[
+            block(0), block(pairs), block(2 * pairs),
+            row(0), row(pairs), row(2 * pairs),
+            block(0),
+            pl.BlockSpec((3, tokens, lanes), lambda r, h: (0, r, 0)),
+            pl.BlockSpec((1, tokens, 1), lambda r, h: (r, 0, 0)),
+            pl.BlockSpec((1, 1, tokens), lambda r, h: (r, 0, 0)),
+        ],
+        out_specs=[block(0)] * 4,
+        out_shape=[out] * 4,
+        compiler_params=pltpu.CompilerParams(vmem_limit_bytes=56 * 2**20),
+        cost_estimate=pl.CostEstimate(
+            flops=rows * pairs * 2 * 12 * tokens * tokens * lanes,
+            bytes_accessed=rows * tokens * att_rows * 20,
+            transcendentals=rows * pairs * 2 * tokens * tokens,
+        ),
+        name="attention",
+    )(proj, proj, proj, bias, bias, bias, d_joined, rope, seg[:, :, None], seg[:, None, :])
+
+
+def split_heads(
+    n_dp, n_seq, tokens, cotangent, segment_ids, doc_positions,
+    in_weight, in_first, in_second, in_average,
+    out_weight, out_first, out_second, out_average,
+    small_params, small_first, small_second, small_average,
+):
+    bf16, f32 = jnp.bfloat16, jnp.float32
+    rows, own_tokens, width = tokens.shape
+    row_tokens = own_tokens * n_seq
+    all_tokens = rows * row_tokens
+    head_size = width // HEADS
+    ffn = (in_weight.shape[1] - 3 * width) // 2
+    in_rows, own = in_weight.shape[0], out_weight.shape[0]
+    dp_rows = own * n_seq
+    att = width // n_seq
+    late = width - dp_rows
+    act = [(dp_rows - late) // n_seq, own, own]
+    act_all = sum(act)
+    cuts = [0, act[0] * n_seq, (act[0] + own) * n_seq, ffn]
+    lead = att - own
+    slot = act[0] + late
+    p, s = lax.axis_index("dp"), lax.axis_index("seq")
+
+    def share(v):
+        parts = [v[:, i * width : (i + 1) * width].reshape(-1, n_seq, att) for i in range(3)]
+        for half in range(2):
+            base = 3 * width + half * ffn
+            for i in range(3):
+                parts.append(v[:, base + cuts[i] : base + cuts[i + 1]].reshape(-1, n_seq, act[i]))
+        return jnp.transpose(jnp.concatenate(parts, axis=2), (1, 0, 2))
+
+    def unshare(v):
+        v = jnp.transpose(v, (1, 0, 2))
+        sizes = [att] * 3 + act * 2
+        parts, at = [], 0
+        for size in sizes:
+            parts.append(v[:, :, at : at + size].reshape(v.shape[0], n_seq * size))
+            at += size
+        return jnp.concatenate(parts, axis=1)
+
+    in_low = lax.all_to_all(share(in_weight.astype(bf16)), "seq", 0, 0, tiled=True)
+    in_low = in_low.reshape(n_seq * in_rows, 3 * att + 2 * act_all)
+    in_low = lax.all_gather(in_low, "dp", axis=0, tiled=True)
+    small_low = lax.all_gather(small_params.astype(bf16), ("dp", "seq"), axis=0, tiled=True)
+    small_low = small_low.astype(f32)
+    gain, shift = small_low[:, 0], small_low[:, 1]
+    bias = lax.dynamic_slice_in_dim(small_low[:, 2:5], s * att, att, 0).T.reshape(1, 3 * att)
+
+    out_low = out_weight.astype(bf16)
+    from_next = lax.ppermute(out_low[:late], "seq", [(k, (k - 1) % n_seq) for k in range(n_seq)])
+    start = jnp.where(p == 0, lead * s, jnp.where(p == 1, late - lead * s, 0))
+    joined_rows = jnp.concatenate([out_low, from_next, out_low[:lead]], axis=0)
+    main = lax.dynamic_slice_in_dim(joined_rows, start, att, 0)
+    late_slot = jnp.concatenate([main[: act[0]], from_next], axis=0)
+    plain_slot = jnp.concatenate([main, main[: slot - att]], axis=0)
+    slots = lax.all_gather(jnp.where(p == 1, late_slot, plain_slot), "dp", axis=0)
+    last = s == n_seq - 1
+    keep = att - late
+    out_mine = jnp.concatenate(
+        [
+            slots[0, :keep],
+            jnp.where(last, slots[1, act[0] : slot], slots[0, keep:att]),
+            slots[1, : act[0]],
+            slots[2, :own],
+            slots[3, :own],
+        ],
+        axis=0,
+    )
+
+    x_full = lax.all_gather(tokens, "seq", axis=1, tiled=True).reshape(all_tokens, width)
+    g_full = lax.all_gather(cotangent, "seq", axis=1, tiled=True).reshape(all_tokens, width)
+    seg_full = lax.all_gather(segment_ids, "seq", axis=1, tiled=True)
+    pos_full = lax.all_gather(doc_positions, "seq", axis=1, tiled=True)
+
+    def normalise(v):
+        v = v.astype(f32)
+        centered = v - jnp.mean(v, axis=-1, keepdims=True)
+        inv_std = lax.rsqrt(jnp.mean(centered * centered, axis=-1, keepdims=True) + norm_eps)
+        return centered * inv_std, inv_std
+
+    hidden = (normalise(x_full)[0] * gain + shift).astype(bf16)
+    proj = jnp.dot(hidden, in_low, preferred_element_type=f32)
+    d_joined = lax.dot_general(
+        g_full, out_mine, (((1,), (1,)), ((), ())), preferred_element_type=f32
+    ).astype(bf16)
+
+    half_rot = ROT // 2
+    inv_freq = rope_base ** (-2.0 * jnp.arange(half_rot, dtype=f32) / ROT)
+    angles = pos_full.reshape(all_tokens, 1).astype(f32) * inv_freq
+    cos, sin = jnp.cos(angles), jnp.sin(angles)
+    rest = head_size - ROT
+    one, zero = jnp.ones((all_tokens, rest), f32), jnp.zeros((all_tokens, rest), f32)
+    none = jnp.zeros_like(sin)
+    rope = jnp.stack(
+        [
+            jnp.concatenate([cos, cos, one] * 2, axis=1),
+            jnp.concatenate([-sin, none, zero] * 2, axis=1),
+            jnp.concatenate([none, sin, zero] * 2, axis=1),
+        ]
+    )
+    att_low, d_query, d_key, d_value = attention_both(
+        proj, bias, d_joined, rope, seg_full, rows, row_tokens, att, head_size
+    )
+
+    gate = proj[:, 3 * att : 3 * att + act_all]
+    up = proj[:, 3 * att + act_all :]
+    sig = jax.nn.sigmoid(gate)
+    silu = gate * sig
+    joined = jnp.concatenate([att_low, (silu * up).astype(bf16)], axis=1)
+    d_act = d_joined[:, att:].astype(f32)
+    d_gate = d_act * up * sig * (1.0 + gate * (1.0 - sig))
+    d_up = d_act * silu
+    d_proj = jnp.concatenate(
+        [d_query, d_key, d_value, d_gate.astype(bf16), d_up.astype(bf16)], axis=1
+    )
+
+    branch = jnp.dot(joined, out_mine, preferred_element_type=f32).astype(bf16)
+    branch = lax.psum_scatter(
+        branch.reshape(rows, row_tokens, width), "seq", scatter_dimension=1, tiled=True
+    )
+    output = (tokens.astype(f32) + branch.astype(f32)).astype(bf16)
+
+    out_part = lax.dot_general(
+        joined, g_full, (((0,), (0,)), ((), ())), preferred_element_type=f32
+    ).astype(bf16)
+    a0 = out_part[:att]
+    a1, a2, a3 = (
+        out_part[att : att + act[0]],
+        out_part[att + act[0] : att + act[0] + own],
+        out_part[att + act[0] + own :],
+    )
+    fill = lambda v: jnp.pad(v, ((0, slot - v.shape[0]), (0, 0)))
+    out_slots = jnp.stack(
+        [fill(a0), jnp.concatenate([a1, a0[keep:]], axis=0), fill(a2), fill(a3)]
+    )
+    out_sum = lax.psum_scatter(out_slots, "dp", scatter_dimension=0, tiled=True)[0]
+    send_at = jnp.where(p == 0, keep, jnp.where(last, act[0], act[0] - late))
+    sent = lax.dynamic_slice_in_dim(out_sum, send_at, late, 0)
+    from_prev = lax.ppermute(sent, "seq", [(k, (k + 1) % n_seq) for k in range(n_seq)])
+    count = jnp.where(p == 0, lead * s, jnp.where(p == 1, late - lead * s, 0))
+    out_grad = lax.dynamic_slice_in_dim(
+        jnp.concatenate([from_prev, out_sum[:own]], axis=0), late - count, own, 0
+    ).astype(f32)
+
+    in_part = lax.dot_general(
+        hidden, d_proj, (((0,), (0,)), ((), ())), preferred_element_type=f32
+    ).astype(bf16)
+    in_sum = lax.psum_scatter(in_part, "dp", scatter_dimension=0, tiled=True)
+    in_sum = lax.all_to_all(in_sum.reshape(n_seq, in_rows, -1), "seq", 0, 0, tiled=True)
+    in_grad = unshare(in_sum).astype(f32)
+
+    d_hidden = lax.dot_general(
+        d_proj, in_low, (((1,), (1,)), ((), ())), preferred_element_type=f32
+    ).astype(bf16)
+    d_hidden = lax.psum_scatter(
+        d_hidden.reshape(rows, row_tokens, width), "seq", scatter_dimension=1, tiled=True
+    ).astype(f32)
+    normed, inv_std = normalise(tokens)
+    d_normed = d_hidden * gain
+    input_grad = cotangent.astype(f32) + inv_std * (
+        d_normed
+        - jnp.mean(d_normed, axis=-1, keepdims=True)
+        - normed * jnp.mean(d_normed * normed, axis=-1, keepdims=True)
+    )
+
+    gain_grad = jnp.sum(d_hidden * normed, axis=(0, 1))
+    shift_grad = jnp.sum(d_hidden, axis=(0, 1))
+    bias_part = jnp.sum(d_proj[:, : 3 * att].astype(f32), axis=0).reshape(3, att).T
+    bias_grad = lax.dynamic_update_slice_in_dim(jnp.zeros((width, 3), f32), bias_part, s * att, 0)
+    small_term = jnp.concatenate([gain_grad[:, None], shift_grad[:, None], bias_grad], axis=1)
+    small_grad = lax.psum_scatter(small_term, ("dp", "seq"), scatter_dimension=0, tiled=True)
+
+    in_new = adam_update(
+        in_weight, in_first, in_second, in_average, in_grad, matrix_rate, weight_decay
+    )
+    out_new = adam_update(
+        out_weight, out_first, out_second, out_average, out_grad, matrix_rate, weight_decay
+    )
+    small_new = adam_update(
+        small_params, small_first, small_second, small_average, small_grad, small_rate, 0.0
+    )
+    return (output, input_grad, *in_new, *out_new, *small_new, small_grad, in_grad, out_grad)
+
+
 def solution(mesh):
+    n_dp, n_seq = mesh.shape["dp"], mesh.shape["seq"]
+
+    def choose(*operands):
+        own_rows = operands[8].shape[0]
+        model_width = operands[0].shape[2]
+        if heads_fit(n_dp, n_seq, own_rows, model_width, operands[4].shape[1]):
+            return split_heads(n_dp, n_seq, *operands)
+        return per_device(*operands)
+
     return jax.shard_map(
-        per_device,
+        choose,
         mesh=mesh,
         in_specs=(
             P("dp", "seq", None),

time: 4860 us -> 920 us (0.19)
  waiting for transfers between devices: 4070 us -> 494 us
  matrix products: 347 us -> 70.7 us
  local copies, waits for them, and re-layouts: 200 us -> 67.3 us
  blocking collectives: 123 us -> 179 us
    reduce_scatter x2 -> x4, waiting for transfers between devices: 3490 us -> 305 us  [the longest x1 128 us: split_heads(): lax.psum_scatter(branch.reshape(rows, row_tokens, width), 'seq', scatter_...]
    all_gather x6 -> x4, waiting for transfers between devices: 535 us -> 38.5 us  [the longest x1 38.5 us: split_heads(): in_low = lax.all_gather(in_low, 'dp', axis=0, tiled=True)]
    dot_general x62 -> x6, matrix products: 347 us -> 70.7 us  [the longest x1 15.3 us: split_heads(): lax.dot_general(hidden, d_proj, (((0,), (0,)), ((), ())), preferred_eleme...]
    all_to_all x0 -> x1, blocking collectives: none -> 85.5 us  [split_heads(): lax.all_to_all(share(in_weight.astype(bf16)), 'seq', 0, 0, tiled=True)]
    reshape x55 -> x16, local copies, waits for them, and re-layouts: 92 us -> 15 us  [the longest x6 9.13 us: share(): v[:, base + cuts[i]:base + cuts[i + 1]].reshape(-1, n_seq, act[i])]
    unnamed x10, waiting for transfers between devices: 50 us -> 126 us
    dynamic_slice x48 -> x1, local copies, waits for them, and re-layouts: 58.5 us -> 1.22 us  [split_heads(): sent = lax.dynamic_slice_in_dim(out_sum, send_at, late, 0)]
    all_gather x4 -> x3, blocking collectives: 123 us -> 93.9 us  [the longest x1 59 us: split_heads(): lax.all_gather(small_params.astype(bf16), ('dp', 'seq'), axis=0, tiled=True)]
  transfers between devices with their start and end apart: 9 -> 12, of which waited for: 7 -> 8; matrix products, arithmetic and copies ran while one was open for 8% -> 13% of each run, Pallas kernels for 0% -> 0%
where the time goes in v1:
time: 920 us; the launch traced here: 906 us
  waiting for transfers between devices  494 us (54%)
  blocking collectives  179 us (19%)
  matrix products  70.7 us (8%)
  local copies, waits for them, and re-layouts  67.3 us (7%)
  other arithmetic  57.9 us (6%)
  between operations  14.9 us (2%)
  Pallas kernels  14.5 us (2%)
    reduce_scatter x1, waiting for transfers between devices, split_heads(): lax.psum_scatter(branch.reshape(rows, row_tokens, width), 'seq', scatter_...  128 us
    unnamed x10, waiting for transfers between devices  126 us
    all_to_all x1, blocking collectives, split_heads(): lax.all_to_all(share(in_weight.astype(bf16)), 'seq', 0, 0, tiled=True)  85.5 us
    reduce_scatter x1, waiting for transfers between devices, split_heads(): in_sum = lax.psum_scatter(in_part, 'dp', scatter_dimension=0, tiled=True)  69.6 us
    reduce_scatter x1, waiting for transfers between devices, split_heads(): lax.psum_scatter(out_slots, 'dp', scatter_dimension=0, tiled=True)[0]  62.8 us
    all_gather x1, blocking collectives, split_heads(): lax.all_gather(small_params.astype(bf16), ('dp', 'seq'), axis=0, tiled=True)  59 us
    reduce_scatter x1, waiting for transfers between devices, split_heads(): lax.psum_scatter(d_hidden.reshape(rows, row_tokens, width), 'seq', scatte...  44.7 us
    all_gather x1, waiting for transfers between devices, split_heads(): in_low = lax.all_gather(in_low, 'dp', axis=0, tiled=True)  38.5 us
  transfers between devices with their start and end apart: 12, of which 8 were waited for; matrix products, arithmetic and copies ran while one was open for 13% of the time, Pallas kernels for 0%

profile of v1, /device:TPU:11, one launch (start us, length us, event | category | flops | bytes accessed | tf_op | source)
XLA Modules:
  0.0 906.4 jit_solution(219859323955282575)
XLA Ops:
  8.0 1.7 convert_element_type.103
  10.0 13.9 %collective-permute-done = bf16[128,2048]{1,0:T(8,128)(2,1)S(1)} collective-permute-done((bf16[128,2048]{1,0:T(8,128)(2,1)S(1)}, bf16[128,2048]{1,0:T(8,128)(2,1)S(1)}, u32[]{:S(2)}, u32[]{:S(2)}) %collective-permute-start) | collective-permute-done | bytes 524320 | tf_op jit(solution)/shard_map/ppermute | solution.py:515
  23.9 1.2 fusion.26
  25.3 1.6 maximum_select_fusion
  27.8 2.5 convert_element_type.102
  31.2 1.1 reshape.237
  33.6 1.4 reshape.239
  35.0 2.0 reshape.240
  37.1 2.1 reshape.241
  39.2 2.1 reshape.242
  41.2 4.1 concatenate.67
  45.7 85.5 %all_to_all.10 = bf16[8,64,2176]{2,1,0:T(8,128)(2,1)} all-to-all(bf16[8,64,2176]{2,1,0:T(8,128)(2,1)S(1)} %copy.87), channel_id=1, replica_groups=mesh['dp'=4,'seq'=8] {'seq'}, dimensions={0} | all-to-all | bytes 4456448 | tf_op jit(solution)/shard_map/all_to_all | solution.py:506
  131.3 59.0 %all-gather = bf16[32,64,5]{1,2,0:T(8,128)(2,1)S(1)} all-gather(bf16[1,64,5]{1,2,0:T(8,128)(2,1)S(1)} %convert_bitcast_fusion), channel_id=1, replica_groups=mesh['dp'=4,'seq'=8] {'dp','seq'}, dimensions={0}, use_global_device_ids=true | all-gather | bytes 21120 | tf_op jit(solution)/shard_map/all_gather | solution.py:509
  191.0 16.8 %all-gather.1 = s32[8,64,2]{1,2,0:T(2,128)S(1)} all-gather(s32[1,64,2]{1,2,0:T(2,128)S(1)} %bitcast.161), channel_id=1, replica_groups=mesh['dp'=4,'seq'=8] {'seq'}, dimensions={0}, use_global_device_ids=true | all-gather | bytes 4608 | tf_op jit(solution)/shard_map/all_gather | solution.py:538
  207.9 1.9 multiply_cosine_fusion
  209.9 1.1 concatenate.78
  211.0 1.1 concatenate.77
  212.2 18.1 %all-gather.2 = s32[8,64,2]{1,2,0:T(2,128)S(1)} all-gather(s32[1,64,2]{1,2,0:T(2,128)S(1)} %bitcast.162), channel_id=1, replica_groups=mesh['dp'=4,'seq'=8] {'seq'}, dimensions={0}, use_global_device_ids=true | all-gather | bytes 4608 | tf_op jit(solution)/shard_map/all_gather | solution.py:537
  232.0 1.1 concatenate.76
  233.1 1.2 pad_maximum_fusion.2.rope_ref
  234.4 3.0 convert_reduce_fusion
  237.9 1.2 multiply_reduce_fusion
  239.1 3.2 fusion.3
  242.3 1.9 fusion.34
  244.2 2.1 fusion.33
  246.3 2.2 fusion.31
  248.5 2.2 fusion.30
  250.7 2.4 fusion.29
  253.1 10.5 %convolution_convert_fusion.4 = bf16[960,1024]{1,0:T(8,128)(2,1)} fusion(bf16[960,2048]{1,0:T(8,128)(2,1)} %fusion.29, bf16[1024,2048]{1,0:T(8,128)(2,1)} %bitcast.163), kind=kOutput, calls=%fused_computation.31 | convolution fusion | flops 4027514880 | bytes 10092544 | tf_op jit(solution)/shard_map/dot_general | solution.py:548
  263.6 2.8 copy.88
  266.5 38.5 %all-gather.10.cloned.1.call-done = bf16[2048,2176]{1,0:T(8,128)(2,1)} async-done(((bf16[512,2176]{1,0:T(8,128)(2,1)}), bf16[2048,2176]{1,0:T(8,128)(2,1)}) %all-gather.10.cloned.1.call-update) | async-done | bytes 8912912 | tf_op jit(solution)/shard_map/all_gather | solution.py:508
  305.0 14.3 %fusion.51.q_ref.k_ref.v_ref = f32[1024,2176]{1,0:T(8,128)S(1)} fusion(bf16[1024,2048]{1,0:T(8,128)(2,1)} %fusion.3, bf16[2048,2176]{1,0:T(8,128)(2,1)} %all-gather.10.cloned.1.call-done), kind=kOutput, calls=%fused_computation.124 | convolution fusion | flops 9126805504 | bytes 22020096 | tf_op jit(solution)/shard_map/dot_general | solution.py:547
  319.3 4.4 fusion.8
  324.2 14.5 %attention.1 = (bf16[1024,256]{1,0:T(8,128)(2,1)}, bf16[1024,256]{1,0:T(8,128)(2,1)}, bf16[1024,256]{1,0:T(8,128)(2,1)}, bf16[1024,256]{1,0:T(8,128)(2,1)}) custom-call(f32[1024,2176]{1,0:T(8,128)} %copy-done, f32[1024,2176]{1,0:T(8,128)} %copy-done, f32[1024,2176]{1,0:T(8,128)} %copy-done, f32[1,768]{1,0:T(1,128)} %bitcast.149, f32[1,768]{1,0:T(1,128)} %bitcast.150, ...), custom_call_target="tpu_custom_call" | custom-call | flops 3221225472 | bytes 5242880 | tf_op jit(solution)/shard_map/attention/pallas_call | solution.py:443
  338.7 7.2 concatenate.80
  345.9 15.1 %convolution_convert_fusion.1 = bf16[1024,2048]{1,0:T(8,128)(2,1)} fusion(bf16[1024,2176]{1,0:T(8,128)(2,1)} %concatenate.80, bf16[2048,2176]{1,0:T(8,128)(2,1)} %all-gather.10.cloned.1.call-done), kind=kOutput, calls=%fused_computation.15 | convolution fusion | flops 9128902656 | bytes 17563648 | tf_op jit(solution)/shard_map/dot_general | solution.py:617
  361.1 15.3 %convolution_convert_fusion = bf16[2048,2176]{1,0:T(8,128)(2,1)} fusion(bf16[1024,2048]{1,0:T(8,128)(2,1)} %fusion.3, bf16[1024,2176]{1,0:T(8,128)(2,1)} %concatenate.80), kind=kOutput, calls=%fused_computation | convolution fusion | flops 9131261952 | bytes 17563648 | tf_op jit(solution)/shard_map/dot_general | solution.py:610
  376.4 1.3 copy-done.12
  377.9 8.4 convolution_convert_fusion.2
  387.8 7.2 convolution_convert_fusion.3
  395.1 1.8 copy-done.7
  397.9 1.2 maximum_bitcast_fusion
  399.1 1.6 fusion.44
  401.4 2.7 fusion.14
  404.0 44.7 %reduce-scatter.10.cloned.1.call-done = bf16[2,64,2048]{2,1,0:T(8,128)(2,1)} async-done(((bf16[2,512,2048]{2,1,0:T(8,128)(2,1)}), bf16[2,64,2048]{2,1,0:T(8,128)(2,1)}) %reduce-scatter.10.cloned.1.call-update) | async-done | bytes 524304 | tf_op jit(solution)/shard_map/reduce_scatter | solution.py:620
  448.7 1.5 fusion.24
  450.3 1.3 copy.102
  451.7 4.8 pad_maximum_fusion
  456.6 69.6 %reduce-scatter.12.cloned.1.call-done = bf16[512,2176]{1,0:T(8,128)(2,1)} async-done(((bf16[2048,2176]{1,0:T(8,128)(2,1)}), bf16[512,2176]{1,0:T(8,128)(2,1)}) %reduce-scatter.12.cloned.1.call-update) | async-done | bytes 2228240 | tf_op jit(solution)/shard_map/reduce_scatter | solution.py:613
  526.2 5.5 all-to-all-start.1
  531.6 128.3 %reduce-scatter.8.cloned.1.call-done = bf16[2,64,2048]{2,1,0:T(8,128)(2,1)} async-done(((bf16[2,512,2048]{2,1,0:T(8,128)(2,1)}), bf16[2,64,2048]{2,1,0:T(8,128)(2,1)}) %reduce-scatter.8.cloned.1.call-update) | async-done | bytes 524304 | tf_op jit(solution)/shard_map/reduce_scatter | solution.py:583
  660.0 2.9 fusion.20
  662.9 124.9 %reduce-scatter.16.cloned.1.call-done = f32[64,5]{1,0:T(8,128)} async-done(((f32[2048,5]{1,0:T(8,128)}), f32[64,5]{1,0:T(8,128)}) %reduce-scatter.16.cloned.1.call-update) | async-done | bytes 1296
  788.7 62.8 %reduce-scatter.14.cloned.1.call-done = bf16[1,352,2048]{2,1,0:T(8,128)(2,1)} async-done(((bf16[4,352,2048]{2,1,0:T(8,128)(2,1)}), bf16[1,352,2048]{2,1,0:T(8,128)(2,1)}) %reduce-scatter.14.cloned.1.call-update) | async-done | bytes 1441808 | tf_op jit(solution)/shard_map/reduce_scatter | solution.py:601
  851.5 1.2 dynamic-slice_bitcast_fusion
  852.7 1.5 collective-permute-start.1
  854.8 1.3 slice_bitcast_fusion
  856.1 9.7 %collective-permute-done.1 = bf16[128,2048]{1,0:T(8,128)(2,1)S(1)} collective-permute-done((bf16[128,2048]{1,0:T(8,128)(2,1)S(1)}, bf16[128,2048]{1,0:T(8,128)(2,1)S(1)}, u32[]{:S(2)}, u32[]{:S(2)}) %collective-permute-start.1) | collective-permute-done | bytes 524320 | tf_op jit(solution)/shard_map/ppermute | solution.py:604
  865.8 6.9 multiply_add_fusion.1
  873.0 1.3 fusion.45
  875.5 1.1 copy.97
  877.6 1.1 copy.98
  880.8 1.1 copy.100
  887.1 12.3 %multiply_add_fusion = (f32[64,17408]{1,0:T(8,128)}, f32[64,17408]{1,0:T(8,128)}, f32[64,17408]{1,0:T(8,128)}, f32[64,17408]{1,0:T(8,128)}) fusion(f32[64,17408]{1,0:T(8,128)} %param.23, f32[64,17408]{1,0:T(8,128)} %param.20, f32[64,17408]{1,0:T(8,128)} %param.21, f32[64,17408]{1,0:T(8,128)} %param.22, bf16[64,17408]{1,0:T(8,128)(2,1)S(1)} %constant_dynamic-update-slice_fusion), kind=kLoop, calls=%fused_computation.10 | loop fusion | flops 22282240 | bytes 37879808 | tf_op jit(solution)/shard_map/add | solution.py:81
  (143 shorter events, 22.8 us)
Async XLA Ops:
  7.2 227.2 %all-gather.8.cloned.1.call-start = ((), (), s32[]{:S(2)}) async-start(), calls=%async_computation.7 | async-start | bytes 4718592 | tf_op jit(solution)/shard_map/all_gather | solution.py:535
  7.9 234.4 %all-gather.12.cloned.1.call-start = ((), (), s32[]{:S(2)}) async-start(), calls=%async_computation.9 | async-start | bytes 7208960 | tf_op jit(solution)/shard_map/all_gather | solution.py:521
  9.7 14.2 %collective-permute-start = (bf16[128,2048]{1,0:T(8,128)(2,1)S(1)}, bf16[128,2048]{1,0:T(8,128)(2,1)S(1)}, u32[]{:S(2)}, u32[]{:S(2)}) collective-permute-start(bf16[128,2048]{1,0:T(8,128)(2,1)S(1)} %slice.180), channel_id=1, source_target_pairs={{0,7},{1,0},{2,1},{3,2},{4,3},{5,4},{6,5},{7,6},{8,15},{9,8},{10,9... | collective-permute-start | bytes 1572872 | tf_op jit(solution)/shard_map/ppermute | solution.py:515
  27.0 226.2 %all-gather.14.cloned.1.call-start = ((), (), s32[]{:S(2)}) async-start(), calls=%async_computation.10 | async-start | bytes 4718592 | tf_op jit(solution)/shard_map/all_gather | solution.py:536
  27.7 277.3 %all-gather.10.cloned.1.call-start = ((), (), s32[]{:S(2)}) async-start(), calls=%async_computation.8 | async-start | bytes 11141120 | tf_op jit(solution)/shard_map/all_gather | solution.py:508
  45.7 85.6 %copy-start.17 = (f32[64,5]{0,1:T(8,128)S(1)}, f32[64,5]{0,1:T(8,128)}, u32[]{:S(2)}) copy-start(f32[64,5]{0,1:T(8,128)} %param.28) | copy-start | bytes 3844
  45.7 145.3 %copy-start.21 = (s32[2,64]{1,0:T(2,128)S(1)}, s32[2,64]{1,0:T(2,128)}, u32[]{:S(2)}) copy-start(s32[2,64]{1,0:T(2,128)} %param.19) | copy-start | bytes 1540
  131.2 317.5 %reduce-scatter.10.cloned.1.call-start = ((), (), s32[]{:S(2)}) async-start(), calls=%async_computation.12 | async-start | bytes 4718592 | tf_op jit(solution)/shard_map/reduce_scatter | solution.py:620
  209.9 2.3 copy-start.22
  234.4 3.5 copy-start.1
  266.5 52.9 %copy-start.2 = (bf16[960,1024]{0,1:T(8,128)(2,1)}, bf16[960,1024]{0,1:T(8,128)(2,1)S(1)}, u32[]{:S(2)}) copy-start(bf16[960,1024]{0,1:T(8,128)(2,1)S(1)} %copy.88) | copy-start | bytes 5898244
  319.3 4.8 copy-start
  324.2 14.5 %copy-start.5 = (bf16[1024,704]{1,0:T(8,128)(2,1)S(1)}, bf16[1024,704]{1,0:T(8,128)(2,1)}, u32[]{:S(2)}) copy-start(bf16[1024,704]{1,0:T(8,128)(2,1)} %get-tuple-element.37) | copy-start | bytes 4325380
  324.2 14.5 %copy-start.6 = (bf16[1024,704]{1,0:T(8,128)(2,1)S(1)}, bf16[1024,704]{1,0:T(8,128)(2,1)}, u32[]{:S(2)}) copy-start(bf16[1024,704]{1,0:T(8,128)(2,1)} %get-tuple-element.38) | copy-start | bytes 4325380
  361.0 165.1 %reduce-scatter.12.cloned.1.call-start = ((), (), s32[]{:S(2)}) async-start(), calls=%async_computation.13 | async-start | bytes 11141120 | tf_op jit(solution)/shard_map/reduce_scatter | solution.py:613
  376.3 1.4 copy-start.12
  376.3 1.5 copy-start.24
  376.4 283.6 %reduce-scatter.8.cloned.1.call-start = ((), (), s32[]{:S(2)}) async-start(), calls=%async_computation.11 | async-start | bytes 4718592 | tf_op jit(solution)/shard_map/reduce_scatter | solution.py:583
  386.3 1.1 copy-start.3
  386.3 401.5 %reduce-scatter.16.cloned.1.call-start = ((), (), s32[]{:S(2)}) async-start(), calls=%async_computation.15 | async-start | bytes 1081344
  395.0 1.9 copy-start.7
  395.0 2.0 copy-start.8
  395.0 2.0 copy-start.9
  395.0 2.6 copy-start.10
  400.7 0.7 copy-start.23
  451.6 399.8 %reduce-scatter.14.cloned.1.call-start = ((), (), s32[]{:S(2)}) async-start(), calls=%async_computation.14 | async-start | bytes 7208960 | tf_op jit(solution)/shard_map/reduce_scatter | solution.py:601
  456.6 203.4 %copy-start.11 = (bf16[2,64,2048]{2,1,0:T(8,128)(2,1)S(1)}, bf16[2,64,2048]{2,1,0:T(8,128)(2,1)}, u32[]{:S(2)}) copy-start(bf16[2,64,2048]{2,1,0:T(8,128)(2,1)} %param.17) | copy-start | bytes 1572868
  526.2 346.6 %all-to-all-start.1 = ((bf16[8,64,2176]{2,1,0:T(8,128)(2,1)}), bf16[8,64,2176]{2,1,0:T(8,128)(2,1)S(1)}, u32[]{:S(2)}, u32[]{:S(2)}) async-start(bf16[8,64,2176]{2,1,0:T(8,128)(2,1)} %bitcast.132), calls=%async_computation.4 | async-start | bytes 4456448 | tf_op jit(solution)/shard_map/all_to_all | solution.py:614
  531.6 322.6 %copy-start.18 = (f32[64,5]{0,1:T(8,128)S(1)}, f32[64,5]{0,1:T(8,128)}, u32[]{:S(2)}) copy-start(f32[64,5]{0,1:T(8,128)} %param.31) | copy-start | bytes 3844
  531.6 322.6 %copy-start.19 = (f32[64,5]{0,1:T(8,128)S(1)}, f32[64,5]{0,1:T(8,128)}, u32[]{:S(2)}) copy-start(f32[64,5]{0,1:T(8,128)} %param.29) | copy-start | bytes 3844
  531.6 322.6 %copy-start.20 = (f32[64,5]{0,1:T(8,128)S(1)}, f32[64,5]{0,1:T(8,128)}, u32[]{:S(2)}) copy-start(f32[64,5]{0,1:T(8,128)} %param.30) | copy-start | bytes 3844
  788.7 84.1 %copy-start.16 = (f32[64,5]{0,1:T(8,128)}, f32[64,5]{0,1:T(8,128)S(1)}, u32[]{:S(2)}) copy-start(f32[64,5]{0,1:T(8,128)S(1)} %copy.103) | copy-start | bytes 3844
  851.5 14.3 %copy-start.4 = (f32[240,2048]{1,0:T(8,128)S(1)}, f32[240,2048]{1,0:T(8,128)}, u32[]{:S(2)}) copy-start(f32[240,2048]{1,0:T(8,128)} %param.24) | copy-start | bytes 5898244
  852.7 13.1 %collective-permute-start.1 = (bf16[128,2048]{1,0:T(8,128)(2,1)S(1)}, bf16[128,2048]{1,0:T(8,128)(2,1)S(1)}, u32[]{:S(2)}, u32[]{:S(2)}) collective-permute-start(bf16[128,2048]{1,0:T(8,128)(2,1)S(1)} %dynamic-slice_bitcast_fusion), channel_id=1, source_target_pairs={{0,1},{1,2},{2,3},{3,4},{4,5},{5,6},{6,7},{7,0},{8,9},{9,10},{10,1... | collective-permute-start | bytes 1572872 | tf_op jit(solution)/shard_map/ppermute | solution.py:604
  879.8 5.3 copy-start.13
  883.0 4.0 copy-start.14
  884.0 3.1 copy-start.15
Sparse Core Ops, SparseCore 0:
  10.2 109.5 all-gather.7
  121.9 45.9 all-gather.11
  170.1 70.8 all-gather.13
  242.4 62.5 all-gather.9
  361.1 87.5 reduce-scatter.9
  451.3 74.7 reduce-scatter.11
  530.8 129.1 reduce-scatter.7
  662.8 124.9 reduce-scatter.15
  790.5 60.8 reduce-scatter.13

commit v2 on v1

--- a/solution.py
+++ b/solution.py
@@ -384,7 +384,19 @@
     q_ref, k_ref, v_ref, bq_ref, bk_ref, bv_ref, da_ref, rope_ref, seg_q_ref, seg_k_ref,
     o_ref, dq_ref, dk_ref, dv_ref, *, head_size, half_rot,
 ):
-    cos, sin_low, sin_high = rope_ref[0], rope_ref[1], rope_ref[2]
+    def whole(v):
+        across, depth = v.shape[:2]
+        parts = [v[x, z].reshape(v.shape[-2:]) for z in range(depth) for x in range(across)]
+        return jnp.concatenate(parts, axis=0)
+
+    def store(ref, v):
+        across, depth, _, some, _ = ref.shape
+        for z in range(depth):
+            for x in range(across):
+                at = (z * across + x) * some
+                ref[x, z, 0] = v[at : at + some].astype(ref.dtype)
+
+    cos, sin_low, sin_high = (whole(rope_ref[i]) for i in range(3))
     tokens, lanes = cos.shape
     scale = head_size ** (-0.5)
 
@@ -395,11 +407,11 @@
             + way * pltpu.roll(v, half_rot, 1) * sin_high
         )
 
-    query = (turn(q_ref[...] + bq_ref[...], 1.0)).astype(jnp.bfloat16) * scale
+    query = (turn(whole(q_ref[...]) + bq_ref[...], 1.0)).astype(jnp.bfloat16) * scale
     query = query.astype(jnp.bfloat16)
-    key = turn(k_ref[...] + bk_ref[...], 1.0).astype(jnp.bfloat16)
-    value = (v_ref[...] + bv_ref[...]).astype(jnp.bfloat16)
-    d_att = da_ref[...]
+    key = turn(whole(k_ref[...]) + bk_ref[...], 1.0).astype(jnp.bfloat16)
+    value = (whole(v_ref[...]) + bv_ref[...]).astype(jnp.bfloat16)
+    d_att = whole(da_ref[...])
     place_q = lax.broadcasted_iota(jnp.int32, (tokens, tokens), 0)
     place_k = lax.broadcasted_iota(jnp.int32, (tokens, tokens), 1)
     mask = (seg_q_ref[0] == seg_k_ref[0]) & (place_k <= place_q)
@@ -428,26 +440,31 @@
         d_query = d_query + jnp.where(mine, dot(d_score, key, (((1,), (0,)), ((), ()))), 0.0)
         d_key = d_key + dot(d_score, q_h, tn)
         d_value = d_value + dot(probs_low, da_h, tn)
-    o_ref[...] = att.astype(jnp.bfloat16)
-    dq_ref[...] = turn(d_query * scale, -1.0).astype(jnp.bfloat16)
-    dk_ref[...] = turn(d_key, -1.0).astype(jnp.bfloat16)
-    dv_ref[...] = d_value.astype(jnp.bfloat16)
-
-
-def attention_both(proj, bias, d_joined, rope, seg, rows, tokens, att_rows, head_size):
+    store(o_ref, att)
+    store(dq_ref, turn(d_query * scale, -1.0))
+    store(dk_ref, turn(d_key, -1.0))
+    store(dv_ref, d_value)
+
+
+def attention_both(proj, bias, d_joined, rope, seg, n_seq, att_rows, head_size):
+    rows, tokens = seg.shape
     lanes = 2 * head_size
     pairs = att_rows // lanes
-    block = lambda first: pl.BlockSpec((tokens, lanes), lambda r, h: (r, first + h))
+    order = (2, n_seq // 2, rows, tokens // n_seq)
+    wide = lambda v: v.reshape(order + v.shape[-1:])
+    shape = (2, n_seq // 2, 1, tokens // n_seq, lanes)
+    block = lambda first: pl.BlockSpec(shape, lambda r, h: (0, 0, r, 0, first + h))
     row = lambda first: pl.BlockSpec((1, lanes), lambda r, h: (0, first + h))
-    out = jax.ShapeDtypeStruct((rows * tokens, att_rows), jnp.bfloat16)
-    return pl.pallas_call(
+    out = jax.ShapeDtypeStruct(order + (att_rows,), jnp.bfloat16)
+    proj, d_joined = wide(proj), wide(d_joined)
+    results = pl.pallas_call(
         functools.partial(attention_kernel, head_size=head_size, half_rot=ROT // 2),
         grid=(rows, pairs),
         in_specs=[
             block(0), block(pairs), block(2 * pairs),
             row(0), row(pairs), row(2 * pairs),
             block(0),
-            pl.BlockSpec((3, tokens, lanes), lambda r, h: (0, r, 0)),
+            pl.BlockSpec((3,) + shape, lambda r, h: (0, 0, 0, r, 0, 0)),
             pl.BlockSpec((1, tokens, 1), lambda r, h: (r, 0, 0)),
             pl.BlockSpec((1, 1, tokens), lambda r, h: (r, 0, 0)),
         ],
@@ -460,8 +477,355 @@
             transcendentals=rows * pairs * 2 * tokens * tokens,
         ),
         name="attention",
-    )(proj, proj, proj, bias, bias, bias, d_joined, rope, seg[:, :, None], seg[:, None, :])
-
+    )(
+        proj, proj, proj, bias, bias, bias, d_joined,
+        rope.reshape((3,) + order + (lanes,)), seg[:, :, None], seg[:, None, :],
+    )
+    return [v.reshape(rows * tokens, att_rows) for v in results]
+
+MESH_ID = pl.DeviceIdType.MESH
+
+
+def remote(src, dst, send_sem, recv_sem, device):
+    return pltpu.make_async_remote_copy(
+        src_ref=src,
+        dst_ref=dst,
+        send_sem=send_sem,
+        recv_sem=recv_sem,
+        device_id=device,
+        device_id_type=MESH_ID,
+    )
+
+
+class Place:
+    def __init__(self, n_seq):
+        self.n_seq = n_seq
+        self.depth = n_seq // 2
+        self.p, self.s = lax.axis_index("dp"), lax.axis_index("seq")
+        self.y, self.c = self.p // 2, lax.rem(self.p, 2)
+        self.z, self.x = self.s // 2, lax.rem(self.s, 2)
+        self.p_y = (1 - self.y) * 2 + self.c
+        self.p_c = self.y * 2 + 1 - self.c
+        self.p_d = (1 - self.y) * 2 + 1 - self.c
+        self.to_y = (self.p_y, self.s)
+        self.to_c = (self.p_c, self.s)
+        self.to_x = (self.p, self.z * 2 + 1 - self.x)
+        self.to_up = (self.p, self.s + 2)
+        self.to_down = (self.p, self.s - 2)
+
+    def seq(self, hop):
+        return lax.rem(self.s + hop + self.n_seq, self.n_seq)
+
+    def meet(self):
+        barrier = pltpu.get_barrier_semaphore()
+
+        def greet(hop, carry):
+            pl.semaphore_signal(
+                barrier, inc=1, device_id=(self.p, self.seq(hop)), device_id_type=MESH_ID
+            )
+            return carry
+
+        lax.fori_loop(1, self.n_seq, greet, 0)
+        for device in (self.to_y, self.to_c):
+            pl.semaphore_signal(barrier, inc=1, device_id=device, device_id_type=MESH_ID)
+        pl.semaphore_wait(barrier, self.n_seq + 1)
+
+
+class Spread:
+    def __init__(self, at, own, full, sems):
+        self.at, self.own, self.full, self.sems = at, own, full, sems
+
+    def along(self, src, up, ref=None):
+        sems, at = self.sems, self.at
+        here = self.full.at[at.x, src]
+        return remote(
+            here if ref is None else ref,
+            here,
+            sems.at[0 if up else 1, src],
+            sems.at[3, src],
+            at.to_up if up else at.to_down,
+        )
+
+    def across(self, src, ref=None):
+        sems, at = self.sems, self.at
+        here = self.full.at[at.x, src]
+        return remote(here if ref is None else ref, here, sems.at[2, src], sems.at[4, src], at.to_x)
+
+    def local(self):
+        return pltpu.make_async_copy(
+            self.own, self.full.at[self.at.x, self.at.z], self.sems.at[5, 0]
+        )
+
+    def begin(self):
+        at = self.at
+
+        @pl.when(at.z < at.depth - 1)
+        def _():
+            self.along(at.z, True, self.own).start()
+
+        @pl.when(at.z > 0)
+        def _():
+            self.along(at.z, False, self.own).start()
+
+        self.across(at.z, self.own).start()
+        self.local().start()
+
+    def step(self, hop):
+        at = self.at
+
+        @pl.when(at.z - hop >= 0)
+        def _():
+            src = at.z - hop
+            self.along(src, True).wait_recv()
+
+            @pl.when(at.z < at.depth - 1)
+            def _():
+                self.along(src, True).start()
+
+            self.across(src).start()
+
+        @pl.when(at.z + hop < at.depth)
+        def _():
+            src = at.z + hop
+            self.along(src, False).wait_recv()
+
+            @pl.when(at.z > 0)
+            def _():
+                self.along(src, False).start()
+
+            self.across(src).start()
+
+    def arrive(self):
+        at = self.at
+        for src in range(at.depth):
+            here = self.full.at[1 - at.x, src]
+            remote(here, here, self.sems.at[2, src], self.sems.at[4, src], at.to_x).wait_recv()
+        self.local().wait()
+
+    def sent(self):
+        at = self.at
+        for src in range(at.depth):
+            self.across(src).wait_send()
+
+            @pl.when((at.z < at.depth - 1) & (src <= at.z))
+            def _():
+                self.along(src, True).wait_send()
+
+            @pl.when((at.z > 0) & (src >= at.z))
+            def _():
+                self.along(src, False).wait_send()
+
+
+class Fan:
+    def __init__(self, at, pick, sems):
+        self.at, self.pick, self.sems = at, pick, sems
+
+    def y(self, k, ref=None):
+        at = self.at
+        here = self.pick(at.p, k)
+        return remote(here if ref is None else ref, here, self.sems.at[0, k], self.sems.at[1, k], at.to_y)
+
+    def core(self, k, ref=None):
+        at = self.at
+        here = self.pick(at.p, k)
+        return remote(here if ref is None else ref, here, self.sems.at[2, k], self.sems.at[3, k], at.to_c)
+
+    def pass_on(self, k):
+        at = self.at
+        here = self.pick(at.p_y, k)
+        return remote(here, here, self.sems.at[4, k], self.sems.at[5, k], at.to_c)
+
+    def from_y(self, k):
+        here = self.pick(self.at.p_y, k)
+        return remote(here, here, self.sems.at[0, k], self.sems.at[1, k], self.at.to_y)
+
+    def from_core(self, k):
+        here = self.pick(self.at.p_c, k)
+        return remote(here, here, self.sems.at[2, k], self.sems.at[3, k], self.at.to_c)
+
+    def from_diagonal(self, k):
+        here = self.pick(self.at.p_d, k)
+        return remote(here, here, self.sems.at[4, k], self.sems.at[5, k], self.at.to_c)
+
+
+def loop(low, high, body):
+    def step(k, carry):
+        body(k)
+        return carry
+
+    lax.fori_loop(low, high, step, 0)
+
+
+def gather_kernel(
+    x_ref, g_ref, w_ref, o_ref, tile_ref,
+    x_full, g_full, w_full, o_full, tiles,
+    x_sems, g_sems, w_sems, w_fan_sems, o_sems, o_fan_sems, t_sems, t_fan_sems, local_sems,
+    *, n_seq, late,
+):
+    at = Place(n_seq)
+    own = o_ref.shape[0]
+    body, extra = pl.ds(0, own), pl.ds(own, late)
+    x_go = Spread(at, x_ref, x_full, x_sems)
+    g_go = Spread(at, g_ref, g_full, g_sems)
+    w_fan = Fan(at, lambda p, k: w_full.at[p, k], w_fan_sems)
+    o_fan = Fan(at, lambda p, k: o_full.at[p, body if k == 0 else extra], o_fan_sems)
+    t_fan = Fan(at, lambda p, k: tiles.at[p], t_fan_sems)
+
+    def w_send(hop):
+        to = at.seq(hop)
+        return remote(w_ref.at[to], w_full.at[at.p, at.s], w_sems.at[0, to], w_sems.at[1, at.s], (at.p, to))
+
+    def w_recv(hop):
+        src = at.seq(-hop)
+        here = w_full.at[at.p, src]
+        return remote(here, here, w_sems.at[0, src], w_sems.at[1, src], (at.p, src))
+
+    def t_send(hop):
+        to = at.seq(hop)
+        return remote(tile_ref, tiles.at[at.p, at.s], t_sems.at[0, to], t_sems.at[1, at.s], (at.p, to))
+
+    def t_recv(hop):
+        src = at.seq(-hop)
+        here = tiles.at[at.p, src]
+        return remote(here, here, t_sems.at[0, src], t_sems.at[1, src], (at.p, src))
+
+    w_local = pltpu.make_async_copy(w_ref.at[at.s], w_full.at[at.p, at.s], local_sems.at[0])
+    o_local = pltpu.make_async_copy(o_ref, o_full.at[at.p, body], local_sems.at[1])
+    t_local = pltpu.make_async_copy(tile_ref, tiles.at[at.p, at.s], local_sems.at[2])
+    head = o_ref.at[pl.ds(0, late)]
+    o_send = remote(
+        head, o_full.at[at.p, extra], o_sems.at[0], o_sems.at[1], (at.p, at.seq(-1))
+    )
+
+    at.meet()
+    x_go.begin()
+    loop(1, n_seq, lambda hop: t_send(hop).start())
+    t_local.start()
+    w_fan.y(at.s, w_ref.at[at.s]).start()
+    loop(1, n_seq, lambda hop: w_send(hop).start())
+    w_fan.core(at.s, w_ref.at[at.s]).start()
+    w_local.start()
+    o_fan.core(0, o_ref).start()
+    o_local.start()
+    for hop in range(1, at.depth):
+        x_go.step(hop)
+    g_go.begin()
+    t_local.wait()
+    loop(1, n_seq, lambda hop: t_recv(hop).wait_recv())
+    t_fan.y(0).start()
+    t_fan.core(0).start()
+
+    @pl.when(at.y == 0)
+    def _():
+        o_send.start()
+
+    def w_step(hop):
+        src = at.seq(-hop)
+        w_recv(hop).wait_recv()
+        w_fan.y(src).start()
+        w_fan.core(src).start()
+
+    loop(1, n_seq, w_step)
+    t_fan.from_y(0).wait_recv()
+    t_fan.pass_on(0).start()
+    o_fan.y(0, o_ref).start()
+    for hop in range(1, at.depth):
+        g_go.step(hop)
+
+    @pl.when(at.y == 0)
+    def _():
+        o_send.wait_recv()
+        o_fan.y(1).start()
+        o_fan.core(1).start()
+
+    def w_pass(hop):
+        src = at.seq(-hop)
+        w_fan.from_y(src).wait_recv()
+        w_fan.pass_on(src).start()
+
+    loop(0, n_seq, w_pass)
+    o_fan.from_y(0).wait_recv()
+    o_fan.pass_on(0).start()
+
+    @pl.when(at.y == 1)
+    def _():
+        o_fan.from_y(1).wait_recv()
+        o_fan.pass_on(1).start()
+
+    x_go.arrive()
+    g_go.arrive()
+    w_local.wait()
+    o_local.wait()
+    t_fan.from_core(0).wait_recv()
+    t_fan.from_diagonal(0).wait_recv()
+    o_fan.from_core(0).wait_recv()
+    o_fan.from_diagonal(0).wait_recv()
+
+    @pl.when(at.y == 0)
+    def _():
+        o_fan.from_core(1).wait_recv()
+
+    @pl.when(at.y == 1)
+    def _():
+        o_fan.from_diagonal(1).wait_recv()
+
+    def w_last(k):
+        w_fan.from_core(k).wait_recv()
+        w_fan.from_diagonal(k).wait_recv()
+        w_fan.y(k).wait_send()
+        w_fan.core(k).wait_send()
+        w_fan.pass_on(k).wait_send()
+
+    loop(0, n_seq, w_last)
+
+    x_go.sent()
+    g_go.sent()
+
+    def seq_sent(hop):
+        w_send(hop).wait_send()
+        t_send(hop).wait_send()
+
+    loop(1, n_seq, seq_sent)
+    for fan in (t_fan, o_fan):
+        fan.y(0).wait_send()
+        fan.core(0).wait_send()
+        fan.pass_on(0).wait_send()
+
+    @pl.when(at.y == 0)
+    def _():
+        o_send.wait_send()
+        o_fan.y(1).wait_send()
+        o_fan.core(1).wait_send()
+
+    @pl.when(at.y == 1)
+    def _():
+        o_fan.pass_on(1).wait_send()
+
+
+def gather_all(n_dp, n_seq, late, x, g, w, o, tile):
+    depth = n_seq // 2
+    own, width = o.shape
+    rest = pl.BlockSpec(memory_space=pl.ANY)
+    dma = pltpu.SemaphoreType.DMA
+    like = lambda lead, ref: jax.ShapeDtypeStruct(lead + ref.shape, ref.dtype)
+    return pl.pallas_call(
+        functools.partial(gather_kernel, n_seq=n_seq, late=late),
+        in_specs=[rest] * 5,
+        out_specs=[rest] * 5,
+        out_shape=[
+            like((2, depth), x),
+            like((2, depth), g),
+            jax.ShapeDtypeStruct((n_dp,) + w.shape, w.dtype),
+            jax.ShapeDtypeStruct((n_dp, own + late, width), o.dtype),
+            like((n_dp, n_seq), tile),
+        ],
+        scratch_shapes=[
+            dma((6, depth)), dma((6, depth)), dma((2, n_seq)), dma((6, n_seq)),
+            dma((2,)), dma((6, 2)), dma((2, n_seq)), dma((6, 1)), dma((3,)),
+        ],
+        compiler_params=pltpu.CompilerParams(collective_id=0, has_side_effects=True),
+        name="gather_all",
+    )(x, g, w, o, tile)
 
 def split_heads(
     n_dp, n_seq, tokens, cotangent, segment_ids, doc_positions,
@@ -503,39 +867,45 @@
             at += size
         return jnp.concatenate(parts, axis=1)
 
-    in_low = lax.all_to_all(share(in_weight.astype(bf16)), "seq", 0, 0, tiled=True)
-    in_low = in_low.reshape(n_seq * in_rows, 3 * att + 2 * act_all)
-    in_low = lax.all_gather(in_low, "dp", axis=0, tiled=True)
-    small_low = lax.all_gather(small_params.astype(bf16), ("dp", "seq"), axis=0, tiled=True)
-    small_low = small_low.astype(f32)
-    gain, shift = small_low[:, 0], small_low[:, 1]
-    bias = lax.dynamic_slice_in_dim(small_low[:, 2:5], s * att, att, 0).T.reshape(1, 3 * att)
-
     out_low = out_weight.astype(bf16)
-    from_next = lax.ppermute(out_low[:late], "seq", [(k, (k - 1) % n_seq) for k in range(n_seq)])
-    start = jnp.where(p == 0, lead * s, jnp.where(p == 1, late - lead * s, 0))
-    joined_rows = jnp.concatenate([out_low, from_next, out_low[:lead]], axis=0)
-    main = lax.dynamic_slice_in_dim(joined_rows, start, att, 0)
-    late_slot = jnp.concatenate([main[: act[0]], from_next], axis=0)
-    plain_slot = jnp.concatenate([main, main[: slot - att]], axis=0)
-    slots = lax.all_gather(jnp.where(p == 1, late_slot, plain_slot), "dp", axis=0)
+    small_low = small_params.astype(bf16).astype(f32).T
+    widen = lambda v, n: jnp.pad(v, ((0, n - v.shape[0]), (0, 128 - v.shape[1])))
+    tile = jnp.concatenate(
+        [
+            widen(small_low, 8),
+            widen(jnp.concatenate([segment_ids, doc_positions], axis=0).astype(f32), 8),
+        ],
+        axis=0,
+    )
+    x_full, g_full, in_low, slots, tiles = gather_all(
+        n_dp, n_seq, late, tokens, cotangent, share(in_weight.astype(bf16)), out_low, tile
+    )
+    x_full, g_full = x_full.reshape(all_tokens, width), g_full.reshape(all_tokens, width)
+    in_low = in_low.reshape(n_dp * n_seq * in_rows, 3 * att + 2 * act_all)
+
+    small_low = jnp.transpose(tiles[:, :, :5, :in_rows], (2, 0, 1, 3)).reshape(5, width)
+    gain, shift = small_low[0], small_low[1]
+    bias = lax.dynamic_slice_in_dim(small_low[2:5], s * att, att, 1).reshape(1, 3 * att)
+    docs = lax.dynamic_index_in_dim(tiles, p, 0, keepdims=False)[:, 8:, :own_tokens]
+    seg_full = jnp.transpose(docs[:, :rows], (1, 0, 2)).reshape(rows, row_tokens)
+    pos_full = docs[:, rows : 2 * rows].reshape(n_seq // 2, 2, rows, own_tokens)
+    pos_full = jnp.transpose(pos_full, (1, 0, 2, 3))
+
+    late_at = late - lead * s
+    first = lax.dynamic_slice_in_dim(slots[0], lead * s, att, 0)
+    second = lax.dynamic_slice_in_dim(slots[1], late_at, act[0], 0)
     last = s == n_seq - 1
     keep = att - late
     out_mine = jnp.concatenate(
         [
-            slots[0, :keep],
-            jnp.where(last, slots[1, act[0] : slot], slots[0, keep:att]),
-            slots[1, : act[0]],
+            first[:keep],
+            jnp.where(last, slots[1, own:], first[keep:]),
+            second,
             slots[2, :own],
             slots[3, :own],
         ],
         axis=0,
     )
-
-    x_full = lax.all_gather(tokens, "seq", axis=1, tiled=True).reshape(all_tokens, width)
-    g_full = lax.all_gather(cotangent, "seq", axis=1, tiled=True).reshape(all_tokens, width)
-    seg_full = lax.all_gather(segment_ids, "seq", axis=1, tiled=True)
-    pos_full = lax.all_gather(doc_positions, "seq", axis=1, tiled=True)
 
     def normalise(v):
         v = v.astype(f32)
@@ -564,7 +934,7 @@
         ]
     )
     att_low, d_query, d_key, d_value = attention_both(
-        proj, bias, d_joined, rope, seg_full, rows, row_tokens, att, head_size
+        proj, bias, d_joined, rope, seg_full, n_seq, att, head_size
     )
 
     gate = proj[:, 3 * att : 3 * att + act_all]
@@ -580,9 +950,12 @@
     )
 
     branch = jnp.dot(joined, out_mine, preferred_element_type=f32).astype(bf16)
-    branch = lax.psum_scatter(
-        branch.reshape(rows, row_tokens, width), "seq", scatter_dimension=1, tiled=True
-    )
+    def to_owner(v):
+        v = jnp.swapaxes(v.reshape(2, n_seq // 2, rows * own_tokens, width), 0, 1)
+        v = lax.psum_scatter(v.reshape(all_tokens, width), "seq", scatter_dimension=0, tiled=True)
+        return v.reshape(rows, own_tokens, width)
+
+    branch = to_owner(branch)
     output = (tokens.astype(f32) + branch.astype(f32)).astype(bf16)
 
     out_part = lax.dot_general(
@@ -617,9 +990,7 @@
     d_hidden = lax.dot_general(
         d_proj, in_low, (((1,), (1,)), ((), ())), preferred_element_type=f32
     ).astype(bf16)
-    d_hidden = lax.psum_scatter(
-        d_hidden.reshape(rows, row_tokens, width), "seq", scatter_dimension=1, tiled=True
-    ).astype(f32)
+    d_hidden = to_owner(d_hidden).astype(f32)
     normed, inv_std = normalise(tokens)
     d_normed = d_hidden * gain
     input_grad = cotangent.astype(f32) + inv_std * (

time: 920 us -> 825 us (0.90)
  blocking collectives: 179 us -> 0 us
  Pallas kernels: 14.5 us -> 165 us
  waiting for transfers between devices: 494 us -> 455 us
  matrix products: 70.7 us -> 58.1 us
  local copies, waits for them, and re-layouts: 67.3 us -> 57.9 us
    pallas_call x0 -> x1, Pallas kernels: none -> 151 us  [gather_all(): pl.pallas_call(functools.partial(gather_kernel, n_seq=n_seq, late=late),...]
    all_gather x3 -> x0, blocking collectives: 93.9 us -> none  [the longest x1 59 us: split_heads(): lax.all_gather(small_params.astype(bf16), ('dp', 'seq'), axis=0, tiled=True)]
    all_to_all x1 -> x0, blocking collectives: 85.5 us -> none  [split_heads(): lax.all_to_all(share(in_weight.astype(bf16)), 'seq', 0, 0, tiled=True)]
    all_gather x4 -> x0, waiting for transfers between devices: 38.5 us -> none  [the longest x1 38.5 us: split_heads(): in_low = lax.all_gather(in_low, 'dp', axis=0, tiled=True)]
    reduce_scatter x2, waiting for transfers between devices: 173 us -> 189 us  [to_owner(): lax.psum_scatter(v.reshape(all_tokens, width), 'seq', scatter_dimension=0...]
    ppermute x1 -> x0, waiting for transfers between devices: 13.9 us -> none  [split_heads(): lax.ppermute(out_low[:late], 'seq', [(k, (k - 1) % n_seq) for k in range(...]
    unnamed x73 -> x90, local copies, waits for them, and re-layouts: 18.6 us -> 13.8 us
    unnamed x10 -> x6, waiting for transfers between devices: 126 us -> 125 us
  transfers between devices with their start and end apart: 12 -> 7, of which waited for: 8 -> 6; matrix products, arithmetic and copies ran while one was open for 13% -> 7% of each run, Pallas kernels for 0% -> 0%
where the time goes in v2:
time: 825 us; the launch traced here: 816 us
  waiting for transfers between devices  455 us (55%)
  Pallas kernels  165 us (20%)
  matrix products  58.1 us (7%)
  local copies, waits for them, and re-layouts  57.9 us (7%)
  other arithmetic  57.5 us (7%)
  between operations  14.9 us (2%)
    reduce_scatter x2, waiting for transfers between devices, to_owner(): lax.psum_scatter(v.reshape(all_tokens, width), 'seq', scatter_dimension=0...  189 us
    pallas_call x1, Pallas kernels, gather_all(): pl.pallas_call(functools.partial(gather_kernel, n_seq=n_seq, late=late),...  151 us
    unnamed x6, waiting for transfers between devices  125 us
    reduce_scatter x1, waiting for transfers between devices, split_heads(): in_sum = lax.psum_scatter(in_part, 'dp', scatter_dimension=0, tiled=True)  68.3 us
    reduce_scatter x1, waiting for transfers between devices, split_heads(): lax.psum_scatter(out_slots, 'dp', scatter_dimension=0, tiled=True)[0]  62.7 us
    add x3, other arithmetic, adam_update(): average_new = average_keep * average + (1.0 - average_keep) * weight_new  20 us
  transfers between devices with their start and end apart: 7, of which 6 were waited for; matrix products, arithmetic and copies ran while one was open for 7% of the time, Pallas kernels for 0%

profile of v2, /device:TPU:11, one launch (start us, length us, event | category | flops | bytes accessed | tf_op | source)
XLA Modules:
  0.0 815.7 jit_solution(5134256667873349051)
XLA Ops:
  7.2 2.5 convert_element_type.104
  10.4 0.9 copy-done.5
  11.3 1.1 convert_element_type.105.o_ref
  16.0 3.8 concatenate.46
  19.9 150.7 %gather_all.1 = (bf16[2,4,2,64,2048]{4,3,2,1,0:T(8,128)(2,1)}, bf16[2,4,2,64,2048]{4,3,2,1,0:T(8,128)(2,1)}, bf16[4,8,64,2176]{3,2,1,0:T(8,128)(2,1)}, bf16[4,368,2048]{2,1,0:T(8,128)(2,1)}, f32[4,8,16,128]{3,2,1,0:T(8,128)}) custom-call(bf16[2,64,2048]{2,1,0:T(8,128)(2,1)} %x_ref.1, bf16[2,64,2048]{2,1,0:T(8,128)(2,1)} %g_ref.1, ...), custom_call_target="tpu_custom_call" | custom-call | tf_op jit(solution)/shard_map/gather_all/pallas_call | solution.py:811
  170.6 0.9 slice_bitcast_fusion.4
  171.6 0.8 dynamic-slice_bitcast_fusion.2
  172.5 0.7 broadcast_in_dim_reshape.7.seg_k_ref
  173.1 1.3 broadcast_in_dim_reshape.8.seg_q_ref
  174.4 3.0 convert_reduce_fusion
  177.9 1.2 multiply_reduce_fusion
  180.5 0.7 add.154
  181.2 1.9 multiply_cosine_fusion
  183.2 1.7 concatenate.51
  184.9 1.7 concatenate.52
  186.7 2.0 fusion.37
  188.7 0.8 fusion.28
  189.6 2.0 fusion.27
  191.5 1.0 bitcast_dynamic-update-slice_fusion.2
  192.5 2.2 bitcast_dynamic-update-slice_fusion.1
  194.7 2.2 bitcast_dynamic-update-slice_fusion
  197.0 1.7 concatenate.50
  198.8 8.1 convolution_convert_fusion.4
  206.9 2.0 add_convert_fusion
  208.9 9.9 %fusion.44 = f32[1024,2176]{1,0:T(8,128)S(1)} fusion(bf16[1024,2048]{1,0:T(8,128)(2,1)S(1)} %bitcast.127, bf16[2048,2176]{1,0:T(8,128)(2,1)S(1)} %bitcast.155), kind=kOutput, calls=%fused_computation.122 | convolution fusion | flops 9126805504 | bytes 22020096 | tf_op jit(solution)/shard_map/dot_general | solution.py:917
  218.9 4.0 fusion.8
  222.9 1.2 pad_maximum_fusion.2.rope_ref
  224.2 14.8 %attention.1 = (bf16[2,4,2,64,256]{4,3,2,1,0:T(8,128)(2,1)}, bf16[2,4,2,64,256]{4,3,2,1,0:T(8,128)(2,1)}, bf16[2,4,2,64,256]{4,3,2,1,0:T(8,128)(2,1)}, bf16[2,4,2,64,256]{4,3,2,1,0:T(8,128)(2,1)}) custom-call(f32[2,4,2,64,2176]{4,3,2,1,0:T(8,128)} %bitcast.114, f32[2,4,2,64,2176]{4,3,2,1,0:T(8,128)} %bitcast.115, f32[2,4,2,64,2176]{4,3,2,1,0:T(8,128)} %bitcast.116, ...), custom_call_target="tpu_custom_call" | custom-call | flops 3221225472 | bytes 5242880 | tf_op jit(solution)/shard_map/attention/pallas_call | solution.py:460
  239.0 7.2 concatenate.54
  246.2 13.8 %convolution_convert_fusion.1 = bf16[1024,2048]{1,0:T(8,128)(2,1)S(1)} fusion(bf16[1024,2176]{1,0:T(8,128)(2,1)} %concatenate.54, bf16[2048,2176]{1,0:T(8,128)(2,1)} %bitcast.152), kind=kOutput, calls=%fused_computation.16 | convolution fusion | flops 9128902656 | bytes 17563648 | tf_op jit(solution)/shard_map/dot_general | solution.py:990
  260.0 2.5 copy.83
  262.8 3.5 fusion.3
  266.2 12.3 %convolution_convert_fusion = bf16[2048,2176]{1,0:T(8,128)(2,1)} fusion(bf16[1024,2048]{1,0:T(8,128)(2,1)S(1)} %fusion.3, bf16[1024,2176]{1,0:T(8,128)(2,1)S(1)} %bitcast.126), kind=kOutput, calls=%fused_computation | convolution fusion | flops 9131261952 | bytes 17563648 | tf_op jit(solution)/shard_map/dot_general | solution.py:983
  278.6 1.3 copy-done.16
  280.1 6.9 convolution_convert_fusion.2
  286.9 2.3 copy.82
  289.3 7.3 convolution_convert_fusion.3
  296.7 2.0 copy-done.8
  300.1 1.6 fusion.38
  302.1 0.7 slice-done
  303.1 1.2 maximum_bitcast_fusion
  304.3 0.7 copy-done.9
  305.0 1.3 fusion.11
  306.3 61.1 %reduce-scatter.10.cloned.1.call-done = bf16[128,2048]{1,0:T(8,128)(2,1)} async-done(((bf16[1024,2048]{1,0:T(8,128)(2,1)}), bf16[128,2048]{1,0:T(8,128)(2,1)}) %reduce-scatter.10.cloned.1.call-update) | async-done | bytes 524304 | tf_op jit(solution)/shard_map/reduce_scatter | solution.py:955
  367.3 1.3 convert_reduce_fusion.3
  368.6 1.7 fusion.21
  370.3 1.3 copy.94
  371.7 4.8 pad_maximum_fusion
  376.6 68.3 %reduce-scatter.12.cloned.1.call-done = bf16[512,2176]{1,0:T(8,128)(2,1)} async-done(((bf16[2048,2176]{1,0:T(8,128)(2,1)}), bf16[512,2176]{1,0:T(8,128)(2,1)}) %reduce-scatter.12.cloned.1.call-update) | async-done | bytes 2228240 | tf_op jit(solution)/shard_map/reduce_scatter | solution.py:986
  444.9 5.5 all-to-all-start
  450.5 128.2 %reduce-scatter.8.cloned.1.call-done = bf16[128,2048]{1,0:T(8,128)(2,1)} async-done(((bf16[1024,2048]{1,0:T(8,128)(2,1)}), bf16[128,2048]{1,0:T(8,128)(2,1)}) %reduce-scatter.8.cloned.1.call-update) | async-done | bytes 524304 | tf_op jit(solution)/shard_map/reduce_scatter | solution.py:955
  578.7 2.9 fusion.20
  581.6 124.7 %reduce-scatter.16.cloned.1.call-done = f32[64,5]{1,0:T(8,128)} async-done(((f32[2048,5]{1,0:T(8,128)}), f32[64,5]{1,0:T(8,128)}) %reduce-scatter.16.cloned.1.call-update) | async-done | bytes 1296
  706.4 0.8 copy.95
  707.2 62.7 %reduce-scatter.14.cloned.1.call-done = bf16[1,352,2048]{2,1,0:T(8,128)(2,1)} async-done(((bf16[4,352,2048]{2,1,0:T(8,128)(2,1)}), bf16[1,352,2048]{2,1,0:T(8,128)(2,1)}) %reduce-scatter.14.cloned.1.call-update) | async-done | bytes 1441808 | tf_op jit(solution)/shard_map/reduce_scatter | solution.py:974
  769.9 1.2 dynamic-slice_bitcast_fusion.1
  771.1 1.3 collective-permute-start
  772.4 0.6 multiply_add_fusion.2
  773.1 1.3 slice_bitcast_fusion
  774.3 9.7 %collective-permute-done = bf16[128,2048]{1,0:T(8,128)(2,1)S(1)} collective-permute-done((bf16[128,2048]{1,0:T(8,128)(2,1)S(1)}, bf16[128,2048]{1,0:T(8,128)(2,1)S(1)}, u32[]{:S(2)}, u32[]{:S(2)}) %collective-permute-start) | collective-permute-done | bytes 524320 | tf_op jit(solution)/shard_map/ppermute | solution.py:977
  784.0 6.9 multiply_add_fusion.1
  791.2 1.4 fusion.39
  793.4 1.1 copy.92
  796.5 12.5 %multiply_add_fusion = (f32[64,17408]{1,0:T(8,128)}, f32[64,17408]{1,0:T(8,128)}, f32[64,17408]{1,0:T(8,128)}, f32[64,17408]{1,0:T(8,128)}) fusion(f32[64,17408]{1,0:T(8,128)} %param.23, f32[64,17408]{1,0:T(8,128)} %param.20, f32[64,17408]{1,0:T(8,128)} %param.21, f32[64,17408]{1,0:T(8,128)} %param.22, bf16[64,17408]{1,0:T(8,128)(2,1)S(1)} %constant_dynamic-update-slice_fusion), kind=kLoop, calls=%fused_computation.12 | loop fusion | flops 22282240 | bytes 37879808 | tf_op jit(solution)/shard_map/add | solution.py:81
  (164 shorter events, 12.0 us)
Async XLA Ops:
  7.2 360.2 %reduce-scatter.10.cloned.1.call-start = ((), (), s32[]{:S(2)}) async-start(), calls=%async_computation.7 | async-start | bytes 4718592 | tf_op jit(solution)/shard_map/reduce_scatter | solution.py:955
  9.7 0.7 copy-start.23
  9.7 1.6 copy-start.5
  12.8 2.6 copy-start.28
  12.8 2.6 copy-start.29
  174.4 3.4 copy-start.1
  197.0 11.9 %slice-start.4 = ((s8[8912896]{0:T(1024)(128)(4,1)}), s8[524288]{0:T(1024)(128)(4,1)S(1)}, s32[]{:S(2)}) async-start(s8[8912896]{0:T(1024)(128)(4,1)} %bitcast.153), calls=%async_computation.15 | async-start | bytes 1048576
  198.8 8.1 copy-start.2
  198.8 8.1 copy-start.20
  198.8 8.1 copy-start.21
  198.8 10.1 %slice-start.5 = ((s8[8912896]{0:T(1024)(128)(4,1)}), s8[4194304]{0:T(1024)(128)(4,1)S(1)}, s32[]{:S(2)}) async-start(s8[8912896]{0:T(1024)(128)(4,1)} %bitcast.153), calls=%async_computation.16 | async-start | bytes 8388608
  198.8 10.1 %slice-start.6 = ((s8[8912896]{0:T(1024)(128)(4,1)}), s8[4194304]{0:T(1024)(128)(4,1)S(1)}, s32[]{:S(2)}) async-start(s8[8912896]{0:T(1024)(128)(4,1)} %bitcast.153), calls=%async_computation.17 | async-start | bytes 8388608
  206.9 11.9 %copy-start.7 = (bf16[1024,960]{1,0:T(8,128)(2,1)}, bf16[1024,960]{1,0:T(8,128)(2,1)S(1)}, u32[]{:S(2)}) copy-start(bf16[1024,960]{1,0:T(8,128)(2,1)S(1)} %convolution_convert_fusion.4) | copy-start | bytes 5898244
  218.8 4.1 copy-start
  218.9 4.0 copy-start.13
  218.9 4.0 copy-start.14
  218.9 4.0 copy-start.15
  262.5 3.7 slice-start.2
  262.5 182.4 %reduce-scatter.12.cloned.1.call-start = ((), (), s32[]{:S(2)}) async-start(), calls=%async_computation.8 | async-start | bytes 11141120 | tf_op jit(solution)/shard_map/reduce_scatter | solution.py:986
  262.8 3.5 slice-start.3
  278.5 1.4 copy-start.16
  278.6 1.5 copy-start.31
  278.6 300.2 %reduce-scatter.8.cloned.1.call-start = ((), (), s32[]{:S(2)}) async-start(), calls=%async_computation.6 | async-start | bytes 4718592 | tf_op jit(solution)/shard_map/reduce_scatter | solution.py:955
  289.3 417.1 %reduce-scatter.16.cloned.1.call-start = ((), (), s32[]{:S(2)}) async-start(), calls=%async_computation.10 | async-start | bytes 1081344
  296.6 2.0 copy-start.8
  296.6 2.0 copy-start.10
  296.6 2.0 copy-start.11
  296.6 2.6 copy-start.12
  296.7 2.9 copy-start.3
  301.7 1.1 slice-start
  301.7 1.4 slice-start.1
  301.9 3.1 copy-start.9
  301.9 3.1 copy-start.30
  371.7 398.3 %reduce-scatter.14.cloned.1.call-start = ((), (), s32[]{:S(2)}) async-start(), calls=%async_computation.9 | async-start | bytes 7208960 | tf_op jit(solution)/shard_map/reduce_scatter | solution.py:974
  376.6 202.2 %copy-start.4 = (bf16[128,2048]{1,0:T(8,128)(2,1)S(1)}, bf16[128,2048]{1,0:T(8,128)(2,1)}, u32[]{:S(2)}) copy-start(bf16[128,2048]{1,0:T(8,128)(2,1)} %reduce-scatter.10.cloned.1.call-done) | copy-start | bytes 1572868
  444.9 346.0 %all-to-all-start = ((bf16[8,64,2176]{2,1,0:T(8,128)(2,1)}), bf16[8,64,2176]{2,1,0:T(8,128)(2,1)S(1)}, u32[]{:S(2)}, u32[]{:S(2)}) async-start(bf16[8,64,2176]{2,1,0:T(8,128)(2,1)} %bitcast.130), calls=%async_computation.3 | async-start | bytes 4456448 | tf_op jit(solution)/shard_map/all_to_all | solution.py:987
  450.4 322.0 %copy-start.24 = (f32[64,5]{0,1:T(8,128)S(1)}, f32[64,5]{0,1:T(8,128)}, u32[]{:S(2)}) copy-start(f32[64,5]{0,1:T(8,128)} %param.28) | copy-start | bytes 3844
  450.4 322.0 %copy-start.25 = (f32[64,5]{0,1:T(8,128)S(1)}, f32[64,5]{0,1:T(8,128)}, u32[]{:S(2)}) copy-start(f32[64,5]{0,1:T(8,128)} %param.31) | copy-start | bytes 3844
  450.4 322.0 %copy-start.26 = (f32[64,5]{0,1:T(8,128)S(1)}, f32[64,5]{0,1:T(8,128)}, u32[]{:S(2)}) copy-start(f32[64,5]{0,1:T(8,128)} %param.29) | copy-start | bytes 3844
  450.4 322.0 %copy-start.27 = (f32[64,5]{0,1:T(8,128)S(1)}, f32[64,5]{0,1:T(8,128)}, u32[]{:S(2)}) copy-start(f32[64,5]{0,1:T(8,128)} %param.30) | copy-start | bytes 3844
  707.2 83.7 %copy-start.22 = (f32[64,5]{0,1:T(8,128)}, f32[64,5]{0,1:T(8,128)S(1)}, u32[]{:S(2)}) copy-start(f32[64,5]{0,1:T(8,128)S(1)} %copy.95) | copy-start | bytes 3844
  769.9 14.1 %copy-start.6 = (f32[240,2048]{1,0:T(8,128)S(1)}, f32[240,2048]{1,0:T(8,128)}, u32[]{:S(2)}) copy-start(f32[240,2048]{1,0:T(8,128)} %param.24) | copy-start | bytes 5898244
  771.1 12.8 %collective-permute-start = (bf16[128,2048]{1,0:T(8,128)(2,1)S(1)}, bf16[128,2048]{1,0:T(8,128)(2,1)S(1)}, u32[]{:S(2)}, u32[]{:S(2)}) collective-permute-start(bf16[128,2048]{1,0:T(8,128)(2,1)S(1)} %dynamic-slice_bitcast_fusion.1), channel_id=1, source_target_pairs={{0,1},{1,2},{2,3},{3,4},{4,5},{5,6},{6,7},{7,0},{8,9},{9,10},{10,1... | collective-permute-start | bytes 1572872 | tf_op jit(solution)/shard_map/ppermute | solution.py:977
  792.6 2.3 copy-start.19
  792.6 2.8 copy-start.18
  792.7 3.1 copy-start.17
Sparse Core Ops, SparseCore 0:
  262.7 104.6 reduce-scatter.9
  370.1 74.7 reduce-scatter.11
  449.6 129.1 reduce-scatter.7
  581.4 124.9 reduce-scatter.15
  708.9 60.9 reduce-scatter.13

commit v3 on v2

--- a/solution.py
+++ b/solution.py
@@ -827,6 +827,333 @@
         name="gather_all",
     )(x, g, w, o, tile)
 
+def add_rows(out, terms, rows=32):
+    count = out.shape[0]
+
+    def some(k):
+        at = pl.ds(pl.multiple_of(k * rows, rows), rows)
+        total = terms[0][at].astype(jnp.float32)
+        for term in terms[1:]:
+            total = total + term[at].astype(jnp.float32)
+        out[at] = total.astype(out.dtype)
+
+    loop(0, count // rows, some)
+
+
+def reduce_kernel(
+    d_ref, b_ref, in_ref, out_ref, normed_ref, small_ref,
+    sums, in_sum, out_sum, out_prev, small_sum,
+    own_parts, x_got, z_got, in_own, in_core, in_y, out_own, out_core, out_y,
+    small_own, small_core, small_y, small_seq,
+    load_sems, x_sems, z_sems, in_core_sems, in_y_sems, in_sems, out_sems, small_sems, local_sem,
+    *, n_seq, late, starts, keep,
+):
+    at = Place(n_seq)
+    depth = at.depth
+    parts = (d_ref, b_ref)
+    main = out_own.shape[1] - late
+    body, extra = pl.ds(0, main), pl.ds(main, late)
+    y, c, z, x, s = at.y, at.c, at.z, at.x, at.s
+
+    def out_start(y_to, c_to):
+        one = jnp.where(y_to == 0, starts[1], starts[3])
+        zero = jnp.where(y_to == 0, starts[0], starts[2])
+        return pl.multiple_of(jnp.where(c_to == 0, zero, one), 16)
+
+    loads = [
+        pltpu.make_async_copy(parts[kind].at[x], own_parts.at[kind], load_sems.at[kind])
+        for kind in range(2)
+    ]
+    for y_to in range(2):
+        p_to = 2 * y_to + c
+        loads.append(pltpu.make_async_copy(in_ref.at[p_to], in_own.at[y_to], load_sems.at[2 + y_to]))
+        loads.append(
+            pltpu.make_async_copy(
+                out_ref.at[pl.ds(out_start(y_to, c), main)],
+                out_own.at[y_to, body],
+                load_sems.at[4 + y_to],
+            )
+        )
+    loads.append(
+        pltpu.make_async_copy(
+            out_ref.at[pl.ds(keep, late)], out_own.at[0, extra], load_sems.at[6]
+        )
+    )
+
+    def in_to_core(y_to, k):
+        return remote(
+            in_ref.at[2 * y_to + 1 - c, k], in_core.at[y_to, k],
+            in_core_sems.at[0, y_to, k], in_core_sems.at[1, y_to, k], at.to_c,
+        )
+
+    def out_to_core(y_to):
+        return remote(
+            out_ref.at[pl.ds(out_start(y_to, 1 - c), main)], out_core.at[y_to, body],
+            out_sems.at[0, y_to], out_sems.at[1, y_to], at.to_c,
+        )
+
+    extra_to_core = remote(
+        out_ref.at[pl.ds(keep, late)], out_core.at[0, extra],
+        out_sems.at[0, 2], out_sems.at[1, 2], at.to_c,
+    )
+
+    def to_across(kind, k):
+        return remote(
+            parts[kind].at[1 - x, k], x_got.at[kind, k],
+            x_sems.at[0, kind, k], x_sems.at[1, kind, k], at.to_x,
+        )
+
+    def to_depth(kind, k):
+        return remote(
+            x_got.at[kind, k], z_got.at[kind, z],
+            z_sems.at[0, kind, k], z_sems.at[1, kind, z], (at.p, 2 * k + x),
+        )
+
+    def from_depth(kind, k):
+        here = z_got.at[kind, k]
+        return remote(here, here, z_sems.at[0, kind, k], z_sems.at[1, kind, k], (at.p, 2 * k + x))
+
+    def in_to_y(k):
+        return remote(
+            in_core.at[1 - y, k], in_y.at[k], in_y_sems.at[0, k], in_y_sems.at[1, k], at.to_y
+        )
+
+    def in_to_owner(k):
+        return remote(
+            in_core.at[y, k], in_sum.at[s], in_sems.at[0, k], in_sems.at[1, s], (at.p, k)
+        )
+
+    def in_from(k):
+        here = in_sum.at[k]
+        return remote(here, here, in_sems.at[0, k], in_sems.at[1, k], (at.p, k))
+
+    in_keep = pltpu.make_async_copy(in_core.at[y, s], in_sum.at[s], local_sem.at[0])
+    out_to_y = remote(
+        out_core.at[1 - y, body], out_y.at[body], out_sems.at[0, 3], out_sems.at[1, 3], at.to_y
+    )
+    extra_to_y = remote(
+        out_core.at[0, extra], out_y.at[extra], out_sems.at[0, 4], out_sems.at[1, 4], at.to_y
+    )
+
+    def out_shift(start):
+        return remote(
+            out_sum.at[pl.ds(start, late)], out_prev,
+            out_sems.at[0, 5], out_sems.at[1, 5], (at.p, at.seq(1)),
+        )
+
+    small_to_core = remote(small_own, small_core, small_sems.at[0, 0], small_sems.at[1, 0], at.to_c)
+    small_to_y = remote(small_core, small_y, small_sems.at[0, 1], small_sems.at[1, 1], at.to_y)
+
+    def small_to(hop):
+        to = at.seq(hop)
+        return remote(
+            small_y, small_seq.at[s], small_sems.at[0, 2 + to], small_sems.at[1, 2 + s], (at.p, to)
+        )
+
+    def small_from(hop):
+        src = at.seq(-hop)
+        here = small_seq.at[src]
+        return remote(
+            here, here, small_sems.at[0, 2 + src], small_sems.at[1, 2 + src], (at.p, src)
+        )
+
+    def around_z(hop):
+        return lax.rem(z + hop, depth)
+
+    at.meet()
+    for hop in range(1, depth + 1):
+        to_across(0, around_z(hop)).start()
+    loop(0, n_seq, lambda hop: in_to_core(1 - y, at.seq(hop)).start())
+    for load in loads:
+        load.start()
+    loop(0, n_seq, lambda hop: in_to_core(y, at.seq(hop)).start())
+    out_to_core(1 - y).start()
+    out_to_core(y).start()
+    extra_to_core.start()
+    for hop in range(1, depth + 1):
+        to_across(1, around_z(hop)).start()
+    for load in loads:
+        load.wait()
+
+    def to_y_step(hop):
+        k = at.seq(hop)
+        in_to_core(1 - y, k).wait_recv()
+        add_rows(in_core.at[1 - y, k], [in_core.at[1 - y, k], in_own.at[1 - y, k]])
+        in_to_y(k).start()
+
+    loop(0, n_seq, to_y_step)
+    out_to_core(1 - y).wait_recv()
+    extra_to_core.wait_recv()
+    add_rows(out_core.at[1 - y, body], [out_core.at[1 - y, body], out_own.at[1 - y, body]])
+    out_to_y.start()
+
+    @pl.when(y == 1)
+    def _():
+        add_rows(out_core.at[0, extra], [out_core.at[0, extra], out_own.at[0, extra]])
+        extra_to_y.start()
+
+    def depth_step(kind, hop):
+        k = around_z(hop)
+        to_across(kind, k).wait_recv()
+        add_rows(x_got.at[kind, k], [x_got.at[kind, k], own_parts.at[kind, k]])
+        if hop < depth:
+            to_depth(kind, k).start()
+
+    def owner_step(hop):
+        k = at.seq(hop)
+        in_to_core(y, k).wait_recv()
+        in_to_y(k).wait_recv()
+        add_rows(in_core.at[y, k], [in_core.at[y, k], in_own.at[y, k], in_y.at[k]])
+
+        @pl.when(k != s)
+        def _():
+            in_to_owner(k).start()
+
+        @pl.when(k == s)
+        def _():
+            in_keep.start()
+
+    for hop in range(1, depth + 1):
+        depth_step(0, hop)
+        for one in range(n_seq // depth):
+            owner_step((hop - 1) * (n_seq // depth) + one + 1)
+
+    def finish(kind):
+        others = [around_z(hop) for hop in range(1, depth)]
+        for k in others:
+            from_depth(kind, k).wait_recv()
+        add_rows(
+            sums.at[kind], [x_got.at[kind, z]] + [z_got.at[kind, k] for k in others], rows=16
+        )
+
+    depth_step(1, 1)
+    finish(0)
+
+    small_own[...] = small_ref[...]
+    d_hidden = sums[0]
+    small_own[0:1, :] = jnp.sum(d_hidden * normed_ref[...], axis=0, keepdims=True)
+    small_own[1:2, :] = jnp.sum(d_hidden, axis=0, keepdims=True)
+    small_to_core.start()
+    depth_step(1, 2)
+    small_to_core.wait_recv()
+    small_core[...] = small_core[...] + small_own[...]
+    small_to_y.start()
+    out_to_core(y).wait_recv()
+    out_to_y.wait_recv()
+    add_rows(out_sum.at[body], [out_core.at[y, body], out_own.at[y, body], out_y.at[body]])
+
+    @pl.when(y == 0)
+    def _():
+        extra_to_y.wait_recv()
+        add_rows(out_sum.at[extra], [out_core.at[0, extra], out_own.at[0, extra], out_y.at[extra]])
+
+        @pl.when(c == 0)
+        def _():
+            out_shift(keep).start()
+
+        @pl.when((c == 1) & (s == n_seq - 1))
+        def _():
+            out_shift(main).start()
+
+        @pl.when((c == 1) & (s < n_seq - 1))
+        def _():
+            out_shift(starts[2] - starts[1] - late).start()
+
+    depth_step(1, 3)
+    small_to_y.wait()
+    small_y[...] = small_core[...] + small_y[...]
+    loop(1, n_seq, lambda hop: small_to(hop).start())
+    for hop in range(4, depth + 1):
+        depth_step(1, hop)
+    small_sum[...] = small_y[...]
+
+    def small_add(hop):
+        small_from(hop).wait_recv()
+        small_sum[...] = small_sum[...] + small_seq[at.seq(-hop)]
+
+    loop(1, n_seq, small_add)
+    finish(1)
+
+    @pl.when(y == 0)
+    def _():
+        out_shift(0).wait()
+
+    def in_last(hop):
+        k = at.seq(hop)
+        in_from(k).wait_recv()
+        in_to_owner(k).wait_send()
+
+    loop(1, n_seq, in_last)
+    in_keep.wait()
+
+    def seq_sent(k):
+        for y_to in range(2):
+            in_to_core(y_to, k).wait_send()
+        in_to_y(k).wait_send()
+
+    loop(0, n_seq, seq_sent)
+    loop(1, n_seq, lambda hop: small_to(hop).wait_send())
+    small_to_core.wait_send()
+    for y_to in range(2):
+        out_to_core(y_to).wait_send()
+    extra_to_core.wait_send()
+    out_to_y.wait_send()
+
+    @pl.when(y == 1)
+    def _():
+        extra_to_y.wait_send()
+
+    for kind in range(2):
+        for k in range(depth):
+            to_across(kind, k).wait_send()
+        for hop in range(1, depth):
+            to_depth(kind, around_z(hop)).wait_send()
+
+
+def reduce_all(n_dp, n_seq, late, starts, keep, d_part, b_part, in_part, out_part, normed, small):
+    depth = n_seq // 2
+    block = d_part.shape[2:]
+    in_block = in_part.shape[2:]
+    width = block[1]
+    main = starts[1] - starts[0]
+    slot = main + late
+    bf16, f32 = jnp.bfloat16, jnp.float32
+    rest, near = pl.BlockSpec(memory_space=pl.ANY), pl.BlockSpec(memory_space=pltpu.VMEM)
+    dma = pltpu.SemaphoreType.DMA
+    return pl.pallas_call(
+        functools.partial(reduce_kernel, n_seq=n_seq, late=late, starts=starts, keep=keep),
+        in_specs=[rest, rest, rest, rest, near, near],
+        out_specs=[near, rest, near, rest, near],
+        out_shape=[
+            jax.ShapeDtypeStruct((2,) + block, f32),
+            jax.ShapeDtypeStruct((n_seq,) + in_block, bf16),
+            jax.ShapeDtypeStruct((slot, width), bf16),
+            jax.ShapeDtypeStruct((late, width), bf16),
+            jax.ShapeDtypeStruct(small.shape, f32),
+        ],
+        scratch_shapes=[
+            pltpu.VMEM((2, depth) + block, bf16),
+            pltpu.VMEM((2, depth) + block, bf16),
+            pltpu.VMEM((2, depth) + block, bf16),
+            pltpu.VMEM((2, n_seq) + in_block, bf16),
+            pltpu.VMEM((2, n_seq) + in_block, bf16),
+            pltpu.VMEM((n_seq,) + in_block, bf16),
+            pltpu.VMEM((2, slot, width), bf16),
+            pltpu.VMEM((2, slot, width), bf16),
+            pltpu.VMEM((slot, width), bf16),
+            pltpu.VMEM(small.shape, f32),
+            pltpu.VMEM(small.shape, f32),
+            pltpu.VMEM(small.shape, f32),
+            pltpu.VMEM((n_seq,) + small.shape, f32),
+            dma((7,)), dma((2, 2, depth)), dma((2, 2, depth)), dma((2, 2, n_seq)), dma((2, n_seq)),
+            dma((2, n_seq)), dma((2, 6)), dma((2, 2 + n_seq)), dma((1,)),
+        ],
+        compiler_params=pltpu.CompilerParams(
+            collective_id=1, has_side_effects=True, vmem_limit_bytes=56 * 2**20
+        ),
+        name="reduce_all",
+    )(d_part, b_part, in_part, out_part, normed, small)
+
 def split_heads(
     n_dp, n_seq, tokens, cotangent, segment_ids, doc_positions,
     in_weight, in_first, in_second, in_average,
@@ -847,7 +1174,6 @@
     act_all = sum(act)
     cuts = [0, act[0] * n_seq, (act[0] + own) * n_seq, ffn]
     lead = att - own
-    slot = act[0] + late
     p, s = lax.axis_index("dp"), lax.axis_index("seq")
 
     def share(v):
@@ -896,6 +1222,7 @@
     second = lax.dynamic_slice_in_dim(slots[1], late_at, act[0], 0)
     last = s == n_seq - 1
     keep = att - late
+    spare = -(att + act_all) % 128
     out_mine = jnp.concatenate(
         [
             first[:keep],
@@ -903,6 +1230,7 @@
             second,
             slots[2, :own],
             slots[3, :own],
+            jnp.zeros((spare, width), bf16),
         ],
         axis=0,
     )
@@ -941,70 +1269,55 @@
     up = proj[:, 3 * att + act_all :]
     sig = jax.nn.sigmoid(gate)
     silu = gate * sig
-    joined = jnp.concatenate([att_low, (silu * up).astype(bf16)], axis=1)
-    d_act = d_joined[:, att:].astype(f32)
+    joined = jnp.concatenate(
+        [att_low, (silu * up).astype(bf16), jnp.zeros((all_tokens, spare), bf16)], axis=1
+    )
+    d_act = d_joined[:, att : att + act_all].astype(f32)
     d_gate = d_act * up * sig * (1.0 + gate * (1.0 - sig))
     d_up = d_act * silu
     d_proj = jnp.concatenate(
         [d_query, d_key, d_value, d_gate.astype(bf16), d_up.astype(bf16)], axis=1
     )
 
+    blocks = lambda v: v.reshape(2, n_seq // 2, rows * own_tokens, width)
     branch = jnp.dot(joined, out_mine, preferred_element_type=f32).astype(bf16)
-    def to_owner(v):
-        v = jnp.swapaxes(v.reshape(2, n_seq // 2, rows * own_tokens, width), 0, 1)
-        v = lax.psum_scatter(v.reshape(all_tokens, width), "seq", scatter_dimension=0, tiled=True)
-        return v.reshape(rows, own_tokens, width)
-
-    branch = to_owner(branch)
-    output = (tokens.astype(f32) + branch.astype(f32)).astype(bf16)
-
+    d_hidden = lax.dot_general(
+        d_proj, in_low, (((1,), (1,)), ((), ())), preferred_element_type=f32
+    ).astype(bf16)
     out_part = lax.dot_general(
         joined, g_full, (((0,), (0,)), ((), ())), preferred_element_type=f32
     ).astype(bf16)
-    a0 = out_part[:att]
-    a1, a2, a3 = (
-        out_part[att : att + act[0]],
-        out_part[att + act[0] : att + act[0] + own],
-        out_part[att + act[0] + own :],
-    )
-    fill = lambda v: jnp.pad(v, ((0, slot - v.shape[0]), (0, 0)))
-    out_slots = jnp.stack(
-        [fill(a0), jnp.concatenate([a1, a0[keep:]], axis=0), fill(a2), fill(a3)]
-    )
-    out_sum = lax.psum_scatter(out_slots, "dp", scatter_dimension=0, tiled=True)[0]
-    send_at = jnp.where(p == 0, keep, jnp.where(last, act[0], act[0] - late))
-    sent = lax.dynamic_slice_in_dim(out_sum, send_at, late, 0)
-    from_prev = lax.ppermute(sent, "seq", [(k, (k + 1) % n_seq) for k in range(n_seq)])
+    in_part = lax.dot_general(
+        hidden, d_proj, (((0,), (0,)), ((), ())), preferred_element_type=f32
+    ).astype(bf16)
+    normed, inv_std = normalise(tokens.reshape(rows * own_tokens, width))
+    bias_part = jnp.sum(d_proj[:, : 3 * att].astype(f32), axis=0).reshape(3, att)
+    small_part = lax.dynamic_update_slice(jnp.zeros((8, width), f32), bias_part, (2, s * att))
+    starts = (0, att, att + act[0], att + act[0] + own)
+    sums, in_sum, out_sum, from_prev, small_sum = reduce_all(
+        n_dp, n_seq, late, starts, keep,
+        blocks(d_hidden), blocks(branch),
+        in_part.reshape(n_dp, n_seq, in_rows, -1), out_part, normed, small_part,
+    )
+    d_hidden, branch = sums[0], sums[1]
+
+    output = (tokens.astype(f32) + branch.reshape(tokens.shape)).astype(bf16)
+    d_normed = d_hidden * gain
+    input_grad = cotangent.astype(f32) + (
+        inv_std
+        * (
+            d_normed
+            - jnp.mean(d_normed, axis=-1, keepdims=True)
+            - normed * jnp.mean(d_normed * normed, axis=-1, keepdims=True)
+        )
+    ).reshape(tokens.shape)
+    small_grad = lax.dynamic_slice(small_sum, (0, (p * n_seq + s) * in_rows), (8, in_rows))[:5].T
+
     count = jnp.where(p == 0, lead * s, jnp.where(p == 1, late - lead * s, 0))
     out_grad = lax.dynamic_slice_in_dim(
         jnp.concatenate([from_prev, out_sum[:own]], axis=0), late - count, own, 0
     ).astype(f32)
-
-    in_part = lax.dot_general(
-        hidden, d_proj, (((0,), (0,)), ((), ())), preferred_element_type=f32
-    ).astype(bf16)
-    in_sum = lax.psum_scatter(in_part, "dp", scatter_dimension=0, tiled=True)
-    in_sum = lax.all_to_all(in_sum.reshape(n_seq, in_rows, -1), "seq", 0, 0, tiled=True)
     in_grad = unshare(in_sum).astype(f32)
-
-    d_hidden = lax.dot_general(
-        d_proj, in_low, (((1,), (1,)), ((), ())), preferred_element_type=f32
-    ).astype(bf16)
-    d_hidden = to_owner(d_hidden).astype(f32)
-    normed, inv_std = normalise(tokens)
-    d_normed = d_hidden * gain
-    input_grad = cotangent.astype(f32) + inv_std * (
-        d_normed
-        - jnp.mean(d_normed, axis=-1, keepdims=True)
-        - normed * jnp.mean(d_normed * normed, axis=-1, keepdims=True)
-    )
-
-    gain_grad = jnp.sum(d_hidden * normed, axis=(0, 1))
-    shift_grad = jnp.sum(d_hidden, axis=(0, 1))
-    bias_part = jnp.sum(d_proj[:, : 3 * att].astype(f32), axis=0).reshape(3, att).T
-    bias_grad = lax.dynamic_update_slice_in_dim(jnp.zeros((width, 3), f32), bias_part, s * att, 0)
-    small_term = jnp.concatenate([gain_grad[:, None], shift_grad[:, None], bias_grad], axis=1)
-    small_grad = lax.psum_scatter(small_term, ("dp", "seq"), scatter_dimension=0, tiled=True)
 
     in_new = adam_update(
         in_weight, in_first, in_second, in_average, in_grad, matrix_rate, weight_decay

time: 825 us -> 557 us (0.68)
  waiting for transfers between devices: 455 us -> 0 us
  Pallas kernels: 165 us -> 365 us
  between operations: 14.9 us -> 1.39 us
  local copies, waits for them, and re-layouts: 57.9 us -> 69.5 us
    reduce_scatter x4 -> x0, waiting for transfers between devices: 320 us -> none  [the longest x2 189 us: to_owner(): lax.psum_scatter(v.reshape(all_tokens, width), 'seq', scatter_dimension=0...]
    pallas_call x0 -> x1, Pallas kernels: none -> 200 us  [reduce_all(): pl.pallas_call(functools.partial(reduce_kernel, n_seq=n_seq, late=late, s...]
    unnamed x6 -> x0, waiting for transfers between devices: 125 us -> none
    ppermute x1 -> x0, waiting for transfers between devices: 9.66 us -> none  [split_heads(): lax.ppermute(sent, 'seq', [(k, (k + 1) % n_seq) for k in range(n_seq)])]
    unnamed x90 -> x79, local copies, waits for them, and re-layouts: 13.8 us -> 16.9 us
  transfers between devices with their start and end apart: 7 -> 0, of which waited for: 6 -> 0; matrix products, arithmetic and copies ran while one was open for 7% -> 0% of each run, Pallas kernels for 0% -> 0%
where the time goes in v3:
time: 557 us; the launch traced here: 553 us
  Pallas kernels  365 us (66%)
  local copies, waits for them, and re-layouts  69.5 us (12%)
  matrix products  63.9 us (11%)
  other arithmetic  54.1 us (10%)
    pallas_call x1, Pallas kernels, reduce_all(): pl.pallas_call(functools.partial(reduce_kernel, n_seq=n_seq, late=late, s...  200 us
    pallas_call x1, Pallas kernels, gather_all(): pl.pallas_call(functools.partial(gather_kernel, n_seq=n_seq, late=late),...  151 us
    add x3, other arithmetic, adam_update(): average_new = average_keep * average + (1.0 - average_keep) * weight_new  21.7 us
    unnamed x79, local copies, waits for them, and re-layouts  16.9 us
    dot_general x1, matrix products, split_heads(): lax.dot_general(hidden, d_proj, (((0,), (0,)), ((), ())), preferred_eleme...  15.8 us
    pallas_call x1, Pallas kernels, attention_both(): pl.pallas_call(functools.partial(attention_kernel, head_size=head_size, h...  14.3 us
    dot_general x1, matrix products, split_heads(): lax.dot_general(d_proj, in_low, (((1,), (1,)), ((), ())), preferred_eleme...  13.8 us
    dot_general x1, matrix products, split_heads(): proj = jnp.dot(hidden, in_low, preferred_element_type=f32)  13.7 us

profile of v3, /device:TPU:11, one launch (start us, length us, event | category | flops | bytes accessed | tf_op | source)
XLA Modules:
  0.0 553.5 jit_solution(11692192192873982497)
XLA Ops:
  0.6 2.5 convert_element_type.91
  3.2 0.8 copy_bitcast_fusion
  4.0 0.8 fusion.31
  4.8 1.4 reshape.391
  6.2 0.8 copy.35
  7.4 0.8 copy.36
  8.6 0.8 copy.38
  9.8 0.8 copy.39
  10.5 0.7 copy.65
  11.2 0.8 fusion.32
  12.0 1.5 reshape.390
  13.6 1.4 reshape.393
  15.0 4.9 concatenate.40
  20.0 1.1 convert_element_type.92.o_ref
  21.7 150.7 %gather_all.1 = (bf16[2,4,2,64,2048]{4,3,2,1,0:T(8,128)(2,1)}, bf16[2,4,2,64,2048]{4,3,2,1,0:T(8,128)(2,1)}, bf16[4,8,64,2176]{3,2,1,0:T(8,128)(2,1)}, bf16[4,368,2048]{2,1,0:T(8,128)(2,1)}, f32[4,8,16,128]{3,2,1,0:T(8,128)}) custom-call(bf16[2,64,2048]{2,1,0:T(8,128)(2,1)} %x_ref.1, bf16[2,64,2048]{2,1,0:T(8,128)(2,1)} %g_ref.1, ...), custom_call_target="tpu_custom_call" | custom-call | tf_op jit(solution)/shard_map/gather_all/pallas_call | solution.py:811
  172.4 3.3 fusion.28
  175.6 0.8 fusion.19
  176.5 2.0 fusion.18
  178.4 2.3 bitcast_dynamic-update-slice_fusion.2
  180.8 2.2 bitcast_dynamic-update-slice_fusion.1
  183.0 2.2 bitcast_dynamic-update-slice_fusion
  185.3 0.7 broadcast_dynamic-update-slice_fusion
  186.0 8.0 %convolution_convert_fusion.4 = bf16[1024,1024]{1,0:T(8,128)(2,1)} fusion(bf16[1024,2048]{1,0:T(8,128)(2,1)S(1)} %bitcast.136, bf16[1024,2048]{1,0:T(8,128)(2,1)} %broadcast_dynamic-update-slice_fusion), kind=kOutput, calls=%fused_computation.31 | convolution fusion | flops 4296015872 | bytes 10485760 | tf_op jit(solution)/shard_map/dot_general | solution.py:1246
  194.7 1.3 multiply_reduce_fusion
  196.9 3.3 add_convert_fusion
  200.2 13.7 %fusion.35 = f32[1024,2176]{1,0:T(8,128)} fusion(bf16[1024,2048]{1,0:T(8,128)(2,1)S(1)} %bitcast.108, bf16[2048,2176]{1,0:T(8,128)(2,1)} %bitcast.134), kind=kOutput, calls=%fused_computation.109 | convolution fusion | flops 9126805504 | bytes 22020096 | tf_op jit(solution)/shard_map/dot_general | solution.py:1245
  214.5 3.0 multiply_cosine_fusion
  217.7 2.6 concatenate.45
  220.3 2.8 concatenate.46
  223.1 1.9 concatenate.44
  225.0 2.5 pad_maximum_fusion.rope_ref
  227.5 0.7 copy.42
  228.2 1.3 broadcast_in_dim_reshape.8.seg_q_ref
  229.5 0.9 slice.179
  231.1 0.7 broadcast_in_dim_reshape.7.seg_k_ref
  231.8 14.3 %attention.1 = (bf16[2,4,2,64,256]{4,3,2,1,0:T(8,128)(2,1)}, bf16[2,4,2,64,256]{4,3,2,1,0:T(8,128)(2,1)}, bf16[2,4,2,64,256]{4,3,2,1,0:T(8,128)(2,1)}, bf16[2,4,2,64,256]{4,3,2,1,0:T(8,128)(2,1)}) custom-call(f32[2,4,2,64,2176]{4,3,2,1,0:T(8,128)} %bitcast.102, f32[2,4,2,64,2176]{4,3,2,1,0:T(8,128)} %bitcast.103, f32[2,4,2,64,2176]{4,3,2,1,0:T(8,128)} %bitcast.104, ...), custom_call_target="tpu_custom_call" | custom-call | flops 3221225472 | bytes 5242880 | tf_op jit(solution)/shard_map/attention/pallas_call | solution.py:460
  246.1 1.6 convert_reduce_fusion.1
  248.4 1.4 dynamic_update_slice.3.small_ref
  249.9 5.4 fusion.8
  255.3 1.1 copy-done.8
  257.0 6.4 %convolution_convert_fusion.2.out_ref = bf16[1024,2048]{1,0:T(8,128)(2,1)} fusion(bf16[1024,2048]{1,0:T(8,128)(2,1)S(1)} %bitcast.137, bf16[1024,704]{1,0:T(8,128)(2,1)S(1)} %get-tuple-element.60, bf16[1024,256]{1,0:T(8,128)(2,1)S(1)} %bitcast.138, bf16[1024]{0:T(1024)(128)(2,1)S(1)} %pad.21.clone), kind=kOutput, calls=%fused_computation.16 | convolution fusion | flops 4303355904 | bytes 10356736 | tf_op jit(solution)/shard_map/dot_general | solution.py:1287
  263.4 1.4 rsqrt.25
  265.4 4.6 fusion.3
  270.0 8.1 %concatenate.47 = bf16[1024,2176]{1,0:T(8,128)(2,1)} concatenate(bf16[1024,256]{1,0:T(8,128)(2,1)} %bitcast.117, bf16[1024,256]{1,0:T(8,128)(2,1)} %bitcast.119, bf16[1024,256]{1,0:T(8,128)(2,1)} %bitcast.121, bf16[1024,704]{1,0:T(8,128)(2,1)} %get-tuple-element.59, bf16[1024,704]{1,0:T(8,128)(2,1)S(1)} %get-tuple-element.58), dimensions={1} | concatenate | bytes 8912896 | tf_op jit(solution)/shard_map/concatenate | solution.py:1278
  278.2 15.8 %convolution_convert_fusion = bf16[2048,2176]{1,0:T(8,128)(2,1)} fusion(bf16[1024,2048]{1,0:T(8,128)(2,1)} %fusion.3, bf16[1024,2176]{1,0:T(8,128)(2,1)} %concatenate.47), kind=kOutput, calls=%fused_computation | convolution fusion | flops 9131261952 | bytes 17563648 | tf_op jit(solution)/shard_map/dot_general | solution.py:1290
  294.0 6.1 %convolution_convert_fusion.3 = bf16[1024,2048]{1,0:T(8,128)(2,1)} fusion(bf16[1024,2048]{1,0:T(8,128)(2,1)S(1)} %copy-done.14, bf16[1024,704]{1,0:T(8,128)(2,1)S(1)} %copy-done.9, bf16[1024,256]{1,0:T(8,128)(2,1)S(1)} %bitcast.139, bf16[1024]{0:T(1024)(128)(2,1)S(1)} %copy-done.25), kind=kOutput, calls=%fused_computation.17 | convolution fusion | flops 4303355904 | bytes 10356736 | tf_op jit(solution)/shard_map/dot_general | solution.py:1283
  300.1 13.8 %convolution_convert_fusion.1 = bf16[1024,2048]{1,0:T(8,128)(2,1)} fusion(bf16[1024,2176]{1,0:T(8,128)(2,1)S(1)} %copy-done.4, bf16[2048,2176]{1,0:T(8,128)(2,1)} %bitcast.135), kind=kOutput, calls=%fused_computation.15 | convolution fusion | flops 9128902656 | bytes 17563648 | tf_op jit(solution)/shard_map/dot_general | solution.py:1284
  314.6 1.3 fusion.13.normed_ref
  315.8 199.7 %reduce_all.1 = (f32[2,128,2048]{2,1,0:T(8,128)}, bf16[8,64,2176]{2,1,0:T(8,128)(2,1)}, bf16[384,2048]{1,0:T(8,128)(2,1)}, bf16[128,2048]{1,0:T(8,128)(2,1)}, f32[8,2048]{1,0:T(8,128)}) custom-call(bf16[2,4,128,2048]{3,2,1,0:T(8,128)(2,1)} %bitcast.110, bf16[2,4,128,2048]{3,2,1,0:T(8,128)(2,1)} %bitcast.109, bf16[4,8,64,2176]{3,2,1,0:T(8,128)(2,1)} %bitcast.105, ...), custom_call_target="tpu_custom_call" | custom-call | tf_op jit(solution)/shard_map/reduce_all/pallas_call | solution.py:1123
  515.6 1.3 slice.166
  516.9 7.1 %multiply_add_fusion.1 = (f32[240,2048]{1,0:T(8,128)}, f32[240,2048]{1,0:T(8,128)}, f32[240,2048]{1,0:T(8,128)}, f32[240,2048]{1,0:T(8,128)}) fusion(f32[240,2048]{1,0:T(8,128)} %param.27, f32[240,2048]{1,0:T(8,128)S(1)} %copy-done.2, f32[240,2048]{1,0:T(8,128)} %param.25, f32[240,2048]{1,0:T(8,128)} %param.26, s32[]{:T(128)S(6)} %select_n.48, ...), kind=kLoop, calls=%fused_computation.29 | loop fusion | flops 11304960 | bytes 17235972 | tf_op jit(solution)/shard_map/add | solution.py:81
  524.1 0.7 constant_dynamic-update-slice_fusion.8
  524.8 0.7 constant_dynamic-update-slice_fusion.7
  525.6 0.7 constant_dynamic-update-slice_fusion.6
  526.9 0.7 constant_dynamic-update-slice_fusion.5
  527.6 1.8 fusion.29
  529.8 0.7 constant_dynamic-update-slice_fusion.4
  531.0 0.7 constant_dynamic-update-slice_fusion.3
  532.1 0.7 constant_dynamic-update-slice_fusion.2
  533.3 0.7 constant_dynamic-update-slice_fusion.1
  534.4 0.7 constant_dynamic-update-slice_fusion
  535.2 14.0 %multiply_add_fusion = (f32[64,17408]{1,0:T(8,128)}, f32[64,17408]{1,0:T(8,128)}, f32[64,17408]{1,0:T(8,128)}, f32[64,17408]{1,0:T(8,128)}) fusion(f32[64,17408]{1,0:T(8,128)} %param.23, f32[64,17408]{1,0:T(8,128)} %param.20, f32[64,17408]{1,0:T(8,128)} %param.21, f32[64,17408]{1,0:T(8,128)} %param.22, bf16[64,17408]{1,0:T(8,128)(2,1)} %constant_dynamic-update-slice_fusion), kind=kLoop, calls=%fused_computation.11 | loop fusion | flops 22282240 | bytes 37879808 | tf_op jit(solution)/shard_map/add | solution.py:81
  550.2 1.7 multiply_add_fusion.2
  551.9 0.8 constant_dynamic-slice_fusion
  (126 shorter events, 12.2 us)
Async XLA Ops:
  12.0 7.9 %copy-start.2 = (f32[240,2048]{1,0:T(8,128)S(1)}, f32[240,2048]{1,0:T(8,128)}, u32[]{:S(2)}) copy-start(f32[240,2048]{1,0:T(8,128)} %param.24) | copy-start | bytes 5898244
  13.6 7.4 %copy-start.15 = (f32[64,5]{0,1:T(8,128)S(1)}, f32[64,5]{0,1:T(8,128)}, u32[]{:S(2)}) copy-start(f32[64,5]{0,1:T(8,128)} %param.28) | copy-start | bytes 3844
  13.6 7.5 %copy-start.26 = (s32[2,64]{1,0:T(2,128)S(1)}, s32[2,64]{1,0:T(2,128)}, u32[]{:S(2)}) copy-start(s32[2,64]{1,0:T(2,128)} %param.19) | copy-start | bytes 1540
  13.6 7.4 %copy-start.27 = (s32[2,64]{1,0:T(2,128)S(1)}, s32[2,64]{1,0:T(2,128)}, u32[]{:S(2)}) copy-start(s32[2,64]{1,0:T(2,128)} %param.18) | copy-start | bytes 1540
  178.4 7.6 %copy-start.28 = (bf16[2,4,2,64,2048]{4,3,2,1,0:T(8,128)(2,1)S(1)}, bf16[2,4,2,64,2048]{4,3,2,1,0:T(8,128)(2,1)}, u32[]{:S(2)}) copy-start(bf16[2,4,2,64,2048]{4,3,2,1,0:T(8,128)(2,1)} %get-tuple-element.31) | copy-start | bytes 12582916
  186.0 8.1 %copy-start = (bf16[2,4,2,64,2048]{4,3,2,1,0:T(8,128)(2,1)S(1)}, bf16[2,4,2,64,2048]{4,3,2,1,0:T(8,128)(2,1)}, u32[]{:S(2)}) copy-start(bf16[2,4,2,64,2048]{4,3,2,1,0:T(8,128)(2,1)} %get-tuple-element.28) | copy-start | bytes 12582916
  194.0 1.9 copy-start.11
  196.0 4.2 copy-start.13
  196.0 0.7 copy-start.10
  196.9 3.3 copy-start.12
  223.0 2.0 copy-start.6
  249.8 7.1 %copy-start.29 = (bf16[2,4,2,64,2048]{4,3,2,1,0:T(8,128)(2,1)S(1)}, bf16[2,4,2,64,2048]{4,3,2,1,0:T(8,128)(2,1)}, u32[]{:S(2)}) copy-start(bf16[2,4,2,64,2048]{4,3,2,1,0:T(8,128)(2,1)} %get-tuple-element.31) | copy-start | bytes 12582916
  249.9 7.1 %copy-start.30 = (bf16[2,4,2,64,256]{4,3,2,1,0:T(8,128)(2,1)S(1)}, bf16[2,4,2,64,256]{4,3,2,1,0:T(8,128)(2,1)}, u32[]{:S(2)}) copy-start(bf16[2,4,2,64,256]{4,3,2,1,0:T(8,128)(2,1)} %get-tuple-element.36) | copy-start | bytes 1572868
  255.3 1.1 copy-start.8
  256.4 0.6 copy-start.24
  278.1 15.9 %copy-start.9 = (bf16[1024,704]{1,0:T(8,128)(2,1)S(1)}, bf16[1024,704]{1,0:T(8,128)(2,1)}, u32[]{:S(2)}) copy-start(bf16[1024,704]{1,0:T(8,128)(2,1)} %copy-done.8) | copy-start | bytes 4325380
  278.1 15.9 %copy-start.14 = (bf16[1024,2048]{1,0:T(8,128)(2,1)S(1)}, bf16[1024,2048]{1,0:T(8,128)(2,1)}, u32[]{:S(2)}) copy-start(bf16[1024,2048]{1,0:T(8,128)(2,1)} %broadcast_dynamic-update-slice_fusion) | copy-start | bytes 12582916
  278.1 15.9 %copy-start.25 = (bf16[1024]{0:T(1024)(128)(2,1)S(1)}, bf16[1024]{0:T(1024)(128)(2,1)}, u32[]{:S(2)}) copy-start(bf16[1024]{0:T(1024)(128)(2,1)} %copy-done.24) | copy-start | bytes 6148
  278.1 15.9 %copy-start.31 = (bf16[2,4,2,64,256]{4,3,2,1,0:T(8,128)(2,1)S(1)}, bf16[2,4,2,64,256]{4,3,2,1,0:T(8,128)(2,1)}, u32[]{:S(2)}) copy-start(bf16[2,4,2,64,256]{4,3,2,1,0:T(8,128)(2,1)} %get-tuple-element.36) | copy-start | bytes 1572868
  294.0 6.1 %copy-start.4 = (bf16[1024,2176]{1,0:T(8,128)(2,1)S(1)}, bf16[1024,2176]{1,0:T(8,128)(2,1)}, u32[]{:S(2)}) copy-start(bf16[1024,2176]{1,0:T(8,128)(2,1)} %concatenate.47) | copy-start | bytes 13369348
  300.1 13.8 %copy-start.1 = (bf16[2,64,2048]{2,1,0:T(8,128)(2,1)S(1)}, bf16[2,64,2048]{2,1,0:T(8,128)(2,1)}, u32[]{:S(2)}) copy-start(bf16[2,64,2048]{2,1,0:T(8,128)(2,1)} %x_ref.1) | copy-start | bytes 1572868
  314.5 201.1 %copy-start.20 = (f32[128]{0:T(128)}, f32[128]{0:T(128)S(1)}, u32[]{:S(2)}) copy-start(f32[128]{0:T(128)S(1)} %rsqrt.27) | copy-start | bytes 1540
  314.6 201.0 %copy-start.22 = (f32[128]{0:T(128)}, f32[128]{0:T(128)S(1)}, u32[]{:S(2)}) copy-start(f32[128]{0:T(128)S(1)} %div.86) | copy-start | bytes 1540
  516.9 7.1 %copy-start.5 = (bf16[8,64,2176]{2,1,0:T(8,128)(2,1)S(1)}, bf16[8,64,2176]{2,1,0:T(8,128)(2,1)}, u32[]{:S(2)}) copy-start(bf16[8,64,2176]{2,1,0:T(8,128)(2,1)} %get-tuple-element.38) | copy-start | bytes 6684676
  535.2 14.0 %copy-start.3 = (f32[2,128,2048]{2,1,0:T(8,128)S(1)}, f32[2,128,2048]{2,1,0:T(8,128)}, u32[]{:S(2)}) copy-start(f32[2,128,2048]{2,1,0:T(8,128)} %get-tuple-element.37) | copy-start | bytes 6291460
  535.2 14.0 %copy-start.21 = (f32[128]{0:T(128)S(1)}, f32[128]{0:T(128)}, u32[]{:S(2)}) copy-start(f32[128]{0:T(128)} %copy-done.20) | copy-start | bytes 1540
  535.2 14.0 %copy-start.23 = (f32[128]{0:T(128)S(1)}, f32[128]{0:T(128)}, u32[]{:S(2)}) copy-start(f32[128]{0:T(128)} %copy-done.22) | copy-start | bytes 1540
  549.2 1.0 copy-start.7
  549.7 3.0 copy-start.16
  549.7 3.0 copy-start.17
  549.7 3.0 copy-start.18
  549.7 3.0 copy-start.19

commit v4 on v3

--- a/solution.py
+++ b/solution.py
@@ -380,24 +380,52 @@
     )
 
 
-def attention_kernel(
-    q_ref, k_ref, v_ref, bq_ref, bk_ref, bv_ref, da_ref, rope_ref, seg_q_ref, seg_k_ref,
-    o_ref, dq_ref, dk_ref, dv_ref, *, head_size, half_rot,
+def middle_kernel(
+    q_ref, k_ref, v_ref, bq_ref, bk_ref, bv_ref, da_ref, act_ref, d_act_ref, rope_ref,
+    seg_q_ref, seg_k_ref,
+    joined_ref, d_proj_ref, bias_ref,
+    *, head_size, half_rot, att_rows, act_rows,
 ):
+    row, pair = pl.program_id(0), pl.program_id(1)
+    lanes = 2 * head_size
+    half = act_ref.shape[3]
+    bf16, f32 = jnp.bfloat16, jnp.float32
+
+    def feed_forward(step):
+        x, z = lax.rem(step, 2), step // 2
+        raw = act_ref[x, z, 0]
+        gate = raw[:, 3 * att_rows : 3 * att_rows + act_rows]
+        up = raw[:, 3 * att_rows + act_rows :]
+        d_act = d_act_ref[x, z, 0][:, att_rows : att_rows + act_rows].astype(f32)
+        sig = 1.0 / (1.0 + jnp.exp(-gate))
+        silu = gate * sig
+        spare = joined_ref.shape[4] - att_rows - act_rows
+        rows = pl.ds(pl.multiple_of(pair * half, half), half)
+        joined_ref[x, z, row, rows, att_rows:] = jnp.concatenate(
+            [silu * up, jnp.zeros((half, spare), f32)], axis=1
+        ).astype(bf16)
+        d_gate = d_act * up * sig * (1.0 + gate * (1.0 - sig))
+        d_proj_ref[x, z, row, rows, 3 * att_rows :] = jnp.concatenate(
+            [d_gate, d_act * silu], axis=1
+        ).astype(bf16)
+
+    loop(0, act_ref.shape[0] * act_ref.shape[1], feed_forward)
+
     def whole(v):
         across, depth = v.shape[:2]
         parts = [v[x, z].reshape(v.shape[-2:]) for z in range(depth) for x in range(across)]
         return jnp.concatenate(parts, axis=0)
 
-    def store(ref, v):
+    def store(ref, first, v):
         across, depth, _, some, _ = ref.shape
+        columns = pl.ds(pl.multiple_of(first + pair * lanes, lanes), lanes)
         for z in range(depth):
             for x in range(across):
                 at = (z * across + x) * some
-                ref[x, z, 0] = v[at : at + some].astype(ref.dtype)
-
-    cos, sin_low, sin_high = (whole(rope_ref[i]) for i in range(3))
-    tokens, lanes = cos.shape
+                ref[x, z, row, :, columns] = v[at : at + some]
+
+    cos, sin_low, sin_high = (rope_ref[0, i].T for i in range(3))
+    tokens = cos.shape[0]
     scale = head_size ** (-0.5)
 
     def turn(v, way):
@@ -407,10 +435,10 @@
             + way * pltpu.roll(v, half_rot, 1) * sin_high
         )
 
-    query = (turn(whole(q_ref[...]) + bq_ref[...], 1.0)).astype(jnp.bfloat16) * scale
-    query = query.astype(jnp.bfloat16)
-    key = turn(whole(k_ref[...]) + bk_ref[...], 1.0).astype(jnp.bfloat16)
-    value = (whole(v_ref[...]) + bv_ref[...]).astype(jnp.bfloat16)
+    query = (turn(whole(q_ref[...]) + bq_ref[...], 1.0)).astype(bf16) * scale
+    query = query.astype(bf16)
+    key = turn(whole(k_ref[...]) + bk_ref[...], 1.0).astype(bf16)
+    value = (whole(v_ref[...]) + bv_ref[...]).astype(bf16)
     d_att = whole(da_ref[...])
     place_q = lax.broadcasted_iota(jnp.int32, (tokens, tokens), 0)
     place_k = lax.broadcasted_iota(jnp.int32, (tokens, tokens), 1)
@@ -418,11 +446,11 @@
     lane = lax.broadcasted_iota(jnp.int32, (tokens, lanes), 1)
     nt = (((1,), (1,)), ((), ()))
     tn = (((0,), (0,)), ((), ()))
-    dot = functools.partial(lax.dot_general, preferred_element_type=jnp.float32)
-    att = jnp.zeros((tokens, lanes), jnp.float32)
-    d_query = jnp.zeros((tokens, lanes), jnp.float32)
-    d_key = jnp.zeros((tokens, lanes), jnp.float32)
-    d_value = jnp.zeros((tokens, lanes), jnp.float32)
+    dot = functools.partial(lax.dot_general, preferred_element_type=f32)
+    att = jnp.zeros((tokens, lanes), f32)
+    d_query = jnp.zeros((tokens, lanes), f32)
+    d_key = jnp.zeros((tokens, lanes), f32)
+    d_value = jnp.zeros((tokens, lanes), f32)
     for head in range(lanes // head_size):
         mine = (lane >= head * head_size) & (lane < (head + 1) * head_size)
         q_h = jnp.where(mine, query, jnp.zeros_like(query))
@@ -431,57 +459,76 @@
         top = jnp.max(scores, axis=1, keepdims=True)
         weights = jnp.exp(scores - top)
         probs = weights * (1.0 / jnp.sum(weights, axis=1, keepdims=True))
-        probs_low = probs.astype(jnp.bfloat16)
+        probs_low = probs.astype(bf16)
         att_h = jnp.where(mine, dot(probs_low, value, (((1,), (0,)), ((), ()))), 0.0)
-        out_dot = jnp.sum(att_h * d_att.astype(jnp.float32), axis=1, keepdims=True)
+        out_dot = jnp.sum(att_h * d_att.astype(f32), axis=1, keepdims=True)
         d_prob = dot(da_h, value, nt)
-        d_score = (probs * (d_prob - out_dot)).astype(jnp.bfloat16)
+        d_score = (probs * (d_prob - out_dot)).astype(bf16)
         att = att + att_h
         d_query = d_query + jnp.where(mine, dot(d_score, key, (((1,), (0,)), ((), ()))), 0.0)
         d_key = d_key + dot(d_score, q_h, tn)
         d_value = d_value + dot(probs_low, da_h, tn)
-    store(o_ref, att)
-    store(dq_ref, turn(d_query * scale, -1.0))
-    store(dk_ref, turn(d_key, -1.0))
-    store(dv_ref, d_value)
-
-
-def attention_both(proj, bias, d_joined, rope, seg, n_seq, att_rows, head_size):
+    store(joined_ref, 0, att.astype(bf16))
+    grads = (turn(d_query * scale, -1.0), turn(d_key, -1.0), d_value)
+    columns = pl.ds(pl.multiple_of(pair * lanes, lanes), lanes)
+    for i, grad in enumerate(grads):
+        grad = grad.astype(bf16)
+        store(d_proj_ref, i * att_rows, grad)
+        total = jnp.sum(grad.astype(f32), axis=0, keepdims=True)
+
+        @pl.when(row == 0)
+        def _():
+            bias_ref[i : i + 1, columns] = total
+
+        @pl.when(row > 0)
+        def _():
+            bias_ref[i : i + 1, columns] = bias_ref[i : i + 1, columns] + total
+
+
+def middle(proj, bias, d_joined, rope, seg, n_seq, att_rows, act_rows, head_size):
     rows, tokens = seg.shape
     lanes = 2 * head_size
     pairs = att_rows // lanes
+    bf16, f32 = jnp.bfloat16, jnp.float32
     order = (2, n_seq // 2, rows, tokens // n_seq)
     wide = lambda v: v.reshape(order + v.shape[-1:])
     shape = (2, n_seq // 2, 1, tokens // n_seq, lanes)
     block = lambda first: pl.BlockSpec(shape, lambda r, h: (0, 0, r, 0, first + h))
     row = lambda first: pl.BlockSpec((1, lanes), lambda r, h: (0, first + h))
-    out = jax.ShapeDtypeStruct(order + (att_rows,), jnp.bfloat16)
+    half = lambda v: pl.BlockSpec(
+        (2, n_seq // 2, 1, tokens // n_seq // pairs, v.shape[-1]), lambda r, h: (0, 0, r, h, 0)
+    )
+    all_of = lambda v: pl.BlockSpec(v.shape, lambda r, h: (0,) * len(v.shape))
+    outs = [
+        jax.ShapeDtypeStruct(order + (d_joined.shape[-1],), bf16),
+        jax.ShapeDtypeStruct(order + (proj.shape[-1],), bf16),
+        jax.ShapeDtypeStruct((8, att_rows), f32),
+    ]
     proj, d_joined = wide(proj), wide(d_joined)
-    results = pl.pallas_call(
-        functools.partial(attention_kernel, head_size=head_size, half_rot=ROT // 2),
+    joined, d_proj, bias_sums = pl.pallas_call(
+        functools.partial(
+            middle_kernel,
+            head_size=head_size, half_rot=ROT // 2, att_rows=att_rows, act_rows=act_rows,
+        ),
         grid=(rows, pairs),
         in_specs=[
             block(0), block(pairs), block(2 * pairs),
             row(0), row(pairs), row(2 * pairs),
-            block(0),
-            pl.BlockSpec((3,) + shape, lambda r, h: (0, 0, 0, r, 0, 0)),
+            block(0), half(proj), half(d_joined),
+            pl.BlockSpec((1, 3, lanes, tokens), lambda r, h: (r, 0, 0, 0)),
             pl.BlockSpec((1, tokens, 1), lambda r, h: (r, 0, 0)),
             pl.BlockSpec((1, 1, tokens), lambda r, h: (r, 0, 0)),
         ],
-        out_specs=[block(0)] * 4,
-        out_shape=[out] * 4,
+        out_specs=[all_of(v) for v in outs],
+        out_shape=outs,
         compiler_params=pltpu.CompilerParams(vmem_limit_bytes=56 * 2**20),
-        cost_estimate=pl.CostEstimate(
-            flops=rows * pairs * 2 * 12 * tokens * tokens * lanes,
-            bytes_accessed=rows * tokens * att_rows * 20,
-            transcendentals=rows * pairs * 2 * tokens * tokens,
-        ),
-        name="attention",
+        name="middle",
     )(
-        proj, proj, proj, bias, bias, bias, d_joined,
-        rope.reshape((3,) + order + (lanes,)), seg[:, :, None], seg[:, None, :],
-    )
-    return [v.reshape(rows * tokens, att_rows) for v in results]
+        proj, proj, proj, bias, bias, bias, d_joined, proj, d_joined,
+        rope, seg[:, :, None], seg[:, None, :],
+    )
+    flat = lambda v: v.reshape(rows * tokens, v.shape[-1])
+    return flat(joined), flat(d_proj), bias_sums
 
 MESH_ID = pl.DeviceIdType.MESH
 
@@ -556,7 +603,11 @@
             self.own, self.full.at[self.at.x, self.at.z], self.sems.at[5, 0]
         )
 
-    def begin(self):
+    def begin_across(self):
+        self.across(self.at.z, self.own).start()
+        self.local().start()
+
+    def begin_along(self):
         at = self.at
 
         @pl.when(at.z < at.depth - 1)
@@ -566,9 +617,6 @@
         @pl.when(at.z > 0)
         def _():
             self.along(at.z, False, self.own).start()
-
-        self.across(at.z, self.own).start()
-        self.local().start()
 
     def step(self, hop):
         at = self.at
@@ -658,12 +706,18 @@
 
 def gather_kernel(
     x_ref, g_ref, w_ref, o_ref, tile_ref,
-    x_full, g_full, w_full, o_full, tiles,
+    x_full, g_full, w_full, o_full, tiles, hidden, out_mine, proj, d_joined,
+    x_block, hid, w_near, p_block, g_near, o_near, t_near, small,
     x_sems, g_sems, w_sems, w_fan_sems, o_sems, o_fan_sems, t_sems, t_fan_sems, local_sems,
-    *, n_seq, late,
+    x_in_sems, hid_sems, w_in_sems, p_sems, g_in_sems, o_in_sems,
+    *, n_seq, late, lead,
 ):
     at = Place(n_seq)
-    own = o_ref.shape[0]
+    depth = at.depth
+    bf16, f32 = jnp.bfloat16, jnp.float32
+    own, width = o_ref.shape
+    att = own + lead
+    first_act = own - lead
     body, extra = pl.ds(0, own), pl.ds(own, late)
     x_go = Spread(at, x_ref, x_full, x_sems)
     g_go = Spread(at, g_ref, g_full, g_sems)
@@ -697,53 +751,182 @@
         head, o_full.at[at.p, extra], o_sems.at[0], o_sems.at[1], (at.p, at.seq(-1))
     )
 
+    def place(i):
+        return lax.rem(at.x + i // depth, 2), lax.rem(at.z + i, depth)
+
+    def block_in(i):
+        col, deep = place(i)
+        return pltpu.make_async_copy(x_full.at[col, deep], x_block, x_in_sems.at[0])
+
+    def hid_out(i):
+        col, deep = place(i)
+        return pltpu.make_async_copy(hid.at[col, deep], hidden.at[col, deep], hid_sems.at[i])
+
+    def norm_block(i):
+        col, deep = place(i)
+
+        @pl.when(i >= depth)
+        def _():
+            here = x_full.at[1 - at.x, deep]
+            remote(here, here, x_sems.at[2, deep], x_sems.at[4, deep], at.to_x).wait_recv()
+
+        block_in(i).start()
+        block_in(i).wait()
+        some = 32
+
+        def rows(k):
+            part = pl.ds(pl.multiple_of(lax.rem(k, 2) * some, some), some)
+            v = x_block[k // 2, part, :].astype(f32)
+            centered = v - jnp.mean(v, axis=-1, keepdims=True)
+            inv_std = lax.rsqrt(jnp.mean(centered * centered, axis=-1, keepdims=True) + norm_eps)
+            done = centered * inv_std * small[0:1, :] + small[1:2, :]
+            hid[col, deep, pl.ds(pl.multiple_of(k * some, some), some), :] = done.astype(bf16)
+
+        loop(0, hid.shape[2] // some, rows)
+        hid_out(i).start()
+
+    def w_in(p, k):
+        return pltpu.make_async_copy(w_full.at[p], w_near.at[p], w_in_sems.at[k])
+
+    def g_in():
+        return pltpu.make_async_copy(g_full, g_near, g_in_sems.at[0])
+
+    def o_in(k):
+        last = at.s == n_seq - 1
+        lead_at = pl.multiple_of(lead * at.s, 16)
+        late_at = pl.multiple_of(late - lead * at.s, 16)
+        src, dst, count = [
+            (o_full.at[0, pl.ds(lead_at, att - late)], 0, att - late),
+            (o_full.at[0, pl.ds(lead_at + (att - late), late)], att - late, late),
+            (o_full.at[1, pl.ds(late_at, first_act)], att, first_act),
+            (o_full.at[2, body], att + first_act, own),
+            (o_full.at[3, body], att + first_act + own, own),
+            (o_full.at[1, extra], att - late, late),
+        ][k]
+        return pltpu.make_async_copy(src, o_near.at[pl.ds(dst, count)], o_in_sems.at[k])
+
+    step_rows = p_block.shape[1]
+    steps = hid.shape[0] * depth * hid.shape[2] // step_rows
+    per_block = step_rows // hid.shape[2]
+
+    def p_out(k):
+        return pltpu.make_async_copy(
+            p_block.at[lax.rem(k, 2)],
+            proj.at[pl.ds(pl.multiple_of(k * step_rows, step_rows), step_rows)],
+            p_sems.at[lax.rem(k, 2)],
+        )
+
+    def project(k):
+        @pl.when(k >= 2)
+        def _():
+            p_out(k - 2).wait()
+
+        rows = per_block * k
+        left = hid[rows // depth, pl.ds(lax.rem(rows, depth), per_block)]
+        left = left.reshape(step_rows, width)
+        columns = p_block.shape[2]
+        for n in range(0, columns, 512):
+            some = min(512, columns - n)
+            right = w_near[:, :, :, n : n + some].reshape(width, some)
+            p_block[lax.rem(k, 2), :, n : n + some] = jnp.dot(
+                left, right, preferred_element_type=f32
+            )
+        p_out(k).start()
+
+    def join_back(k):
+        rows = per_block * k
+        left = g_near[rows // depth, pl.ds(lax.rem(rows, depth), per_block)]
+        left = left.reshape(step_rows, width)
+        d_joined[pl.ds(pl.multiple_of(k * step_rows, step_rows), step_rows), :] = (
+            lax.dot_general(
+                left, o_near[...], (((1,), (1,)), ((), ())), preferred_element_type=f32
+            ).astype(bf16)
+        )
+
     at.meet()
-    x_go.begin()
+    x_go.begin_along()
+    x_go.begin_across()
+    g_go.begin_across()
     loop(1, n_seq, lambda hop: t_send(hop).start())
     t_local.start()
     w_fan.y(at.s, w_ref.at[at.s]).start()
-    loop(1, n_seq, lambda hop: w_send(hop).start())
     w_fan.core(at.s, w_ref.at[at.s]).start()
     w_local.start()
+    o_fan.y(0, o_ref).start()
     o_fan.core(0, o_ref).start()
     o_local.start()
-    for hop in range(1, at.depth):
+    w_send(1).start()
+    w_send(n_seq - 1).start()
+    for hop in range(1, depth):
         x_go.step(hop)
-    g_go.begin()
-    t_local.wait()
-    loop(1, n_seq, lambda hop: t_recv(hop).wait_recv())
-    t_fan.y(0).start()
-    t_fan.core(0).start()
+        if hop == 1:
+            t_local.wait()
+            loop(1, n_seq, lambda k: t_recv(k).wait_recv())
+            t_fan.y(0).start()
+            t_fan.core(0).start()
+        if hop == 2:
+            t_fan.from_y(0).wait_recv()
+            t_fan.pass_on(0).start()
+        w_send(hop + 1).start()
+        if hop + 1 < n_seq - hop - 1:
+            w_send(n_seq - hop - 1).start()
+    g_go.begin_along()
 
     @pl.when(at.y == 0)
     def _():
         o_send.start()
+
+    t_fan.from_core(0).wait_recv()
+    t_fan.from_diagonal(0).wait_recv()
+    t_load = pltpu.make_async_copy(tiles, t_near, local_sems.at[3])
+    t_load.start()
+    t_load.wait()
+    for p in range(t_near.shape[0]):
+        for pair in range(n_seq // 2):
+            two = t_near[p, 2 * pair, 0:8] + t_near[p, 2 * pair + 1, 0:8]
+            lanes = two.shape[1]
+            first = (p * (n_seq // 2) + pair) * lanes
+            small[:, first : first + lanes] = two
+    o_near[att + first_act + 2 * own :, :] = jnp.zeros_like(o_near[att + first_act + 2 * own :, :])
+    x_go.local().wait()
 
     def w_step(hop):
         src = at.seq(-hop)
         w_recv(hop).wait_recv()
         w_fan.y(src).start()
         w_fan.core(src).start()
+        norm_block(hop - 1)
 
     loop(1, n_seq, w_step)
-    t_fan.from_y(0).wait_recv()
-    t_fan.pass_on(0).start()
-    o_fan.y(0, o_ref).start()
-    for hop in range(1, at.depth):
-        g_go.step(hop)
-
-    @pl.when(at.y == 0)
-    def _():
-        o_send.wait_recv()
-        o_fan.y(1).start()
-        o_fan.core(1).start()
-
+    norm_block(n_seq - 1)
+    w_local.wait()
+    w_in(at.p, 0).start()
     def w_pass(hop):
         src = at.seq(-hop)
         w_fan.from_y(src).wait_recv()
         w_fan.pass_on(src).start()
 
-    loop(0, n_seq, w_pass)
+    for hop in range(1, depth):
+        g_go.step(hop)
+        loop((hop - 1) * 3, min(hop * 3, n_seq), w_pass)
+        if hop == 1:
+
+            @pl.when(at.y == 0)
+            def _():
+                o_send.wait_recv()
+                o_fan.y(1).start()
+                o_fan.core(1).start()
+
+    loop((depth - 1) * 3, n_seq, w_pass)
+    w_in(at.p_y, 1).start()
+
+    def w_last(k):
+        w_fan.from_core(k).wait_recv()
+        w_fan.from_diagonal(k).wait_recv()
+
+    loop(0, n_seq, w_last)
+    w_in(at.p_c, 2).start()
+    w_in(at.p_d, 3).start()
     o_fan.from_y(0).wait_recv()
     o_fan.pass_on(0).start()
 
@@ -752,12 +935,11 @@
         o_fan.from_y(1).wait_recv()
         o_fan.pass_on(1).start()
 
-    x_go.arrive()
-    g_go.arrive()
-    w_local.wait()
+    for k, p in enumerate((at.p, at.p_y, at.p_c, at.p_d)):
+        w_in(p, k).wait()
+    loop(0, steps, project)
+
     o_local.wait()
-    t_fan.from_core(0).wait_recv()
-    t_fan.from_diagonal(0).wait_recv()
     o_fan.from_core(0).wait_recv()
     o_fan.from_diagonal(0).wait_recv()
 
@@ -769,17 +951,40 @@
     def _():
         o_fan.from_diagonal(1).wait_recv()
 
-    def w_last(k):
-        w_fan.from_core(k).wait_recv()
-        w_fan.from_diagonal(k).wait_recv()
+    for k in (0, 2, 3, 4):
+        o_in(k).start()
+
+    @pl.when(at.s < n_seq - 1)
+    def _():
+        o_in(1).start()
+        o_in(1).wait()
+
+    @pl.when(at.s == n_seq - 1)
+    def _():
+        o_in(5).start()
+        o_in(5).wait()
+
+    for k in (0, 2, 3, 4):
+        o_in(k).wait()
+    o_out = pltpu.make_async_copy(o_near, out_mine, o_in_sems.at[6])
+    o_out.start()
+    g_go.arrive()
+    g_in().start()
+    g_in().wait()
+    loop(0, steps, join_back)
+
+    o_out.wait()
+    loop(steps - 2, steps, lambda k: p_out(k).wait())
+    loop(0, n_seq, lambda i: hid_out(i).wait())
+    x_go.sent()
+    g_go.sent()
+
+    def w_sent(k):
         w_fan.y(k).wait_send()
         w_fan.core(k).wait_send()
         w_fan.pass_on(k).wait_send()
 
-    loop(0, n_seq, w_last)
-
-    x_go.sent()
-    g_go.sent()
+    loop(0, n_seq, w_sent)
 
     def seq_sent(hop):
         w_send(hop).wait_send()
@@ -802,28 +1007,48 @@
         o_fan.pass_on(1).wait_send()
 
 
-def gather_all(n_dp, n_seq, late, x, g, w, o, tile):
+def gather_all(n_dp, n_seq, late, lead, x, g, w, o, tile):
     depth = n_seq // 2
     own, width = o.shape
-    rest = pl.BlockSpec(memory_space=pl.ANY)
+    block = x.shape[0] * x.shape[1]
+    tokens = n_seq * block
+    columns = w.shape[2]
+    mine = -(-(own * n_dp) // 128) * 128
+    bf16, f32 = jnp.bfloat16, jnp.float32
+    rest, near = pl.BlockSpec(memory_space=pl.ANY), pl.BlockSpec(memory_space=pltpu.VMEM)
     dma = pltpu.SemaphoreType.DMA
     like = lambda lead, ref: jax.ShapeDtypeStruct(lead + ref.shape, ref.dtype)
     return pl.pallas_call(
-        functools.partial(gather_kernel, n_seq=n_seq, late=late),
+        functools.partial(gather_kernel, n_seq=n_seq, late=late, lead=lead),
         in_specs=[rest] * 5,
-        out_specs=[rest] * 5,
+        out_specs=[rest] * 8 + [near],
         out_shape=[
             like((2, depth), x),
             like((2, depth), g),
             jax.ShapeDtypeStruct((n_dp,) + w.shape, w.dtype),
             jax.ShapeDtypeStruct((n_dp, own + late, width), o.dtype),
             like((n_dp, n_seq), tile),
+            jax.ShapeDtypeStruct((2, depth, block, width), bf16),
+            jax.ShapeDtypeStruct((mine, width), bf16),
+            jax.ShapeDtypeStruct((tokens, columns), f32),
+            jax.ShapeDtypeStruct((tokens, mine), bf16),
         ],
         scratch_shapes=[
+            pltpu.VMEM(x.shape, bf16),
+            pltpu.VMEM((2, depth, block, width), bf16),
+            pltpu.VMEM((n_dp,) + w.shape, bf16),
+            pltpu.VMEM((2, 2 * block, columns), f32),
+            pltpu.VMEM((2, depth) + g.shape, bf16),
+            pltpu.VMEM((mine, width), bf16),
+            pltpu.VMEM((n_dp, n_seq) + tile.shape, f32),
+            pltpu.VMEM((8, width), f32),
             dma((6, depth)), dma((6, depth)), dma((2, n_seq)), dma((6, n_seq)),
-            dma((2,)), dma((6, 2)), dma((2, n_seq)), dma((6, 1)), dma((3,)),
+            dma((2,)), dma((6, 2)), dma((2, n_seq)), dma((6, 1)), dma((4,)),
+            dma((1,)), dma((n_seq,)), dma((4,)), dma((2,)), dma((1,)), dma((7,)),
         ],
-        compiler_params=pltpu.CompilerParams(collective_id=0, has_side_effects=True),
+        compiler_params=pltpu.CompilerParams(
+            collective_id=0, has_side_effects=True, vmem_limit_bytes=56 * 2**20
+        ),
         name="gather_all",
     )(x, g, w, o, tile)
 
@@ -1203,37 +1428,23 @@
         ],
         axis=0,
     )
-    x_full, g_full, in_low, slots, tiles = gather_all(
-        n_dp, n_seq, late, tokens, cotangent, share(in_weight.astype(bf16)), out_low, tile
-    )
-    x_full, g_full = x_full.reshape(all_tokens, width), g_full.reshape(all_tokens, width)
+    odd = jnp.concatenate([jnp.zeros_like(tile[:8, :in_rows]), tile[:8, :in_rows]], axis=1)
+    tile = jnp.concatenate([jnp.where(s % 2 == 1, odd, tile[:8]), tile[8:]], axis=0)
+    _, g_full, in_low, _, tiles, hidden, out_mine, proj, d_joined = gather_all(
+        n_dp, n_seq, late, lead, tokens, cotangent, share(in_weight.astype(bf16)), out_low, tile
+    )
+    g_full, hidden = g_full.reshape(all_tokens, width), hidden.reshape(all_tokens, width)
     in_low = in_low.reshape(n_dp * n_seq * in_rows, 3 * att + 2 * act_all)
 
-    small_low = jnp.transpose(tiles[:, :, :5, :in_rows], (2, 0, 1, 3)).reshape(5, width)
-    gain, shift = small_low[0], small_low[1]
+    pairs = tiles[:, :, :5].reshape(n_dp, n_seq // 2, 2, 5, 2 * in_rows).sum(axis=2)
+    small_low = jnp.transpose(pairs, (2, 0, 1, 3)).reshape(5, width)
+    gain = small_low[0]
     bias = lax.dynamic_slice_in_dim(small_low[2:5], s * att, att, 1).reshape(1, 3 * att)
     docs = lax.dynamic_index_in_dim(tiles, p, 0, keepdims=False)[:, 8:, :own_tokens]
     seg_full = jnp.transpose(docs[:, :rows], (1, 0, 2)).reshape(rows, row_tokens)
-    pos_full = docs[:, rows : 2 * rows].reshape(n_seq // 2, 2, rows, own_tokens)
-    pos_full = jnp.transpose(pos_full, (1, 0, 2, 3))
-
-    late_at = late - lead * s
-    first = lax.dynamic_slice_in_dim(slots[0], lead * s, att, 0)
-    second = lax.dynamic_slice_in_dim(slots[1], late_at, act[0], 0)
+    pos_full = jnp.transpose(docs[:, rows : 2 * rows], (1, 0, 2)).reshape(rows, row_tokens)
     last = s == n_seq - 1
     keep = att - late
-    spare = -(att + act_all) % 128
-    out_mine = jnp.concatenate(
-        [
-            first[:keep],
-            jnp.where(last, slots[1, own:], first[keep:]),
-            second,
-            slots[2, :own],
-            slots[3, :own],
-            jnp.zeros((spare, width), bf16),
-        ],
-        axis=0,
-    )
 
     def normalise(v):
         v = v.astype(f32)
@@ -1241,42 +1452,22 @@
         inv_std = lax.rsqrt(jnp.mean(centered * centered, axis=-1, keepdims=True) + norm_eps)
         return centered * inv_std, inv_std
 
-    hidden = (normalise(x_full)[0] * gain + shift).astype(bf16)
-    proj = jnp.dot(hidden, in_low, preferred_element_type=f32)
-    d_joined = lax.dot_general(
-        g_full, out_mine, (((1,), (1,)), ((), ())), preferred_element_type=f32
-    ).astype(bf16)
-
     half_rot = ROT // 2
     inv_freq = rope_base ** (-2.0 * jnp.arange(half_rot, dtype=f32) / ROT)
-    angles = pos_full.reshape(all_tokens, 1).astype(f32) * inv_freq
+    angles = pos_full[:, None, :] * inv_freq[:, None]
     cos, sin = jnp.cos(angles), jnp.sin(angles)
-    rest = head_size - ROT
-    one, zero = jnp.ones((all_tokens, rest), f32), jnp.zeros((all_tokens, rest), f32)
-    none = jnp.zeros_like(sin)
+    one, zero = jnp.ones((rows, head_size - ROT, row_tokens), f32), jnp.zeros_like(cos)
+    rest = 0.0 * one
     rope = jnp.stack(
         [
             jnp.concatenate([cos, cos, one] * 2, axis=1),
-            jnp.concatenate([-sin, none, zero] * 2, axis=1),
-            jnp.concatenate([none, sin, zero] * 2, axis=1),
-        ]
-    )
-    att_low, d_query, d_key, d_value = attention_both(
-        proj, bias, d_joined, rope, seg_full, n_seq, att, head_size
-    )
-
-    gate = proj[:, 3 * att : 3 * att + act_all]
-    up = proj[:, 3 * att + act_all :]
-    sig = jax.nn.sigmoid(gate)
-    silu = gate * sig
-    joined = jnp.concatenate(
-        [att_low, (silu * up).astype(bf16), jnp.zeros((all_tokens, spare), bf16)], axis=1
-    )
-    d_act = d_joined[:, att : att + act_all].astype(f32)
-    d_gate = d_act * up * sig * (1.0 + gate * (1.0 - sig))
-    d_up = d_act * silu
-    d_proj = jnp.concatenate(
-        [d_query, d_key, d_value, d_gate.astype(bf16), d_up.astype(bf16)], axis=1
+            jnp.concatenate([-sin, zero, rest] * 2, axis=1),
+            jnp.concatenate([zero, sin, rest] * 2, axis=1),
+        ],
+        axis=1,
+    )
+    joined, d_proj, bias_part = middle(
+        proj, bias, d_joined, rope, seg_full, n_seq, att, act_all, head_size
     )
 
     blocks = lambda v: v.reshape(2, n_seq // 2, rows * own_tokens, width)
@@ -1291,8 +1482,7 @@
         hidden, d_proj, (((0,), (0,)), ((), ())), preferred_element_type=f32
     ).astype(bf16)
     normed, inv_std = normalise(tokens.reshape(rows * own_tokens, width))
-    bias_part = jnp.sum(d_proj[:, : 3 * att].astype(f32), axis=0).reshape(3, att)
-    small_part = lax.dynamic_update_slice(jnp.zeros((8, width), f32), bias_part, (2, s * att))
+    small_part = lax.dynamic_update_slice(jnp.zeros((8, width), f32), bias_part[:3], (2, s * att))
     starts = (0, att, att + act[0], att + act[0] + own)
     sums, in_sum, out_sum, from_prev, small_sum = reduce_all(
         n_dp, n_seq, late, starts, keep,

time: 557 us -> 471 us (0.85)
  local copies, waits for them, and re-layouts: 69.5 us -> 31.3 us
  matrix products: 63.9 us -> 39.6 us
  other arithmetic: 54.1 us -> 33.4 us
    dot_general x2 -> x0, matrix products: 21.7 us -> none  [the longest x1 13.7 us: split_heads(): proj = jnp.dot(hidden, in_low, preferred_element_type=f32)]
    concatenate x5 -> x2, local copies, waits for them, and re-layouts: 14.2 us -> 0.03 us  [the longest x1 0.01 us: split_heads(): jnp.concatenate([zero, sin, rest] * 2, axis=1)]
    convert_element_type x3 -> x0, other arithmetic: 13.3 us -> none  [the longest x2 7.9 us: split_heads(): hidden = (normalise(x_full)[0] * gain + shift).astype(bf16)]
    unnamed x79 -> x56, local copies, waits for them, and re-layouts: 16.9 us -> 7.35 us
    pallas_call x1, Pallas kernels: 200 us -> 192 us  [reduce_all(): pl.pallas_call(functools.partial(reduce_kernel, n_seq=n_seq, late=late, s...]
where the time goes in v4:
time: 471 us; the launch traced here: 467 us
  Pallas kernels  361 us (77%)
  matrix products  39.6 us (8%)
  other arithmetic  33.4 us (7%)
  local copies, waits for them, and re-layouts  31.3 us (7%)
    pallas_call x1, Pallas kernels, reduce_all(): pl.pallas_call(functools.partial(reduce_kernel, n_seq=n_seq, late=late, s...  192 us
    pallas_call x1, Pallas kernels, gather_all(): pl.pallas_call(functools.partial(gather_kernel, n_seq=n_seq, late=late, l...  147 us
    pallas_call x1, Pallas kernels, middle(): pl.pallas_call(functools.partial(middle_kernel, head_size=head_size, half...  22.4 us
    add x3, other arithmetic, adam_update(): average_new = average_keep * average + (1.0 - average_keep) * weight_new  21.7 us
    dot_general x1, matrix products, split_heads(): lax.dot_general(hidden, d_proj, (((0,), (0,)), ((), ())), preferred_eleme...  12.5 us
    dot_general x1, matrix products, split_heads(): lax.dot_general(d_proj, in_low, (((1,), (1,)), ((), ())), preferred_eleme...  11.5 us
    dot_general x1, matrix products, split_heads(): lax.dot_general(joined, g_full, (((0,), (0,)), ((), ())), preferred_eleme...  9.56 us

profile of v4, /device:TPU:11, one launch (start us, length us, event | category | flops | bytes accessed | tf_op | source)
XLA Modules:
  0.0 466.9 jit_solution(810057715272642984)
XLA Ops:
  0.7 0.7 convert_bitcast_fusion
  1.4 0.7 add_convert_fusion.1
  2.1 0.6 select_maximum_fusion.tile_ref
  2.7 2.5 convert_element_type.54
  5.2 0.8 fusion.16
  6.0 0.8 copy_bitcast_fusion
  6.9 0.4 reshape.211
  7.4 0.4 reshape.212
  7.9 0.4 reshape.214
  8.4 0.4 reshape.215
  8.9 1.7 copy.110
  10.6 0.7 fusion.15
  11.3 1.3 reshape.210
  12.7 0.4 reshape.213
  13.2 4.9 %concatenate.27 = bf16[64,8,2176]{2,0,1:T(8,128)(2,1)} concatenate(bf16[64,8,256]{2,0,1:T(8,128)(2,1)} %bitcast.96, bf16[64,8,256]{2,0,1:T(8,128)(2,1)} %get-tuple-element.88, bf16[64,8,256]{2,0,1:T(8,128)(2,1)} %get-tuple-element.87, bf16[64,8,224]{2,0,1:T(8,128)(2,1)S(1)} %copy.79, bf16[64,8,240]{2,0,1:T(8,128)(2,1)S(1)} %copy.80, bf16[64,8,240]{2,0,1:T(8,128)(2,1)S(1)} %copy.81, ...), dimensions={2} | concatenate | bytes 4456448 | tf_op jit(solution)/shard_map/concatenate | solution.py:1410
  18.0 1.1 convert_element_type.55.o_ref
  19.1 146.6 %gather_all.1 = (bf16[2,4,2,64,2048]{4,3,2,1,0:T(8,128)(2,1)}, bf16[2,4,2,64,2048]{4,3,2,1,0:T(8,128)(2,1)}, bf16[4,8,64,2176]{3,2,1,0:T(8,128)(2,1)}, bf16[4,36...) custom-call(bf16[2,64,2048]{2,1,0:T(8,128)(2,1)} %x_ref.1, ...), custom_call_target="tpu_custom_call" | custom-call | tf_op jit(solution)/shard_map/gather_all/pallas_call | solution.py:1021
  165.7 0.8 dynamic-slice_bitcast_fusion
  166.7 0.2 constant_dynamic-update-slice_fusion.3
  166.9 0.2 constant_dynamic-update-slice_fusion.2
  167.1 0.2 constant_dynamic-update-slice_fusion.1
  167.4 0.2 constant_dynamic-update-slice_fusion
  167.6 0.2 constant_dynamic-update-slice_fusion.8
  167.9 1.3 pad_maximum_fusion.rope_ref
  169.1 1.3 broadcast_in_dim_reshape.9.seg_q_ref
  170.5 0.6 copy.106
  171.1 0.7 broadcast_in_dim_reshape.8.seg_k_ref
  171.7 22.4 %middle.1 = (bf16[2,4,2,64,1024]{4,3,2,1,0:T(8,128)(2,1)}, bf16[2,4,2,64,2176]{4,3,2,1,0:T(8,128)(2,1)}, f32[8,256]{1,0:T(8,128)}) custom-call(f32[2,4,2,64,2176]{4,3,2,1,0:T(8,128)} %bitcast.81, f32[2,4,2,64,2176]{4,3,2,1,0:T(8,128)} %bitcast.82, f32[2,4,2,64,2176]{4,3,2,1,0:T(8,128)} %bitcast.83, f32[1,768]{1,0:T(1,128)} %bitcast.111, f32[1,768]{1,0:T(1,128)} %bitcast.112, ...), custom_call_target="tpu_custom_call" | custom-call | tf_op jit(solution)/shard_map/middle/pallas_call | solution.py:508
  194.2 9.6 %bitcast_convert_fusion.out_ref = bf16[1024,2048]{1,0:T(8,128)(2,1)} fusion(bf16[2,4,2,64,1024]{4,3,2,1,0:T(8,128)(2,1)} %get-tuple-element.34, bf16[2,4,2,64,2048]{4,3,2,1,0:T(8,128)(2,1)} %get-tuple-element.37), kind=kOutput, calls=%fused_computation.1 | convolution fusion | flops 4297064448 | bytes 10485760 | tf_op jit(solution)/shard_map/dot_general | solution.py:1478
  203.8 12.5 %convolution_convert_fusion = bf16[2048,2176]{1,0:T(8,128)(2,1)} fusion(bf16[1024,2048]{1,0:T(8,128)(2,1)S(1)} %bitcast.121, bf16[1024,2176]{1,0:T(8,128)(2,1)S(1)} %bitcast.119), kind=kOutput, calls=%fused_computation | convolution fusion | flops 9131261952 | bytes 17563648 | tf_op jit(solution)/shard_map/dot_general | solution.py:1481
  216.3 6.0 %convolution_convert_fusion.2 = bf16[1024,2048]{1,0:T(8,128)(2,1)} fusion(bf16[1024,1024]{1,0:T(8,128)(2,1)S(1)} %bitcast.122, bf16[1024,2048]{1,0:T(8,128)(2,1)S(1)} %copy-done.13), kind=kOutput, calls=%fused_computation.7 | convolution fusion | flops 4297064448 | bytes 10485760 | tf_op jit(solution)/shard_map/dot_general | solution.py:1474
  222.4 11.5 %convolution_convert_fusion.1 = bf16[1024,2048]{1,0:T(8,128)(2,1)} fusion(bf16[1024,2176]{1,0:T(8,128)(2,1)S(1)} %bitcast.120, bf16[2048,2176]{1,0:T(8,128)(2,1)S(1)} %bitcast.118), kind=kOutput, calls=%fused_computation.6 | convolution fusion | flops 9128902656 | bytes 17563648 | tf_op jit(solution)/shard_map/dot_general | solution.py:1475
  233.9 0.6 dynamic_update_slice.3.small_ref
  234.5 0.2 convert_reduce_fusion
  234.7 0.3 multiply_reduce_fusion.1
  235.2 1.3 fusion.2.normed_ref
  236.5 192.1 %reduce_all.1 = (f32[2,128,2048]{2,1,0:T(8,128)}, bf16[8,64,2176]{2,1,0:T(8,128)(2,1)}, bf16[384,2048]{1,0:T(8,128)(2,1)}, bf16[128,2048]{1,0:T(8,128)(2,1)}, f32[8,2048]{1,0:T(8,128)}) custom-call(bf16[2,4,128,2048]{3,2,1,0:T(8,128)(2,1)} %bitcast.90, bf16[2,4,128,2048]{3,2,1,0:T(8,128)(2,1)} %bitcast.89, bf16[4,8,64,2176]{3,2,1,0:T(8,128)(2,1)} %bitcast.85, ...), custom_call_target="tpu_custom_call" | custom-call | tf_op jit(solution)/shard_map/reduce_all/pallas_call | solution.py:1348
  428.5 1.3 slice.122
  429.8 7.1 %multiply_add_fusion.1 = (f32[240,2048]{1,0:T(8,128)}, f32[240,2048]{1,0:T(8,128)}, f32[240,2048]{1,0:T(8,128)}, f32[240,2048]{1,0:T(8,128)}) fusion(f32[240,2048]{1,0:T(8,128)} %param.27, f32[240,2048]{1,0:T(8,128)S(1)} %copy-done.1, f32[240,2048]{1,0:T(8,128)} %param.25, f32[240,2048]{1,0:T(8,128)} %param.26, s32[]{:T(128)S(6)} %select_n.43, ...), kind=kLoop, calls=%fused_computation.10 | loop fusion | flops 11304960 | bytes 17235972 | tf_op jit(solution)/shard_map/add | solution.py:81
  437.0 0.7 constant_dynamic-update-slice_fusion.20
  437.8 0.7 constant_dynamic-update-slice_fusion.19
  438.5 0.7 constant_dynamic-update-slice_fusion.18
  439.4 0.2 copy.93
  439.6 0.3 reshape.230
  439.8 0.7 constant_dynamic-update-slice_fusion.17
  440.6 1.8 fusion.12
  442.3 0.2 copy.94
  442.5 0.3 reshape.231
  442.8 0.7 constant_dynamic-update-slice_fusion.16
  443.5 0.1 copy.95
  443.6 0.3 reshape.232
  443.9 0.7 constant_dynamic-update-slice_fusion.15
  444.8 0.3 reshape.233
  445.1 0.7 constant_dynamic-update-slice_fusion.14
  445.9 0.3 reshape.234
  446.2 0.7 constant_dynamic-update-slice_fusion.13
  447.1 0.3 reshape.235
  447.4 0.7 constant_dynamic-update-slice_fusion.12
  448.1 14.0 %multiply_add_fusion = (f32[64,17408]{1,0:T(8,128)}, f32[64,17408]{1,0:T(8,128)}, f32[64,17408]{1,0:T(8,128)}, f32[64,17408]{1,0:T(8,128)}) fusion(f32[64,17408]{1,0:T(8,128)} %param.23, f32[64,17408]{1,0:T(8,128)} %param.20, f32[64,17408]{1,0:T(8,128)} %param.21, f32[64,17408]{1,0:T(8,128)} %param.22, bf16[64,17408]{1,0:T(8,128)(2,1)} %constant_dynamic-update-slice_fusion.12), kind=kLoop, calls=%fused_computation.4 | loop fusion | flops 22282240 | bytes 37879808 | tf_op jit(solution)/shard_map/add | solution.py:81
  462.1 0.4 fusion.3
  462.8 0.7 copy-done.4
  463.5 1.7 multiply_add_fusion.2
  465.2 0.8 constant_dynamic-slice_fusion
  466.0 0.6 multiply_add_fusion.3
  (86 shorter events, 2.0 us)
Async XLA Ops:
  13.2 4.9 %copy-start.1 = (f32[240,2048]{1,0:T(8,128)S(1)}, f32[240,2048]{1,0:T(8,128)}, u32[]{:S(2)}) copy-start(f32[240,2048]{1,0:T(8,128)} %param.24) | copy-start | bytes 5898244
  167.6 2.8 copy-start.6
  194.1 9.6 %copy-start.12 = (bf16[2,4,2,64,2176]{4,3,2,1,0:T(8,128)(2,1)S(1)}, bf16[2,4,2,64,2176]{4,3,2,1,0:T(8,128)(2,1)}, u32[]{:S(2)}) copy-start(bf16[2,4,2,64,2176]{4,3,2,1,0:T(8,128)(2,1)} %get-tuple-element.32) | copy-start | bytes 13369348
  194.2 9.6 %copy-start.14 = (bf16[2,4,128,2048]{3,2,1,0:T(8,128)(2,1)S(1)}, bf16[2,4,128,2048]{3,2,1,0:T(8,128)(2,1)}, u32[]{:S(2)}) copy-start(bf16[2,4,128,2048]{3,2,1,0:T(8,128)(2,1)} %get-tuple-element.36) | copy-start | bytes 12582916
  194.2 28.2 %slice-start = ((s8[8912896]{0:T(1024)(128)(4,1)}), s8[4194304]{0:T(1024)(128)(4,1)S(1)}, s32[]{:S(2)}) async-start(s8[8912896]{0:T(1024)(128)(4,1)} %bitcast.116), calls=%async_computation | async-start | bytes 8388608
  203.7 12.6 %copy-start.13 = (bf16[1024,2048]{1,0:T(8,128)(2,1)S(1)}, bf16[1024,2048]{1,0:T(8,128)(2,1)}, u32[]{:S(2)}) copy-start(bf16[1024,2048]{1,0:T(8,128)(2,1)} %get-tuple-element.35) | copy-start | bytes 12582916
  203.7 12.6 %copy-start.15 = (bf16[2,4,2,64,1024]{4,3,2,1,0:T(8,128)(2,1)S(1)}, bf16[2,4,2,64,1024]{4,3,2,1,0:T(8,128)(2,1)}, u32[]{:S(2)}) copy-start(bf16[2,4,2,64,1024]{4,3,2,1,0:T(8,128)(2,1)} %get-tuple-element.34) | copy-start | bytes 6291460
  203.8 18.6 %slice-start.1 = ((s8[8912896]{0:T(1024)(128)(4,1)}), s8[4194304]{0:T(1024)(128)(4,1)S(1)}, s32[]{:S(2)}) async-start(s8[8912896]{0:T(1024)(128)(4,1)} %bitcast.116), calls=%async_computation.1 | async-start | bytes 8388608
  203.8 18.6 %slice-start.2 = ((s8[8912896]{0:T(1024)(128)(4,1)}), s8[524288]{0:T(1024)(128)(4,1)S(1)}, s32[]{:S(2)}) async-start(s8[8912896]{0:T(1024)(128)(4,1)} %bitcast.116), calls=%async_computation.2 | async-start | bytes 1048576
  222.3 11.5 %copy-start.11 = (f32[8,256]{1,0:T(8,128)S(1)}, f32[8,256]{1,0:T(8,128)}, u32[]{:S(2)}) copy-start(f32[8,256]{1,0:T(8,128)} %get-tuple-element.38) | copy-start | bytes 24580
  222.4 12.2 %copy-start = (bf16[2,64,2048]{2,1,0:T(8,128)(2,1)S(1)}, bf16[2,64,2048]{2,1,0:T(8,128)(2,1)}, u32[]{:S(2)}) copy-start(bf16[2,64,2048]{2,1,0:T(8,128)(2,1)} %x_ref.1) | copy-start | bytes 1572868
  234.5 1.9 copy-start.5
  429.8 7.1 %copy-start.3 = (bf16[8,64,2176]{2,1,0:T(8,128)(2,1)S(1)}, bf16[8,64,2176]{2,1,0:T(8,128)(2,1)}, u32[]{:S(2)}) copy-start(bf16[8,64,2176]{2,1,0:T(8,128)(2,1)} %get-tuple-element.40) | copy-start | bytes 6684676
  448.1 14.0 %copy-start.2 = (f32[2,128,2048]{2,1,0:T(8,128)S(1)}, f32[2,128,2048]{2,1,0:T(8,128)}, u32[]{:S(2)}) copy-start(f32[2,128,2048]{2,1,0:T(8,128)} %get-tuple-element.39) | copy-start | bytes 6291460
  462.5 1.0 copy-start.4
  463.5 2.5 copy-start.7
  463.5 2.5 copy-start.8
  463.5 2.5 copy-start.9
  463.5 2.5 copy-start.10

commit v5 on v4

--- a/solution.py
+++ b/solution.py
@@ -384,11 +384,12 @@
     q_ref, k_ref, v_ref, bq_ref, bk_ref, bv_ref, da_ref, act_ref, d_act_ref, rope_ref,
     seg_q_ref, seg_k_ref,
     joined_ref, d_proj_ref, bias_ref,
-    *, head_size, half_rot, att_rows, act_rows,
+    *, head_size, half_rot, att_rows, act,
 ):
     row, pair = pl.program_id(0), pl.program_id(1)
     lanes = 2 * head_size
     half = act_ref.shape[3]
+    act_rows = sum(act)
     bf16, f32 = jnp.bfloat16, jnp.float32
 
     def feed_forward(step):
@@ -396,14 +397,19 @@
         raw = act_ref[x, z, 0]
         gate = raw[:, 3 * att_rows : 3 * att_rows + act_rows]
         up = raw[:, 3 * att_rows + act_rows :]
-        d_act = d_act_ref[x, z, 0][:, att_rows : att_rows + act_rows].astype(f32)
+        joint = d_act_ref[x, z, 0]
+        d_act = jnp.concatenate(
+            [joint[:, (i + 1) * att_rows :][:, :some] for i, some in enumerate(act)], axis=1
+        ).astype(f32)
         sig = 1.0 / (1.0 + jnp.exp(-gate))
         silu = gate * sig
-        spare = joined_ref.shape[4] - att_rows - act_rows
         rows = pl.ds(pl.multiple_of(pair * half, half), half)
-        joined_ref[x, z, row, rows, att_rows:] = jnp.concatenate(
-            [silu * up, jnp.zeros((half, spare), f32)], axis=1
-        ).astype(bf16)
+        active, parts, first = silu * up, [], 0
+        for some in act:
+            parts.append(active[:, first : first + some])
+            parts.append(jnp.zeros((half, att_rows - some), f32))
+            first += some
+        joined_ref[x, z, row, rows, att_rows:] = jnp.concatenate(parts, axis=1).astype(bf16)
         d_gate = d_act * up * sig * (1.0 + gate * (1.0 - sig))
         d_proj_ref[x, z, row, rows, 3 * att_rows :] = jnp.concatenate(
             [d_gate, d_act * silu], axis=1
@@ -485,7 +491,7 @@
             bias_ref[i : i + 1, columns] = bias_ref[i : i + 1, columns] + total
 
 
-def middle(proj, bias, d_joined, rope, seg, n_seq, att_rows, act_rows, head_size):
+def middle(proj, bias, d_joined, rope, seg, n_seq, att_rows, act, head_size):
     rows, tokens = seg.shape
     lanes = 2 * head_size
     pairs = att_rows // lanes
@@ -508,7 +514,7 @@
     joined, d_proj, bias_sums = pl.pallas_call(
         functools.partial(
             middle_kernel,
-            head_size=head_size, half_rot=ROT // 2, att_rows=att_rows, act_rows=act_rows,
+            head_size=head_size, half_rot=ROT // 2, att_rows=att_rows, act=act,
         ),
         grid=(rows, pairs),
         in_specs=[
@@ -799,8 +805,8 @@
             (o_full.at[0, pl.ds(lead_at, att - late)], 0, att - late),
             (o_full.at[0, pl.ds(lead_at + (att - late), late)], att - late, late),
             (o_full.at[1, pl.ds(late_at, first_act)], att, first_act),
-            (o_full.at[2, body], att + first_act, own),
-            (o_full.at[3, body], att + first_act + own, own),
+            (o_full.at[2, body], 2 * att, own),
+            (o_full.at[3, body], 3 * att, own),
             (o_full.at[1, extra], att - late, late),
         ][k]
         return pltpu.make_async_copy(src, o_near.at[pl.ds(dst, count)], o_in_sems.at[k])
@@ -887,7 +893,8 @@
             lanes = two.shape[1]
             first = (p * (n_seq // 2) + pair) * lanes
             small[:, first : first + lanes] = two
-    o_near[att + first_act + 2 * own :, :] = jnp.zeros_like(o_near[att + first_act + 2 * own :, :])
+    for k, some in enumerate((first_act, own, own)):
+        o_near[(k + 1) * att + some : (k + 2) * att, :] = jnp.zeros((att - some, width), bf16)
     x_go.local().wait()
 
     def w_step(hop):
@@ -1013,7 +1020,7 @@
     block = x.shape[0] * x.shape[1]
     tokens = n_seq * block
     columns = w.shape[2]
-    mine = -(-(own * n_dp) // 128) * 128
+    mine = n_dp * (own + lead)
     bf16, f32 = jnp.bfloat16, jnp.float32
     rest, near = pl.BlockSpec(memory_space=pl.ANY), pl.BlockSpec(memory_space=pltpu.VMEM)
     dma = pltpu.SemaphoreType.DMA
@@ -1066,12 +1073,15 @@
 
 
 def reduce_kernel(
-    d_ref, b_ref, in_ref, out_ref, normed_ref, small_ref,
+    d_ref, b_ref, in_ref, out_ref, d_proj_ref, joined_ref, hidden_ref, g_ref, w_ref, o_ref,
+    normed_ref, small_ref,
     sums, in_sum, out_sum, out_prev, small_sum,
     own_parts, x_got, z_got, in_own, in_core, in_y, out_own, out_core, out_y,
     small_own, small_core, small_y, small_seq,
+    d_near, j_near, h_near, g_near, w_near, o_near,
     load_sems, x_sems, z_sems, in_core_sems, in_y_sems, in_sems, out_sems, small_sems, local_sem,
-    *, n_seq, late, starts, keep,
+    w_sems, o_sems,
+    *, n_seq, late, first_act, keep, plan,
 ):
     at = Place(n_seq)
     depth = at.depth
@@ -1080,63 +1090,129 @@
     body, extra = pl.ds(0, main), pl.ds(main, late)
     y, c, z, x, s = at.y, at.c, at.z, at.x, at.s
 
-    def out_start(y_to, c_to):
-        one = jnp.where(y_to == 0, starts[1], starts[3])
-        zero = jnp.where(y_to == 0, starts[0], starts[2])
-        return pl.multiple_of(jnp.where(c_to == 0, zero, one), 16)
-
     loads = [
-        pltpu.make_async_copy(parts[kind].at[x], own_parts.at[kind], load_sems.at[kind])
-        for kind in range(2)
+        pltpu.make_async_copy(d_proj_ref, d_near, load_sems.at[0]),
+        pltpu.make_async_copy(joined_ref, j_near, load_sems.at[1]),
+        pltpu.make_async_copy(g_ref, g_near, load_sems.at[2]),
     ]
+    feats = h_near.shape[4]
     for y_to in range(2):
-        p_to = 2 * y_to + c
-        loads.append(pltpu.make_async_copy(in_ref.at[p_to], in_own.at[y_to], load_sems.at[2 + y_to]))
+        first = pl.multiple_of((2 * y_to + c) * feats, feats)
         loads.append(
             pltpu.make_async_copy(
-                out_ref.at[pl.ds(out_start(y_to, c), main)],
-                out_own.at[y_to, body],
-                load_sems.at[4 + y_to],
+                hidden_ref.at[:, :, :, pl.ds(first, feats)], h_near.at[y_to], load_sems.at[3 + y_to]
             )
         )
-    loads.append(
-        pltpu.make_async_copy(
-            out_ref.at[pl.ds(keep, late)], out_own.at[0, extra], load_sems.at[6]
-        )
-    )
+    dot = functools.partial(lax.dot_general, preferred_element_type=jnp.float32)
+    low = jnp.bfloat16
+    block_rows, width = own_parts.shape[2:]
+    flat = lambda v: v.reshape(-1, v.shape[-1])
+
+    def w_load(i):
+        some = w_near.shape[1]
+        return pltpu.make_async_copy(
+            w_ref.at[pl.ds(pl.multiple_of(i * some, some), some)],
+            w_near.at[lax.rem(i, 2)], w_sems.at[lax.rem(i, 2)],
+        )
+
+    def o_load(i):
+        some = o_near.shape[2]
+        return pltpu.make_async_copy(
+            o_ref.at[:, pl.ds(pl.multiple_of(i * some, some), some)],
+            o_near.at[lax.rem(i, 2)], o_sems.at[lax.rem(i, 2)],
+        )
+
+    def streamed(kind, load, count, some, product):
+        load(0).start()
+
+        def one(i):
+            @pl.when(i + 1 < count)
+            def _():
+                load(i + 1).start()
+
+            load(i).wait()
+            done = product(lax.rem(i, 2)).astype(low)
+            columns = pl.ds(pl.multiple_of(i * some, some), some)
+            own_parts[kind, :, :, columns] = done.reshape(depth, block_rows, some)
+
+        loop(0, count, one)
+
+    def work(i):
+        if i == 0:
+            some = w_near.shape[1]
+            left = flat(d_near[x])
+            streamed(
+                0, w_load, width // some, some,
+                lambda k: dot(left, w_near[k], (((1,), (1,)), ((), ()))),
+            )
+        elif i == 1:
+            some = o_near.shape[2]
+            left = flat(j_near[x])
+            streamed(
+                1, o_load, width // some, some,
+                lambda k: dot(left, o_near[k], (((1,), (0,)), ((), ()))),
+            )
+        elif i < 4:
+            y_to = 1 - y if i == 2 else y
+            left = flat(h_near[y_to])
+            right = flat(d_near[...])
+            total = right.shape[1]
+            for first in range(0, total, 512):
+                some = min(512, total - first)
+                done = dot(left, right[:, first : first + some], (((0,), (0,)), ((), ())))
+                in_own[y_to, :, :, first : first + some] = done.astype(low).reshape(
+                    n_seq, -1, some
+                )
+        else:
+            right = flat(g_near[...])
+            for y_to in range(2):
+                columns = pl.ds(pl.multiple_of((2 * y_to + c) * main, main), main)
+                out_own[y_to, body] = dot(
+                    flat(j_near[:, :, :, columns]), right, (((0,), (0,)), ((), ()))
+                ).astype(low)
+            out_own[0, extra] = dot(
+                flat(j_near[:, :, :, keep : keep + late]), right, (((0,), (0,)), ((), ()))
+            ).astype(low)
 
     def in_to_core(y_to, k):
         return remote(
-            in_ref.at[2 * y_to + 1 - c, k], in_core.at[y_to, k],
+            in_ref.at[y_to, k], in_core.at[y_to, k],
             in_core_sems.at[0, y_to, k], in_core_sems.at[1, y_to, k], at.to_c,
         )
 
     def out_to_core(y_to):
         return remote(
-            out_ref.at[pl.ds(out_start(y_to, 1 - c), main)], out_core.at[y_to, body],
+            out_ref.at[pl.ds(pl.multiple_of(y_to * main, main), main)], out_core.at[y_to, body],
             out_sems.at[0, y_to], out_sems.at[1, y_to], at.to_c,
         )
 
     extra_to_core = remote(
-        out_ref.at[pl.ds(keep, late)], out_core.at[0, extra],
+        out_ref.at[pl.ds(2 * main, late)], out_core.at[0, extra],
         out_sems.at[0, 2], out_sems.at[1, 2], at.to_c,
     )
 
     def to_across(kind, k):
         return remote(
-            parts[kind].at[1 - x, k], x_got.at[kind, k],
+            parts[kind].at[k], x_got.at[kind, k],
             x_sems.at[0, kind, k], x_sems.at[1, kind, k], at.to_x,
         )
 
-    def to_depth(kind, k):
+    def to_up(kind, k):
         return remote(
-            x_got.at[kind, k], z_got.at[kind, z],
-            z_sems.at[0, kind, k], z_sems.at[1, kind, z], (at.p, 2 * k + x),
-        )
-
-    def from_depth(kind, k):
-        here = z_got.at[kind, k]
-        return remote(here, here, z_sems.at[0, kind, k], z_sems.at[1, kind, k], (at.p, 2 * k + x))
+            x_got.at[kind, k], z_got.at[kind, k],
+            z_sems.at[0, kind, k], z_sems.at[1, kind, k], at.to_up,
+        )
+
+    def to_down(kind, k):
+        slot = jnp.where(k == z - 1, depth, k)
+        return remote(
+            x_got.at[kind, k], z_got.at[kind, slot],
+            z_sems.at[0, kind, k], z_sems.at[1, kind, slot], at.to_down,
+        )
+
+    def from_depth(kind, slot):
+        here = z_got.at[kind, slot]
+        return remote(here, here, z_sems.at[0, kind, slot], z_sems.at[1, kind, slot], at.to_up)
 
     def in_to_y(k):
         return remote(
@@ -1171,8 +1247,10 @@
 
     def small_to(hop):
         to = at.seq(hop)
+        first = (at.p * n_seq + to) // 2 * lanes
         return remote(
-            small_y, small_seq.at[s], small_sems.at[0, 2 + to], small_sems.at[1, 2 + s], (at.p, to)
+            small_y.at[:, pl.ds(pl.multiple_of(first, lanes), lanes)], small_seq.at[s],
+            small_sems.at[0, 2 + to], small_sems.at[1, 2 + s], (at.p, to),
         )
 
     def small_from(hop):
@@ -1182,23 +1260,77 @@
             here, here, small_sems.at[0, 2 + src], small_sems.at[1, 2 + src], (at.p, src)
         )
 
+    chained, steps = plan
+    lanes = small_sum.shape[1]
+
     def around_z(hop):
         return lax.rem(z + hop, depth)
 
-    at.meet()
-    for hop in range(1, depth + 1):
-        to_across(0, around_z(hop)).start()
-    loop(0, n_seq, lambda hop: in_to_core(1 - y, at.seq(hop)).start())
-    for load in loads:
-        load.start()
-    loop(0, n_seq, lambda hop: in_to_core(y, at.seq(hop)).start())
-    out_to_core(1 - y).start()
-    out_to_core(y).start()
-    extra_to_core.start()
-    for hop in range(1, depth + 1):
-        to_across(1, around_z(hop)).start()
-    for load in loads:
-        load.wait()
+    def to_depth(kind, k):
+        return remote(
+            x_got.at[kind, k], z_got.at[kind, z],
+            z_sems.at[0, kind, k], z_sems.at[1, kind, z], (at.p, 2 * k + x),
+        )
+
+    def turn(i):
+        return jnp.where(lax.rem(i, 2) == 0, depth - 1 - i // 2, i // 2)
+
+    def order(kind, i):
+        return turn(i) if chained[kind] else around_z(i + 1)
+
+    def across(j):
+        to_across(j // depth, order(j // depth, j % depth)).start()
+
+    def straight(kind, i):
+        k = around_z(i + 1)
+        to_across(kind, k).wait_recv()
+        add_rows(x_got.at[kind, k], [x_got.at[kind, k], own_parts.at[kind, k]])
+        if i + 1 < depth:
+            to_depth(kind, k).start()
+
+    def chain(kind, i):
+        k = turn(i)
+        to_across(kind, k).wait_recv()
+        got, mine = x_got.at[kind, k], own_parts.at[kind, k]
+        begins = ((z == 0) & (k > 0)) | ((z == depth - 1) & (k < depth - 1)) | (z == k)
+
+        @pl.when(begins)
+        def _():
+            add_rows(got, [got, mine])
+
+        @pl.when(jnp.logical_not(begins))
+        def _():
+            from_depth(kind, k).wait_recv()
+            add_rows(got, [got, mine, z_got.at[kind, k]])
+
+        @pl.when(z < k)
+        def _():
+            to_up(kind, k).start()
+
+        @pl.when(z > k)
+        def _():
+            to_down(kind, k).start()
+
+    def finish(kind):
+        if not chained[kind]:
+            others = [around_z(hop) for hop in range(1, depth)]
+            for k in others:
+                from_depth(kind, k).wait_recv()
+            add_rows(
+                sums.at[kind], [x_got.at[kind, z]] + [z_got.at[kind, k] for k in others], rows=16
+            )
+            return
+        add_rows(sums.at[kind], [x_got.at[kind, z]], rows=16)
+
+        @pl.when(z > 0)
+        def _():
+            from_depth(kind, z).wait_recv()
+            add_rows(sums.at[kind], [sums.at[kind], z_got.at[kind, z]], rows=16)
+
+        @pl.when(z < depth - 1)
+        def _():
+            from_depth(kind, depth).wait_recv()
+            add_rows(sums.at[kind], [sums.at[kind], z_got.at[kind, depth]], rows=16)
 
     def to_y_step(hop):
         k = at.seq(hop)
@@ -1206,24 +1338,6 @@
         add_rows(in_core.at[1 - y, k], [in_core.at[1 - y, k], in_own.at[1 - y, k]])
         in_to_y(k).start()
 
-    loop(0, n_seq, to_y_step)
-    out_to_core(1 - y).wait_recv()
-    extra_to_core.wait_recv()
-    add_rows(out_core.at[1 - y, body], [out_core.at[1 - y, body], out_own.at[1 - y, body]])
-    out_to_y.start()
-
-    @pl.when(y == 1)
-    def _():
-        add_rows(out_core.at[0, extra], [out_core.at[0, extra], out_own.at[0, extra]])
-        extra_to_y.start()
-
-    def depth_step(kind, hop):
-        k = around_z(hop)
-        to_across(kind, k).wait_recv()
-        add_rows(x_got.at[kind, k], [x_got.at[kind, k], own_parts.at[kind, k]])
-        if hop < depth:
-            to_depth(kind, k).start()
-
     def owner_step(hop):
         k = at.seq(hop)
         in_to_core(y, k).wait_recv()
@@ -1238,65 +1352,103 @@
         def _():
             in_keep.start()
 
-    for hop in range(1, depth + 1):
-        depth_step(0, hop)
-        for one in range(n_seq // depth):
-            owner_step((hop - 1) * (n_seq // depth) + one + 1)
-
-    def finish(kind):
-        others = [around_z(hop) for hop in range(1, depth)]
-        for k in others:
-            from_depth(kind, k).wait_recv()
-        add_rows(
-            sums.at[kind], [x_got.at[kind, z]] + [z_got.at[kind, k] for k in others], rows=16
-        )
-
-    depth_step(1, 1)
-    finish(0)
-
-    small_own[...] = small_ref[...]
-    d_hidden = sums[0]
-    small_own[0:1, :] = jnp.sum(d_hidden * normed_ref[...], axis=0, keepdims=True)
-    small_own[1:2, :] = jnp.sum(d_hidden, axis=0, keepdims=True)
-    small_to_core.start()
-    depth_step(1, 2)
-    small_to_core.wait_recv()
-    small_core[...] = small_core[...] + small_own[...]
-    small_to_y.start()
-    out_to_core(y).wait_recv()
-    out_to_y.wait_recv()
-    add_rows(out_sum.at[body], [out_core.at[y, body], out_own.at[y, body], out_y.at[body]])
-
-    @pl.when(y == 0)
-    def _():
-        extra_to_y.wait_recv()
-        add_rows(out_sum.at[extra], [out_core.at[0, extra], out_own.at[0, extra], out_y.at[extra]])
-
-        @pl.when(c == 0)
+    def out_y_step():
+        out_to_core(1 - y).wait_recv()
+        extra_to_core.wait_recv()
+        add_rows(out_core.at[1 - y, body], [out_core.at[1 - y, body], out_own.at[1 - y, body]])
+        out_to_y.start()
+
+        @pl.when(y == 1)
         def _():
-            out_shift(keep).start()
-
-        @pl.when((c == 1) & (s == n_seq - 1))
+            add_rows(out_core.at[0, extra], [out_core.at[0, extra], out_own.at[0, extra]])
+            extra_to_y.start()
+
+    def out_end():
+        out_to_core(y).wait_recv()
+        out_to_y.wait_recv()
+        add_rows(out_sum.at[body], [out_core.at[y, body], out_own.at[y, body], out_y.at[body]])
+
+        @pl.when(y == 0)
         def _():
-            out_shift(main).start()
-
-        @pl.when((c == 1) & (s < n_seq - 1))
-        def _():
-            out_shift(starts[2] - starts[1] - late).start()
-
-    depth_step(1, 3)
-    small_to_y.wait()
-    small_y[...] = small_core[...] + small_y[...]
-    loop(1, n_seq, lambda hop: small_to(hop).start())
-    for hop in range(4, depth + 1):
-        depth_step(1, hop)
-    small_sum[...] = small_y[...]
-
-    def small_add(hop):
-        small_from(hop).wait_recv()
-        small_sum[...] = small_sum[...] + small_seq[at.seq(-hop)]
-
-    loop(1, n_seq, small_add)
+            extra_to_y.wait_recv()
+            add_rows(
+                out_sum.at[extra], [out_core.at[0, extra], out_own.at[0, extra], out_y.at[extra]]
+            )
+
+            @pl.when(c == 0)
+            def _():
+                out_shift(keep).start()
+
+            @pl.when((c == 1) & (s == n_seq - 1))
+            def _():
+                out_shift(main).start()
+
+            @pl.when((c == 1) & (s < n_seq - 1))
+            def _():
+                out_shift(first_act - late).start()
+
+    def small_step(i):
+        if i == 0:
+            finish(0)
+            small_own[...] = small_ref[...]
+            d_hidden = sums[0]
+            small_own[0:1, :] = jnp.sum(d_hidden * normed_ref[...], axis=0, keepdims=True)
+            small_own[1:2, :] = jnp.sum(d_hidden, axis=0, keepdims=True)
+            small_to_core.start()
+        elif i == 1:
+            small_to_core.wait_recv()
+            small_core[...] = small_core[...] + small_own[...]
+            small_to_y.start()
+        elif i == 2:
+            small_to_y.wait()
+            small_y[...] = small_core[...] + small_y[...]
+            loop(1, n_seq, lambda hop: small_to(hop).start())
+        else:
+            first = (at.p * n_seq + s) // 2 * lanes
+            small_sum[...] = small_y[:, pl.ds(pl.multiple_of(first, lanes), lanes)]
+
+            def small_add(hop):
+                small_from(hop).wait_recv()
+                small_sum[...] = small_sum[...] + small_seq[at.seq(-hop)]
+
+            loop(1, n_seq, small_add)
+
+    def core_step(i):
+        if i == 0:
+            loop(0, n_seq, lambda hop: in_to_core(1 - y, at.seq(hop)).start())
+            for load in loads:
+                load.start()
+        elif i == 1:
+            loop(0, n_seq, lambda hop: in_to_core(y, at.seq(hop)).start())
+        elif i == 2:
+            out_to_core(1 - y).start()
+            out_to_core(y).start()
+            extra_to_core.start()
+        else:
+            for load in loads:
+                load.wait()
+
+    at.meet()
+    for what, i in steps:
+        if what == 0:
+            across(i)
+        elif what == 1:
+            core_step(i)
+        elif what == 2:
+            to_y_step(i)
+        elif what == 3:
+            owner_step(i)
+        elif what == 4:
+            kind = i // depth
+            (chain if chained[kind] else straight)(kind, i % depth)
+        elif what == 5:
+            small_step(i)
+        elif what == 7:
+            work(i)
+        elif i == 0:
+            out_y_step()
+        else:
+            out_end()
     finish(1)
 
     @pl.when(y == 0)
@@ -1331,35 +1483,46 @@
     for kind in range(2):
         for k in range(depth):
             to_across(kind, k).wait_send()
-        for hop in range(1, depth):
-            to_depth(kind, around_z(hop)).wait_send()
-
-
-def reduce_all(n_dp, n_seq, late, starts, keep, d_part, b_part, in_part, out_part, normed, small):
+
+            @pl.when(z < k)
+            def _():
+                (to_up if chained[kind] else to_depth)(kind, k).wait_send()
+
+            @pl.when(z > k)
+            def _():
+                (to_down if chained[kind] else to_depth)(kind, k).wait_send()
+
+
+def reduce_all(
+    plan, n_dp, n_seq, late, first_act, keep, sent, d_proj, joined, hidden, g, w, o, normed, small
+):
     depth = n_seq // 2
-    block = d_part.shape[2:]
-    in_block = in_part.shape[2:]
+    d_sent, _, in_sent, out_sent = sent
+    block = d_sent.shape[1:]
+    in_block = in_sent.shape[2:]
     width = block[1]
-    main = starts[1] - starts[0]
+    main = joined.shape[-1] // n_dp
     slot = main + late
     bf16, f32 = jnp.bfloat16, jnp.float32
     rest, near = pl.BlockSpec(memory_space=pl.ANY), pl.BlockSpec(memory_space=pltpu.VMEM)
     dma = pltpu.SemaphoreType.DMA
     return pl.pallas_call(
-        functools.partial(reduce_kernel, n_seq=n_seq, late=late, starts=starts, keep=keep),
-        in_specs=[rest, rest, rest, rest, near, near],
+        functools.partial(
+            reduce_kernel, n_seq=n_seq, late=late, first_act=first_act, keep=keep, plan=plan
+        ),
+        in_specs=[rest] * 10 + [near, near],
         out_specs=[near, rest, near, rest, near],
         out_shape=[
             jax.ShapeDtypeStruct((2,) + block, f32),
             jax.ShapeDtypeStruct((n_seq,) + in_block, bf16),
             jax.ShapeDtypeStruct((slot, width), bf16),
             jax.ShapeDtypeStruct((late, width), bf16),
-            jax.ShapeDtypeStruct(small.shape, f32),
+            jax.ShapeDtypeStruct((small.shape[0], 128), f32),
         ],
         scratch_shapes=[
             pltpu.VMEM((2, depth) + block, bf16),
             pltpu.VMEM((2, depth) + block, bf16),
-            pltpu.VMEM((2, depth) + block, bf16),
+            pltpu.VMEM((2, depth + 1) + block, bf16),
             pltpu.VMEM((2, n_seq) + in_block, bf16),
             pltpu.VMEM((2, n_seq) + in_block, bf16),
             pltpu.VMEM((n_seq,) + in_block, bf16),
@@ -1369,15 +1532,87 @@
             pltpu.VMEM(small.shape, f32),
             pltpu.VMEM(small.shape, f32),
             pltpu.VMEM(small.shape, f32),
-            pltpu.VMEM((n_seq,) + small.shape, f32),
-            dma((7,)), dma((2, 2, depth)), dma((2, 2, depth)), dma((2, 2, n_seq)), dma((2, n_seq)),
-            dma((2, n_seq)), dma((2, 6)), dma((2, 2 + n_seq)), dma((1,)),
+            pltpu.VMEM((n_seq, small.shape[0], 128), f32),
+            pltpu.VMEM(d_proj.shape, bf16),
+            pltpu.VMEM(joined.shape, bf16),
+            pltpu.VMEM((2,) + hidden.shape[:3] + (width // n_dp,), bf16),
+            pltpu.VMEM(g.shape, bf16),
+            pltpu.VMEM((2, 256, w.shape[1]), bf16),
+            pltpu.VMEM((2, o.shape[0], 512), bf16),
+            dma((7,)), dma((2, 2, depth)), dma((2, 2, depth + 1)), dma((2, 2, n_seq)), dma((2, n_seq)),
+            dma((2, n_seq)), dma((2, 6)), dma((2, 2 + n_seq)), dma((1,)), dma((2,)), dma((2,)),
         ],
         compiler_params=pltpu.CompilerParams(
-            collective_id=1, has_side_effects=True, vmem_limit_bytes=56 * 2**20
+            collective_id=1, has_side_effects=True, vmem_limit_bytes=60 * 2**20
         ),
         name="reduce_all",
-    )(d_part, b_part, in_part, out_part, normed, small)
+    )(*sent, d_proj, joined, hidden, g, w, o, normed, small)
+
+def shares(n_seq, width, ffn, att, act):
+    stretches, at = [], 0
+    for i in range(3):
+        stretches.append((i * width, at, att))
+        at += att
+    for half in range(2):
+        first = 3 * width + half * ffn
+        for some in act:
+            stretches.append((first, at, some))
+            at += some
+            first += some * n_seq
+    return stretches
+
+
+def share_kernel(w_ref, out_ref, *, stretches):
+    for s in range(out_ref.shape[0]):
+        parts = [w_ref[:, first + s * some : first + (s + 1) * some] for first, _, some in stretches]
+        out_ref[s] = jnp.concatenate(parts, axis=1).astype(out_ref.dtype)
+
+
+def share_out(weight, n_seq, stretches):
+    rows, columns = weight.shape
+    step = 16
+    return pl.pallas_call(
+        functools.partial(share_kernel, stretches=stretches),
+        grid=(rows // step,),
+        in_specs=[pl.BlockSpec((step, columns), lambda i: (i, 0))],
+        out_specs=pl.BlockSpec((n_seq, step, columns // n_seq), lambda i: (0, i, 0)),
+        out_shape=jax.ShapeDtypeStruct((n_seq, rows, columns // n_seq), jnp.bfloat16),
+        compiler_params=pltpu.CompilerParams(vmem_limit_bytes=56 * 2**20),
+        name="share_out",
+    )(weight)
+
+
+def update_kernel(
+    sum_ref, w_ref, m_ref, v_ref, a_ref, w_out, v_out, a_out, g_out, *, stretches, rate, decay
+):
+    n_seq = sum_ref.shape[0]
+    for first, at, some in stretches:
+        columns = slice(first, first + n_seq * some)
+        parts = [sum_ref[s, :, at : at + some].astype(jnp.float32) for s in range(n_seq)]
+        gradient = jnp.concatenate(parts, axis=1)
+        g_out[:, columns] = gradient
+        w_out[:, columns], v_out[:, columns], a_out[:, columns] = adam_update(
+            w_ref[:, columns], m_ref[:, columns], v_ref[:, columns], a_ref[:, columns],
+            gradient, rate, decay,
+        )
+
+
+def update_in(sums, weight, first, second, average, stretches):
+    n_seq, rows, share = sums.shape
+    step = 16
+    wide = pl.BlockSpec((step, weight.shape[1]), lambda i: (i, 0))
+    out = jax.ShapeDtypeStruct(weight.shape, jnp.float32)
+    return pl.pallas_call(
+        functools.partial(
+            update_kernel, stretches=stretches, rate=matrix_rate, decay=weight_decay
+        ),
+        grid=(rows // step,),
+        in_specs=[pl.BlockSpec((n_seq, step, share), lambda i: (0, i, 0))] + [wide] * 4,
+        out_specs=[wide] * 4,
+        out_shape=[out] * 4,
+        compiler_params=pltpu.CompilerParams(vmem_limit_bytes=56 * 2**20),
+        name="update_in",
+    )(sums, weight, first, second, average)
 
 def split_heads(
     n_dp, n_seq, tokens, cotangent, segment_ids, doc_positions,
@@ -1397,27 +1632,10 @@
     late = width - dp_rows
     act = [(dp_rows - late) // n_seq, own, own]
     act_all = sum(act)
-    cuts = [0, act[0] * n_seq, (act[0] + own) * n_seq, ffn]
     lead = att - own
     p, s = lax.axis_index("dp"), lax.axis_index("seq")
 
-    def share(v):
-        parts = [v[:, i * width : (i + 1) * width].reshape(-1, n_seq, att) for i in range(3)]
-        for half in range(2):
-            base = 3 * width + half * ffn
-            for i in range(3):
-                parts.append(v[:, base + cuts[i] : base + cuts[i + 1]].reshape(-1, n_seq, act[i]))
-        return jnp.transpose(jnp.concatenate(parts, axis=2), (1, 0, 2))
-
-    def unshare(v):
-        v = jnp.transpose(v, (1, 0, 2))
-        sizes = [att] * 3 + act * 2
-        parts, at = [], 0
-        for size in sizes:
-            parts.append(v[:, :, at : at + size].reshape(v.shape[0], n_seq * size))
-            at += size
-        return jnp.concatenate(parts, axis=1)
-
+    stretches = shares(n_seq, width, ffn, att, act)
     out_low = out_weight.astype(bf16)
     small_low = small_params.astype(bf16).astype(f32).T
     widen = lambda v, n: jnp.pad(v, ((0, n - v.shape[0]), (0, 128 - v.shape[1])))
@@ -1431,7 +1649,7 @@
     odd = jnp.concatenate([jnp.zeros_like(tile[:8, :in_rows]), tile[:8, :in_rows]], axis=1)
     tile = jnp.concatenate([jnp.where(s % 2 == 1, odd, tile[:8]), tile[8:]], axis=0)
     _, g_full, in_low, _, tiles, hidden, out_mine, proj, d_joined = gather_all(
-        n_dp, n_seq, late, lead, tokens, cotangent, share(in_weight.astype(bf16)), out_low, tile
+        n_dp, n_seq, late, lead, tokens, cotangent, share_out(in_weight, n_seq, stretches), out_low, tile
     )
     g_full, hidden = g_full.reshape(all_tokens, width), hidden.reshape(all_tokens, width)
     in_low = in_low.reshape(n_dp * n_seq * in_rows, 3 * att + 2 * act_all)
@@ -1467,27 +1685,34 @@
         axis=1,
     )
     joined, d_proj, bias_part = middle(
-        proj, bias, d_joined, rope, seg_full, n_seq, att, act_all, head_size
-    )
-
-    blocks = lambda v: v.reshape(2, n_seq // 2, rows * own_tokens, width)
-    branch = jnp.dot(joined, out_mine, preferred_element_type=f32).astype(bf16)
-    d_hidden = lax.dot_general(
-        d_proj, in_low, (((1,), (1,)), ((), ())), preferred_element_type=f32
+        proj, bias, d_joined, rope, seg_full, n_seq, att, act, head_size
+    )
+
+    blocks = lambda v: v.reshape(2, n_seq // 2, rows * own_tokens, v.shape[-1])
+    x, c = s % 2, p % 2
+    across = lambda v: lax.dynamic_index_in_dim(blocks(v), 1 - x, 0, keepdims=False)
+    d_sent = jnp.einsum("ztk,fk->ztf", across(d_proj), in_low, preferred_element_type=f32)
+    b_sent = jnp.einsum("ztk,kf->ztf", across(joined), out_mine, preferred_element_type=f32)
+
+    def to_core(v):
+        some = v.shape[1] // n_dp
+        firsts = [(2 * y_to + 1 - c) * some for y_to in range(2)]
+        return [lax.dynamic_slice_in_dim(v, first, some, 1) for first in firsts]
+
+    over_tokens = lambda a, b: lax.dot_general(
+        a, b, (((0,), (0,)), ((), ())), preferred_element_type=f32
     ).astype(bf16)
-    out_part = lax.dot_general(
-        joined, g_full, (((0,), (0,)), ((), ())), preferred_element_type=f32
-    ).astype(bf16)
-    in_part = lax.dot_general(
-        hidden, d_proj, (((0,), (0,)), ((), ())), preferred_element_type=f32
-    ).astype(bf16)
+    in_sent = over_tokens(jnp.concatenate(to_core(hidden), axis=1), d_proj).reshape(2, n_seq, in_rows, -1)
+    left = jnp.concatenate([*to_core(joined), joined[:, keep:att]], axis=1)
+    out_sent = over_tokens(left, g_full)
     normed, inv_std = normalise(tokens.reshape(rows * own_tokens, width))
     small_part = lax.dynamic_update_slice(jnp.zeros((8, width), f32), bias_part[:3], (2, s * att))
-    starts = (0, att, att + act[0], att + act[0] + own)
+    plan = ((1, 1), ((0, 0), (0, 1), (1, 0), (1, 1), (1, 2), (0, 2), (0, 3), (1, 3), (7, 2), (0, 4), (0, 5), (0, 6), (0, 7), (7, 0), (2, 0), (2, 1), (2, 2), (2, 3), (2, 4), (2, 5), (2, 6), (2, 7), (7, 4), (6, 0), (7, 3), (4, 0), (3, 0), (3, 1), (4, 1), (3, 2), (3, 3), (7, 1), (4, 2), (3, 4), (4, 3), (3, 5), (5, 0), (4, 4), (5, 1), (4, 5), (5, 2), (4, 6), (6, 1), (4, 7), (3, 6), (3, 7), (5, 3)))
     sums, in_sum, out_sum, from_prev, small_sum = reduce_all(
-        n_dp, n_seq, late, starts, keep,
-        blocks(d_hidden), blocks(branch),
-        in_part.reshape(n_dp, n_seq, in_rows, -1), out_part, normed, small_part,
+        plan, n_dp, n_seq, late, act[0], keep,
+        (d_sent.astype(bf16), b_sent.astype(bf16), in_sent, out_sent),
+        blocks(d_proj), blocks(joined), blocks(hidden), blocks(g_full), in_low, out_mine,
+        normed, small_part,
     )
     d_hidden, branch = sums[0], sums[1]
 
@@ -1501,16 +1726,15 @@
             - normed * jnp.mean(d_normed * normed, axis=-1, keepdims=True)
         )
     ).reshape(tokens.shape)
-    small_grad = lax.dynamic_slice(small_sum, (0, (p * n_seq + s) * in_rows), (8, in_rows))[:5].T
+    small_grad = lax.dynamic_slice(small_sum, (0, s % 2 * in_rows), (8, in_rows))[:5].T
 
     count = jnp.where(p == 0, lead * s, jnp.where(p == 1, late - lead * s, 0))
     out_grad = lax.dynamic_slice_in_dim(
         jnp.concatenate([from_prev, out_sum[:own]], axis=0), late - count, own, 0
     ).astype(f32)
-    in_grad = unshare(in_sum).astype(f32)
-
-    in_new = adam_update(
-        in_weight, in_first, in_second, in_average, in_grad, matrix_rate, weight_decay
+
+    *in_new, in_grad = update_in(
+        in_sum, in_weight, in_first, in_second, in_average, stretches
     )
     out_new = adam_update(
         out_weight, out_first, out_second, out_average, out_grad, matrix_rate, weight_decay

time: 471 us -> 441 us (0.936)
  local copies, waits for them, and re-layouts: 31.3 us -> 11.5 us
  other arithmetic: 33.4 us -> 16.8 us
  Pallas kernels: 361 us -> 377 us
  matrix products: 39.6 us -> 31.2 us
    add x3 -> x2, other arithmetic: 21.7 us -> 7.58 us  [adam_update(): average_new = average_keep * average + (1.0 - average_keep) * weight_new]
    pallas_call x1 -> x3, Pallas kernels: 192 us -> 205 us  [the longest x1 187 us: reduce_all(): pl.pallas_call(functools.partial(reduce_kernel, n_seq=n_seq, late=late, f...]
    dot_general x4, matrix products: 39.6 us -> 31.2 us  [the longest x2 15.7 us: split_heads(): lax.dot_general(a, b, (((0,), (0,)), ((), ())), preferred_element_type=f32)]
    reshape x23 -> x0, local copies, waits for them, and re-layouts: 7.94 us -> none  [the longest x12 3.76 us: share(): v[:, base + cuts[i]:base + cuts[i + 1]].reshape(-1, n_seq, act[i])]
    unnamed x56 -> x33, local copies, waits for them, and re-layouts: 7.35 us -> 0.72 us
    concatenate x3 -> x0, local copies, waits for them, and re-layouts: 5.59 us -> none  [the longest x1 4.86 us: share(): return jnp.transpose(jnp.concatenate(parts, axis=2), (1, 0, 2))]
where the time goes in v5:
time: 441 us; the launch traced here: 437 us
  Pallas kernels  377 us (85%)
  matrix products  31.2 us (7%)
  other arithmetic  16.8 us (4%)
  local copies, waits for them, and re-layouts  11.5 us (3%)
    pallas_call x1, Pallas kernels, reduce_all(): pl.pallas_call(functools.partial(reduce_kernel, n_seq=n_seq, late=late, f...  187 us
    pallas_call x1, Pallas kernels, gather_all(): pl.pallas_call(functools.partial(gather_kernel, n_seq=n_seq, late=late, l...  147 us
    pallas_call x1, Pallas kernels, middle(): pl.pallas_call(functools.partial(middle_kernel, head_size=head_size, half...  24.9 us
    dot_general x2, matrix products, split_heads(): lax.dot_general(a, b, (((0,), (0,)), ((), ())), preferred_element_type=f32)  15.7 us
    pallas_call x1, Pallas kernels, update_in(): pl.pallas_call(functools.partial(update_kernel, stretches=stretches, rate...  13.5 us
    dot_general x1, matrix products, split_heads(): jnp.einsum('ztk,fk->ztf', across(d_proj), in_low, preferred_element_type=...  9.35 us

profile of v5, /device:TPU:11, one launch (start us, length us, event | category | flops | bytes accessed | tf_op | source)
XLA Modules:
  0.0 437.4 jit_solution(1790409134946364930)
XLA Ops:
  0.7 0.7 convert_bitcast_fusion
  1.4 0.1 pad_select_fusion
  1.4 0.7 add_convert_fusion.1
  2.1 0.6 select_maximum_fusion.tile_ref
  2.7 0.0 copy-start.1
  2.7 4.7 %share_out.1.w_ref = bf16[8,64,2176]{2,1,0:T(8,128)(2,1)} custom-call(f32[64,17408]{1,0:T(8,128)} %w_ref.3), custom_call_target="tpu_custom_call" | custom-call | tf_op jit(solution)/shard_map/share_out/pallas_call | solution.py:1574
  7.5 0.0 copy-done.1
  7.5 1.1 convert_element_type.48.o_ref
  8.6 146.6 %gather_all.1 = (bf16[2,4,2,64,2048]{4,3,2,1,0:T(8,128)(2,1)}, bf16[2,4,2,64,2048]{4,3,2,1,0:T(8,128)(2,1)}, bf16[4,8,64,2176]{3,2,1,0:T(8,128)(2,1)}, bf16[4,36...) custom-call(bf16[2,64,2048]{2,1,0:T(8,128)(2,1)} %x_ref.1, ...), custom_call_target="tpu_custom_call" | custom-call | tf_op jit(solution)/shard_map/gather_all/pallas_call | solution.py:1028
  155.2 0.8 dynamic-slice_bitcast_fusion
  156.1 0.1 mul.185
  156.2 0.2 fusion.24
  156.4 0.2 fusion.23
  156.6 0.2 fusion.22
  156.8 0.2 fusion.25
  157.1 0.0 copy-start.5
  157.1 0.2 fusion.27
  157.3 1.3 pad_maximum_fusion.rope_ref
  158.6 1.3 broadcast_in_dim_reshape.9.seg_q_ref
  159.9 0.7 broadcast_in_dim_reshape.8.seg_k_ref
  160.5 0.0 copy-done.5
  160.6 0.6 copy.45
  161.2 24.9 %middle.1 = (bf16[2,4,2,64,1024]{4,3,2,1,0:T(8,128)(2,1)}, bf16[2,4,2,64,2176]{4,3,2,1,0:T(8,128)(2,1)}, f32[8,256]{1,0:T(8,128)}) custom-call(f32[2,4,2,64,2176]{4,3,2,1,0:T(8,128)} %bitcast.66, f32[2,4,2,64,2176]{4,3,2,1,0:T(8,128)} %bitcast.67, f32[2,4,2,64,2176]{4,3,2,1,0:T(8,128)} %bitcast.68, f32[1,768]{1,0:T(1,128)} %bitcast.95, f32[1,768]{1,0:T(1,128)} %bitcast.96, ...), custom_call_target="tpu_custom_call" | custom-call | tf_op jit(solution)/shard_map/middle/pallas_call | solution.py:514
  186.1 1.3 constant_dynamic-slice_fusion.2
  187.4 1.0 slice.59
  188.4 6.6 %convolution_convert_fusion.1.out_ref = bf16[640,2048]{1,0:T(8,128)(2,1)} fusion(bf16[1024,2048]{1,0:T(8,128)(2,1)} %bitcast.83, bf16[1024,128]{1,0:T(8,128)(2,1)S(1)} %slice.59, bf16[1024,256]{1,0:T(8,128)(2,1)S(1)} %get-tuple-element.67, bf16[1024,256]{1,0:T(8,128)(2,1)S(1)} %get-tuple-element.66), kind=kOutput, calls=%fused_computation.3 | convolution fusion | flops 2689597440 | bytes 8126464 | tf_op jit(solution)/shard_map/dot_general | solution.py:1702
  195.0 1.7 constant_dynamic-slice_fusion.4
  196.6 9.1 %convolution_convert_fusion = bf16[1024,2176]{1,0:T(8,128)(2,1)} fusion(bf16[1024,2176]{1,0:T(8,128)(2,1)} %bitcast.79, bf16[1024,512]{1,0:T(8,128)(2,1)S(1)} %get-tuple-element.63, bf16[1024,512]{1,0:T(8,128)(2,1)S(1)} %get-tuple-element.62), kind=kOutput, calls=%fused_computation | convolution fusion | flops 4569825280 | bytes 11010048 | tf_op jit(solution)/shard_map/dot_general | solution.py:1702
  205.8 6.2 %fusion.2.b_ref = bf16[4,128,2048]{2,1,0:T(8,128)(2,1)} fusion(bf16[1024,2048]{1,0:T(8,128)(2,1)} %get-tuple-element.39.o_ref, bf16[2,4,128,1024]{3,2,1,0:T(8,128)(2,1)} %bitcast.77, s32[]{:T(128)S(6)} %select_n.67), kind=kOutput, calls=%fused_computation.4 | convolution fusion | flops 2148532224 | bytes 7340036 | tf_op jit(solution)/shard_map/ztk,kf->ztf/dot_general | solution.py:1695
  211.9 0.0 copy-start.11
  211.9 9.4 %convolution_convert_fusion.2.d_ref = bf16[4,128,2048]{2,1,0:T(8,128)(2,1)} fusion(bf16[2048,2176,1]{1,0,2:T(8,128)(2,1)} %bitcast.71, bf16[2,4,128,2176]{3,2,1,0:T(8,128)(2,1)} %bitcast.80, s32[]{:T(128)S(6)} %select_n.67), kind=kOutput, calls=%fused_computation.5 | convolution fusion | flops 4564451328 | bytes 13238276 | tf_op jit(solution)/shard_map/ztk,fk->ztf/dot_general | solution.py:1694
  221.3 0.0 copy-done.11
  221.3 0.4 dynamic_update_slice.3.small_ref
  221.7 0.0 copy-start.4
  221.7 0.0 copy-done
  221.8 0.2 convert_reduce_fusion
  221.9 0.3 multiply_reduce_fusion.1
  222.2 0.1 rsqrt.13
  222.3 0.1 div.56
  222.4 1.3 fusion.16.normed_ref
  223.7 0.0 copy-done.4
  223.7 187.2 %reduce_all.1 = (f32[2,128,2048]{2,1,0:T(8,128)}, bf16[8,64,2176]{2,1,0:T(8,128)(2,1)}, bf16[384,2048]{1,0:T(8,128)(2,1)}, bf16[128,2048]{1,0:T(8,128)(2,1)}, f32[8,128]{1,0:T(8,128)}) custom-call(bf16[4,128,2048]{2,1,0:T(8,128)(2,1)} %convolution_convert_fusion.2.d_ref, bf16[4,128,2048]{2,1,0:T(8,128)(2,1)} %fusion.2.b_ref, ...), custom_call_target="tpu_custom_call" | custom-call | tf_op jit(solution)/shard_map/reduce_all/pallas_call | solution.py:1509
  410.9 1.3 slice.54
  412.2 7.0 %multiply_add_fusion = (f32[240,2048]{1,0:T(8,128)}, f32[240,2048]{1,0:T(8,128)}, f32[240,2048]{1,0:T(8,128)}, f32[240,2048]{1,0:T(8,128)}) fusion(f32[240,2048]{1,0:T(8,128)} %param.27, f32[240,2048]{1,0:T(8,128)S(1)} %copy-done.1, f32[240,2048]{1,0:T(8,128)} %param.25, f32[240,2048]{1,0:T(8,128)} %param.26, s32[]{:T(128)S(6)} %select_n.75, ...), kind=kLoop, calls=%fused_computation.13 | loop fusion | flops 11304960 | bytes 17235972 | tf_op jit(solution)/shard_map/add | solution.py:81
  419.2 13.5 %update_in.1 = (f32[64,17408]{1,0:T(8,128)}, f32[64,17408]{1,0:T(8,128)}, f32[64,17408]{1,0:T(8,128)}, f32[64,17408]{1,0:T(8,128)}) custom-call(bf16[8,64,2176]{2,1,0:T(8,128)(2,1)} %get-tuple-element.44.sum_ref, f32[64,17408]{1,0:T(8,128)} %w_ref.3, f32[64,17408]{1,0:T(8,128)} %m_ref.1, f32[64,17408]{1,0:T(8,128)} %v_ref.1, f32[64,17408]{1,0:T(8,128)} %a_ref.1), custom_call_target="tpu_custom_call" | custom-call | tf_op jit(solution)/shard_map/update_in/pallas_call | solution.py:1605
  432.7 0.0 copy-done.2
  432.7 0.4 fusion.19
  433.0 0.1 div.59
  433.1 0.1 div.61
  433.2 1.8 fusion.39
  435.0 0.0 copy-done.3
  435.0 0.0 copy-start.10
  435.0 0.0 copy-start.6
  435.0 0.0 copy-start.7
  435.0 0.0 copy-start.8
  435.0 0.0 copy-start.9
  435.0 1.7 multiply_add_fusion.1
  436.7 0.0 copy-done.10
  436.7 0.1 constant_dynamic-slice_fusion
  436.8 0.0 copy-done.6
  436.8 0.0 copy-done.7
  436.8 0.0 copy-done.8
  436.8 0.0 copy-done.9
  436.8 0.6 multiply_add_fusion.2
  (28 shorter events, 0.2 us)
Async XLA Ops:
  2.7 4.7 %copy-start.1 = (f32[240,2048]{1,0:T(8,128)S(1)}, f32[240,2048]{1,0:T(8,128)}, u32[]{:S(2)}) copy-start(f32[240,2048]{1,0:T(8,128)} %param.24) | copy-start | bytes 5898244
  157.1 3.5 copy-start.5
  211.9 9.4 %copy-start.11 = (f32[8,256]{1,0:T(8,128)S(1)}, f32[8,256]{1,0:T(8,128)}, u32[]{:S(2)}) copy-start(f32[8,256]{1,0:T(8,128)} %get-tuple-element.42) | copy-start | bytes 24580
  211.9 9.8 %copy-start = (bf16[2,64,2048]{2,1,0:T(8,128)(2,1)S(1)}, bf16[2,64,2048]{2,1,0:T(8,128)(2,1)}, u32[]{:S(2)}) copy-start(bf16[2,64,2048]{2,1,0:T(8,128)(2,1)} %x_ref.1) | copy-start | bytes 1572868
  221.7 1.9 copy-start.4
  419.2 13.5 %copy-start.2 = (f32[2,128,2048]{2,1,0:T(8,128)S(1)}, f32[2,128,2048]{2,1,0:T(8,128)}, u32[]{:S(2)}) copy-start(f32[2,128,2048]{2,1,0:T(8,128)} %get-tuple-element.43) | copy-start | bytes 6291460
  433.2 1.8 copy-start.3
  435.0 1.7 copy-start.10
  435.0 1.8 copy-start.6
  435.0 1.8 copy-start.7
  435.0 1.8 copy-start.8
  435.0 1.8 copy-start.9

commit v6 on v5

--- a/solution.py
+++ b/solution.py
@@ -1073,12 +1073,12 @@
 
 
 def reduce_kernel(
-    d_ref, b_ref, in_ref, out_ref, d_proj_ref, joined_ref, hidden_ref, g_ref, w_ref, o_ref,
+    d_ref, in_ref, d_proj_ref, joined_ref, hidden_ref, g_ref, w_ref, o_ref,
     normed_ref, small_ref,
     sums, in_sum, out_sum, out_prev, small_sum,
     own_parts, x_got, z_got, in_own, in_core, in_y, out_own, out_core, out_y,
     small_own, small_core, small_y, small_seq,
-    d_near, j_near, h_near, g_near, w_near, o_near,
+    d_near, j_near, h_near, g_near, w_near, o_near, b_ref, out_ref,
     load_sems, x_sems, z_sems, in_core_sems, in_y_sems, in_sems, out_sems, small_sems, local_sem,
     w_sems, o_sems,
     *, n_seq, late, first_act, keep, plan,
@@ -1122,7 +1122,7 @@
             o_near.at[lax.rem(i, 2)], o_sems.at[lax.rem(i, 2)],
         )
 
-    def streamed(kind, load, count, some, product):
+    def streamed(out, load, count, some, product):
         load(0).start()
 
         def one(i):
@@ -1133,7 +1133,7 @@
             load(i).wait()
             done = product(lax.rem(i, 2)).astype(low)
             columns = pl.ds(pl.multiple_of(i * some, some), some)
-            own_parts[kind, :, :, columns] = done.reshape(depth, block_rows, some)
+            out[:, :, columns] = done.reshape(depth, block_rows, some)
 
         loop(0, count, one)
 
@@ -1142,14 +1142,14 @@
             some = w_near.shape[1]
             left = flat(d_near[x])
             streamed(
-                0, w_load, width // some, some,
+                own_parts.at[0], w_load, width // some, some,
                 lambda k: dot(left, w_near[k], (((1,), (1,)), ((), ()))),
             )
-        elif i == 1:
+        elif i in (1, 5):
             some = o_near.shape[2]
-            left = flat(j_near[x])
+            left = flat(j_near[x if i == 1 else 1 - x])
             streamed(
-                1, o_load, width // some, some,
+                own_parts.at[1] if i == 1 else b_ref, o_load, width // some, some,
                 lambda k: dot(left, o_near[k], (((1,), (0,)), ((), ()))),
             )
         elif i < 4:
@@ -1157,22 +1157,30 @@
             left = flat(h_near[y_to])
             right = flat(d_near[...])
             total = right.shape[1]
-            for first in range(0, total, 512):
-                some = min(512, total - first)
+            for first in range(0, total, 256):
+                some = min(256, total - first)
                 done = dot(left, right[:, first : first + some], (((0,), (0,)), ((), ())))
                 in_own[y_to, :, :, first : first + some] = done.astype(low).reshape(
                     n_seq, -1, some
                 )
         else:
-            right = flat(g_near[...])
-            for y_to in range(2):
-                columns = pl.ds(pl.multiple_of((2 * y_to + c) * main, main), main)
-                out_own[y_to, body] = dot(
-                    flat(j_near[:, :, :, columns]), right, (((0,), (0,)), ((), ()))
-                ).astype(low)
-            out_own[0, extra] = dot(
-                flat(j_near[:, :, :, keep : keep + late]), right, (((0,), (0,)), ((), ()))
-            ).astype(low)
+            core = c if i == 4 else 1 - c
+            for first in range(0, width, width // 4):
+                at_n = slice(first, first + width // 4)
+                right = flat(g_near[:, :, :, at_n])
+                for y_to in range(2):
+                    columns = pl.ds(pl.multiple_of((2 * y_to + core) * main, main), main)
+                    done = dot(flat(j_near[:, :, :, columns]), right, (((0,), (0,)), ((), ())))
+                    if i == 4:
+                        out_own[y_to, body, at_n] = done.astype(low)
+                    else:
+                        out_ref[y_to * main : (y_to + 1) * main, at_n] = done.astype(low)
+                if i == 4:
+                    out_own[0, extra, at_n] = dot(
+                        flat(j_near[:, :, :, keep : keep + late]), right, (((0,), (0,)), ((), ()))
+                    ).astype(low)
+            if i == 6:
+                out_ref[2 * main :] = out_own[0, extra]
 
     def in_to_core(y_to, k):
         return remote(
@@ -1497,7 +1505,7 @@
     plan, n_dp, n_seq, late, first_act, keep, sent, d_proj, joined, hidden, g, w, o, normed, small
 ):
     depth = n_seq // 2
-    d_sent, _, in_sent, out_sent = sent
+    d_sent, in_sent = sent
     block = d_sent.shape[1:]
     in_block = in_sent.shape[2:]
     width = block[1]
@@ -1510,7 +1518,7 @@
         functools.partial(
             reduce_kernel, n_seq=n_seq, late=late, first_act=first_act, keep=keep, plan=plan
         ),
-        in_specs=[rest] * 10 + [near, near],
+        in_specs=[rest] * 8 + [near, near],
         out_specs=[near, rest, near, rest, near],
         out_shape=[
             jax.ShapeDtypeStruct((2,) + block, f32),
@@ -1538,7 +1546,9 @@
             pltpu.VMEM((2,) + hidden.shape[:3] + (width // n_dp,), bf16),
             pltpu.VMEM(g.shape, bf16),
             pltpu.VMEM((2, 256, w.shape[1]), bf16),
-            pltpu.VMEM((2, o.shape[0], 512), bf16),
+            pltpu.VMEM((2, o.shape[0], 256), bf16),
+            pltpu.VMEM((depth,) + block, bf16),
+            pltpu.VMEM((2 * main + late, width), bf16),
             dma((7,)), dma((2, 2, depth)), dma((2, 2, depth + 1)), dma((2, 2, n_seq)), dma((2, n_seq)),
             dma((2, n_seq)), dma((2, 6)), dma((2, 2 + n_seq)), dma((1,)), dma((2,)), dma((2,)),
         ],
@@ -1692,7 +1702,6 @@
     x, c = s % 2, p % 2
     across = lambda v: lax.dynamic_index_in_dim(blocks(v), 1 - x, 0, keepdims=False)
     d_sent = jnp.einsum("ztk,fk->ztf", across(d_proj), in_low, preferred_element_type=f32)
-    b_sent = jnp.einsum("ztk,kf->ztf", across(joined), out_mine, preferred_element_type=f32)
 
     def to_core(v):
         some = v.shape[1] // n_dp
@@ -1703,14 +1712,12 @@
         a, b, (((0,), (0,)), ((), ())), preferred_element_type=f32
     ).astype(bf16)
     in_sent = over_tokens(jnp.concatenate(to_core(hidden), axis=1), d_proj).reshape(2, n_seq, in_rows, -1)
-    left = jnp.concatenate([*to_core(joined), joined[:, keep:att]], axis=1)
-    out_sent = over_tokens(left, g_full)
     normed, inv_std = normalise(tokens.reshape(rows * own_tokens, width))
     small_part = lax.dynamic_update_slice(jnp.zeros((8, width), f32), bias_part[:3], (2, s * att))
-    plan = ((1, 1), ((0, 0), (0, 1), (1, 0), (1, 1), (1, 2), (0, 2), (0, 3), (1, 3), (7, 2), (0, 4), (0, 5), (0, 6), (0, 7), (7, 0), (2, 0), (2, 1), (2, 2), (2, 3), (2, 4), (2, 5), (2, 6), (2, 7), (7, 4), (6, 0), (7, 3), (4, 0), (3, 0), (3, 1), (4, 1), (3, 2), (3, 3), (7, 1), (4, 2), (3, 4), (4, 3), (3, 5), (5, 0), (4, 4), (5, 1), (4, 5), (5, 2), (4, 6), (6, 1), (4, 7), (3, 6), (3, 7), (5, 3)))
+    plan = ((1, 1), ((0, 0), (0, 1), (0, 2), (0, 3), (1, 0), (1, 1), (1, 3), (7, 2), (2, 0), (2, 1), (2, 2), (2, 3), (2, 4), (2, 5), (2, 6), (2, 7), (7, 4), (7, 6), (1, 2), (7, 0), (4, 0), (7, 3), (3, 0), (3, 1), (6, 0), (4, 1), (7, 5), (0, 4), (0, 5), (0, 6), (0, 7), (3, 2), (3, 3), (4, 2), (3, 4), (3, 5), (7, 1), (4, 3), (3, 6), (3, 7), (5, 0), (4, 4), (5, 1), (4, 5), (5, 2), (6, 1), (4, 6), (4, 7), (5, 3)))
     sums, in_sum, out_sum, from_prev, small_sum = reduce_all(
         plan, n_dp, n_seq, late, act[0], keep,
-        (d_sent.astype(bf16), b_sent.astype(bf16), in_sent, out_sent),
+        (d_sent.astype(bf16), in_sent),
         blocks(d_proj), blocks(joined), blocks(hidden), blocks(g_full), in_low, out_mine,
         normed, small_part,
     )

time: 441 us -> 423 us (0.959)
  matrix products: 31.2 us -> 18.4 us
    dot_general x2 -> x1, matrix products: 15.7 us -> 9.1 us  [split_heads(): lax.dot_general(a, b, (((0,), (0,)), ((), ())), preferred_element_type=f32)]
    dot_general x1 -> x0, matrix products: 6.16 us -> none  [split_heads(): jnp.einsum('ztk,kf->ztf', across(joined), out_mine, preferred_element_typ...]
where the time goes in v6:
time: 423 us; the launch traced here: 418 us
  Pallas kernels  373 us (88%)
  matrix products  18.4 us (4%)
  other arithmetic  16.8 us (4%)
  local copies, waits for them, and re-layouts  8.48 us (2%)
    pallas_call x1, Pallas kernels, reduce_all(): pl.pallas_call(functools.partial(reduce_kernel, n_seq=n_seq, late=late, f...  184 us
    pallas_call x1, Pallas kernels, gather_all(): pl.pallas_call(functools.partial(gather_kernel, n_seq=n_seq, late=late, l...  147 us
    pallas_call x1, Pallas kernels, middle(): pl.pallas_call(functools.partial(middle_kernel, head_size=head_size, half...  24.9 us
    pallas_call x1, Pallas kernels, update_in(): pl.pallas_call(functools.partial(update_kernel, stretches=stretches, rate...  13.5 us
    dot_general x1, matrix products, split_heads(): jnp.einsum('ztk,fk->ztf', across(d_proj), in_low, preferred_element_type=...  9.29 us
    dot_general x1, matrix products, split_heads(): lax.dot_general(a, b, (((0,), (0,)), ((), ())), preferred_element_type=f32)  9.1 us

profile of v6, /device:TPU:11, one launch (start us, length us, event | category | flops | bytes accessed | tf_op | source)
XLA Modules:
  0.0 418.1 jit_solution(7141749362603901195)
XLA Ops:
  0.7 0.7 convert_bitcast_fusion
  1.4 0.1 pad_select_fusion
  1.4 0.7 add_convert_fusion.1
  2.1 0.6 select_maximum_fusion.tile_ref
  2.7 0.0 copy-start.1
  2.7 4.7 %share_out.1.w_ref = bf16[8,64,2176]{2,1,0:T(8,128)(2,1)} custom-call(f32[64,17408]{1,0:T(8,128)} %w_ref.3), custom_call_target="tpu_custom_call" | custom-call | tf_op jit(solution)/shard_map/share_out/pallas_call | solution.py:1584
  7.5 0.0 copy-done.1
  7.5 1.1 convert_element_type.42.o_ref
  8.6 146.6 %gather_all.1 = (bf16[2,4,2,64,2048]{4,3,2,1,0:T(8,128)(2,1)}, bf16[2,4,2,64,2048]{4,3,2,1,0:T(8,128)(2,1)}, bf16[4,8,64,2176]{3,2,1,0:T(8,128)(2,1)}, bf16[4,36...) custom-call(bf16[2,64,2048]{2,1,0:T(8,128)(2,1)} %x_ref.1, ...), custom_call_target="tpu_custom_call" | custom-call | tf_op jit(solution)/shard_map/gather_all/pallas_call | solution.py:1028
  155.2 0.8 dynamic-slice_bitcast_fusion
  156.1 0.1 mul.179
  156.1 0.2 fusion.12
  156.3 0.2 fusion.11
  156.6 0.2 fusion.10
  156.8 0.2 fusion.13
  157.1 0.2 fusion.15
  157.3 0.0 copy-start.5
  157.3 1.3 pad_maximum_fusion.rope_ref
  158.6 1.3 broadcast_in_dim_reshape.9.seg_q_ref
  159.9 0.7 broadcast_in_dim_reshape.8.seg_k_ref
  160.5 0.0 copy-done.5
  160.6 0.6 copy.45
  161.2 24.9 %middle.1 = (bf16[2,4,2,64,1024]{4,3,2,1,0:T(8,128)(2,1)}, bf16[2,4,2,64,2176]{4,3,2,1,0:T(8,128)(2,1)}, f32[8,256]{1,0:T(8,128)}) custom-call(f32[2,4,2,64,2176]{4,3,2,1,0:T(8,128)} %bitcast.55, f32[2,4,2,64,2176]{4,3,2,1,0:T(8,128)} %bitcast.56, f32[2,4,2,64,2176]{4,3,2,1,0:T(8,128)} %bitcast.57, f32[1,768]{1,0:T(1,128)} %bitcast.80, f32[1,768]{1,0:T(1,128)} %bitcast.81, ...), custom_call_target="tpu_custom_call" | custom-call | tf_op jit(solution)/shard_map/middle/pallas_call | solution.py:514
  186.1 1.7 constant_dynamic-slice_fusion.2
  187.8 9.1 %convolution_convert_fusion = bf16[1024,2176]{1,0:T(8,128)(2,1)} fusion(bf16[1024,2176]{1,0:T(8,128)(2,1)} %bitcast.64, bf16[1024,512]{1,0:T(8,128)(2,1)S(1)} %get-tuple-element.63, bf16[1024,512]{1,0:T(8,128)(2,1)S(1)} %get-tuple-element.62), kind=kOutput, calls=%fused_computation | convolution fusion | flops 4569825280 | bytes 11010048 | tf_op jit(solution)/shard_map/dot_general | solution.py:1711
  196.9 0.0 copy-start.11
  196.9 0.0 copy-start
  196.9 9.3 %convolution_convert_fusion.1.d_ref = bf16[4,128,2048]{2,1,0:T(8,128)(2,1)} fusion(bf16[2048,2176,1]{1,0,2:T(8,128)(2,1)} %bitcast.60, bf16[2,4,128,2176]{3,2,1,0:T(8,128)(2,1)} %bitcast.65, s32[]{:T(128)S(6)} %select_n.59), kind=kOutput, calls=%fused_computation.1 | convolution fusion | flops 4564451328 | bytes 13238276 | tf_op jit(solution)/shard_map/ztk,fk->ztf/dot_general | solution.py:1704
  206.2 0.0 copy-done.11
  206.2 0.4 dynamic_update_slice.3.small_ref
  206.6 0.0 copy-start.4
  206.6 0.0 copy-done
  206.7 0.2 convert_reduce_fusion
  206.8 0.3 multiply_reduce_fusion.1
  207.1 0.1 rsqrt.13
  207.2 0.1 div.56
  207.3 1.3 fusion.6.normed_ref
  208.6 0.0 copy-done.4
  208.6 183.7 %reduce_all.1 = (f32[2,128,2048]{2,1,0:T(8,128)}, bf16[8,64,2176]{2,1,0:T(8,128)(2,1)}, bf16[384,2048]{1,0:T(8,128)(2,1)}, bf16[128,2048]{1,0:T(8,128)(2,1)}, f32[8,128]{1,0:T(8,128)}) custom-call(bf16[4,128,2048]{2,1,0:T(8,128)(2,1)} %convolution_convert_fusion.1.d_ref, bf16[2,8,64,2176]{3,2,1,0:T(8,128)(2,1)} %bitcast.67, ...), custom_call_target="tpu_custom_call" | custom-call | tf_op jit(solution)/shard_map/reduce_all/pallas_call | solution.py:1517
  392.3 1.3 slice.50
  393.6 6.9 %multiply_add_fusion = (f32[240,2048]{1,0:T(8,128)}, f32[240,2048]{1,0:T(8,128)}, f32[240,2048]{1,0:T(8,128)}, f32[240,2048]{1,0:T(8,128)}) fusion(f32[240,2048]{1,0:T(8,128)} %param.27, f32[240,2048]{1,0:T(8,128)S(1)} %copy-done.1, f32[240,2048]{1,0:T(8,128)} %param.25, f32[240,2048]{1,0:T(8,128)} %param.26, s32[]{:T(128)S(6)} %select_n.65, ...), kind=kLoop, calls=%fused_computation.9 | loop fusion | flops 11304960 | bytes 17235972 | tf_op jit(solution)/shard_map/add | solution.py:81
  400.6 0.0 copy-start.2
  400.6 13.5 %update_in.1 = (f32[64,17408]{1,0:T(8,128)}, f32[64,17408]{1,0:T(8,128)}, f32[64,17408]{1,0:T(8,128)}, f32[64,17408]{1,0:T(8,128)}) custom-call(bf16[8,64,2176]{2,1,0:T(8,128)(2,1)} %get-tuple-element.44.sum_ref, f32[64,17408]{1,0:T(8,128)} %w_ref.3, f32[64,17408]{1,0:T(8,128)} %m_ref.1, f32[64,17408]{1,0:T(8,128)} %v_ref.1, f32[64,17408]{1,0:T(8,128)} %a_ref.1), custom_call_target="tpu_custom_call" | custom-call | tf_op jit(solution)/shard_map/update_in/pallas_call | solution.py:1615
  414.0 0.0 copy-done.2
  414.1 0.4 fusion.7
  414.4 0.1 div.59
  414.5 0.1 div.61
  414.6 0.0 copy-start.3
  414.6 0.1 fusion.25
  414.7 0.9 copy-done.3
  415.6 0.0 copy-start.10
  415.6 0.0 copy-start.6
  415.6 0.0 copy-start.7
  415.6 0.0 copy-start.8
  415.6 0.0 copy-start.9
  415.7 1.7 multiply_add_fusion.1
  417.3 0.0 copy-done.10
  417.4 0.1 constant_dynamic-slice_fusion
  417.4 0.0 copy-done.6
  417.4 0.0 copy-done.7
  417.4 0.0 copy-done.8
  417.4 0.0 copy-done.9
  417.4 0.6 multiply_add_fusion.2
  (25 shorter events, 0.2 us)
Async XLA Ops:
  2.7 4.7 %copy-start.1 = (f32[240,2048]{1,0:T(8,128)S(1)}, f32[240,2048]{1,0:T(8,128)}, u32[]{:S(2)}) copy-start(f32[240,2048]{1,0:T(8,128)} %param.24) | copy-start | bytes 5898244
  157.3 3.2 copy-start.5
  196.9 9.3 %copy-start.11 = (f32[8,256]{1,0:T(8,128)S(1)}, f32[8,256]{1,0:T(8,128)}, u32[]{:S(2)}) copy-start(f32[8,256]{1,0:T(8,128)} %get-tuple-element.42) | copy-start | bytes 24580
  196.9 9.8 %copy-start = (bf16[2,64,2048]{2,1,0:T(8,128)(2,1)S(1)}, bf16[2,64,2048]{2,1,0:T(8,128)(2,1)}, u32[]{:S(2)}) copy-start(bf16[2,64,2048]{2,1,0:T(8,128)(2,1)} %x_ref.1) | copy-start | bytes 1572868
  206.6 1.9 copy-start.4
  400.6 13.5 %copy-start.2 = (f32[2,128,2048]{2,1,0:T(8,128)S(1)}, f32[2,128,2048]{2,1,0:T(8,128)}, u32[]{:S(2)}) copy-start(f32[2,128,2048]{2,1,0:T(8,128)} %get-tuple-element.43) | copy-start | bytes 6291460
  414.6 1.0 copy-start.3
  415.6 1.7 copy-start.10
  415.6 1.8 copy-start.6
  415.6 1.8 copy-start.7
  415.6 1.8 copy-start.8
  415.6 1.8 copy-start.9

commit v7 on v6

--- a/solution.py
+++ b/solution.py
@@ -654,7 +654,6 @@
         for src in range(at.depth):
             here = self.full.at[1 - at.x, src]
             remote(here, here, self.sems.at[2, src], self.sems.at[4, src], at.to_x).wait_recv()
-        self.local().wait()
 
     def sent(self):
         at = self.at
@@ -713,7 +712,7 @@
 def gather_kernel(
     x_ref, g_ref, w_ref, o_ref, tile_ref,
     x_full, g_full, w_full, o_full, tiles, hidden, out_mine, proj, d_joined,
-    x_block, hid, w_near, p_block, g_near, o_near, t_near, small,
+    x_block, hid, w_near, p_all, g_near, o_near, t_near, small,
     x_sems, g_sems, w_sems, w_fan_sems, o_sems, o_fan_sems, t_sems, t_fan_sems, local_sems,
     x_in_sems, hid_sems, w_in_sems, p_sems, g_in_sems, o_in_sems,
     *, n_seq, late, lead,
@@ -794,8 +793,8 @@
     def w_in(p, k):
         return pltpu.make_async_copy(w_full.at[p], w_near.at[p], w_in_sems.at[k])
 
-    def g_in():
-        return pltpu.make_async_copy(g_full, g_near, g_in_sems.at[0])
+    def g_in(col):
+        return pltpu.make_async_copy(g_full.at[col], g_near.at[col], g_in_sems.at[col])
 
     def o_in(k):
         last = at.s == n_seq - 1
@@ -811,33 +810,41 @@
         ][k]
         return pltpu.make_async_copy(src, o_near.at[pl.ds(dst, count)], o_in_sems.at[k])
 
-    step_rows = p_block.shape[1]
+    step_rows = 2 * hid.shape[2]
     steps = hid.shape[0] * depth * hid.shape[2] // step_rows
     per_block = step_rows // hid.shape[2]
 
     def p_out(k):
-        return pltpu.make_async_copy(
-            p_block.at[lax.rem(k, 2)],
-            proj.at[pl.ds(pl.multiple_of(k * step_rows, step_rows), step_rows)],
-            p_sems.at[lax.rem(k, 2)],
-        )
-
-    def project(k):
-        @pl.when(k >= 2)
-        def _():
-            p_out(k - 2).wait()
-
+        rows = pl.ds(pl.multiple_of(k * step_rows, step_rows), step_rows)
+        return pltpu.make_async_copy(p_all.at[rows], proj.at[rows], p_sems.at[k])
+
+    feats = width // w_near.shape[0]
+
+    def project(k, p_one, p_two, last):
         rows = per_block * k
-        left = hid[rows // depth, pl.ds(lax.rem(rows, depth), per_block)]
-        left = left.reshape(step_rows, width)
-        columns = p_block.shape[2]
+        at_rows = pl.ds(pl.multiple_of(k * step_rows, step_rows), step_rows)
+        left = [
+            hid[
+                rows // depth, pl.ds(lax.rem(rows, depth), per_block), :,
+                pl.ds(pl.multiple_of(p * feats, feats), feats),
+            ].reshape(step_rows, feats)
+            for p in (p_one, p_two)
+        ]
+        columns = p_all.shape[1]
         for n in range(0, columns, 512):
             some = min(512, columns - n)
-            right = w_near[:, :, :, n : n + some].reshape(width, some)
-            p_block[lax.rem(k, 2), :, n : n + some] = jnp.dot(
-                left, right, preferred_element_type=f32
+            total = sum(
+                jnp.dot(
+                    part, w_near[p, :, :, n : n + some].reshape(feats, some),
+                    preferred_element_type=f32,
+                )
+                for part, p in zip(left, (p_one, p_two))
             )
-        p_out(k).start()
+            if last:
+                total = total + p_all[at_rows, n : n + some]
+            p_all[at_rows, n : n + some] = total
+        if last:
+            p_out(k).start()
 
     def join_back(k):
         rows = per_block * k
@@ -908,6 +915,8 @@
     norm_block(n_seq - 1)
     w_local.wait()
     w_in(at.p, 0).start()
+    loop(0, n_seq, lambda k: w_fan.from_core(k).wait_recv())
+    w_in(at.p_c, 2).start()
     def w_pass(hop):
         src = at.seq(-hop)
         w_fan.from_y(src).wait_recv()
@@ -924,15 +933,15 @@
                 o_fan.y(1).start()
                 o_fan.core(1).start()
 
+            w_in(at.p, 0).wait()
+            w_in(at.p_c, 2).wait()
+        if hop == 2:
+            loop(0, steps, lambda k: project(k, at.p, at.p_c, False))
+
     loop((depth - 1) * 3, n_seq, w_pass)
     w_in(at.p_y, 1).start()
 
-    def w_last(k):
-        w_fan.from_core(k).wait_recv()
-        w_fan.from_diagonal(k).wait_recv()
-
-    loop(0, n_seq, w_last)
-    w_in(at.p_c, 2).start()
+    loop(0, n_seq, lambda k: w_fan.from_diagonal(k).wait_recv())
     w_in(at.p_d, 3).start()
     o_fan.from_y(0).wait_recv()
     o_fan.pass_on(0).start()
@@ -942,9 +951,9 @@
         o_fan.from_y(1).wait_recv()
         o_fan.pass_on(1).start()
 
-    for k, p in enumerate((at.p, at.p_y, at.p_c, at.p_d)):
-        w_in(p, k).wait()
-    loop(0, steps, project)
+    w_in(at.p_y, 1).wait()
+    w_in(at.p_d, 3).wait()
+    loop(0, steps, lambda k: project(k, at.p_y, at.p_d, True))
 
     o_local.wait()
     o_fan.from_core(0).wait_recv()
@@ -975,13 +984,17 @@
         o_in(k).wait()
     o_out = pltpu.make_async_copy(o_near, out_mine, o_in_sems.at[6])
     o_out.start()
-    g_go.arrive()
-    g_in().start()
-    g_in().wait()
-    loop(0, steps, join_back)
+    g_go.local().wait()
+    half = steps // 2
+    for col in (at.x, 1 - at.x):
+        if col is not at.x:
+            g_go.arrive()
+        g_in(col).start()
+        g_in(col).wait()
+        loop(0, half, lambda k: join_back(col * half + k))
 
     o_out.wait()
-    loop(steps - 2, steps, lambda k: p_out(k).wait())
+    loop(0, steps, lambda k: p_out(k).wait())
     loop(0, n_seq, lambda i: hid_out(i).wait())
     x_go.sent()
     g_go.sent()
@@ -1044,14 +1057,14 @@
             pltpu.VMEM(x.shape, bf16),
             pltpu.VMEM((2, depth, block, width), bf16),
             pltpu.VMEM((n_dp,) + w.shape, bf16),
-            pltpu.VMEM((2, 2 * block, columns), f32),
+            pltpu.VMEM((tokens, columns), f32),
             pltpu.VMEM((2, depth) + g.shape, bf16),
             pltpu.VMEM((mine, width), bf16),
             pltpu.VMEM((n_dp, n_seq) + tile.shape, f32),
             pltpu.VMEM((8, width), f32),
             dma((6, depth)), dma((6, depth)), dma((2, n_seq)), dma((6, n_seq)),
             dma((2,)), dma((6, 2)), dma((2, n_seq)), dma((6, 1)), dma((4,)),
-            dma((1,)), dma((n_seq,)), dma((4,)), dma((2,)), dma((1,)), dma((7,)),
+            dma((1,)), dma((n_seq,)), dma((4,)), dma((tokens // (2 * block),)), dma((2,)), dma((7,)),
         ],
         compiler_params=pltpu.CompilerParams(
             collective_id=0, has_side_effects=True, vmem_limit_bytes=56 * 2**20
@@ -1073,7 +1086,7 @@
 
 
 def reduce_kernel(
-    d_ref, in_ref, d_proj_ref, joined_ref, hidden_ref, g_ref, w_ref, o_ref,
+    in_ref, d_proj_ref, joined_ref, hidden_ref, g_ref, w_ref, o_ref,
     normed_ref, small_ref,
     sums, in_sum, out_sum, out_prev, small_sum,
     own_parts, x_got, z_got, in_own, in_core, in_y, out_own, out_core, out_y,
@@ -1085,7 +1098,6 @@
 ):
     at = Place(n_seq)
     depth = at.depth
-    parts = (d_ref, b_ref)
     main = out_own.shape[1] - late
     body, extra = pl.ds(0, main), pl.ds(main, late)
     y, c, z, x, s = at.y, at.c, at.z, at.x, at.s
@@ -1138,11 +1150,14 @@
         loop(0, count, one)
 
     def work(i):
-        if i == 0:
+        if i == 5:
+            for k in range(depth):
+                to_across(0, k).wait_send()
+        if i in (0, 7):
             some = w_near.shape[1]
-            left = flat(d_near[x])
+            left = flat(d_near[x if i == 0 else 1 - x])
             streamed(
-                own_parts.at[0], w_load, width // some, some,
+                own_parts.at[0] if i == 0 else b_ref, w_load, width // some, some,
                 lambda k: dot(left, w_near[k], (((1,), (1,)), ((), ()))),
             )
         elif i in (1, 5):
@@ -1201,7 +1216,7 @@
 
     def to_across(kind, k):
         return remote(
-            parts[kind].at[k], x_got.at[kind, k],
+            b_ref.at[k], x_got.at[kind, k],
             x_sems.at[0, kind, k], x_sems.at[1, kind, k], at.to_x,
         )
 
@@ -1423,8 +1438,9 @@
 
     def core_step(i):
         if i == 0:
+            loads[0].start()
             loop(0, n_seq, lambda hop: in_to_core(1 - y, at.seq(hop)).start())
-            for load in loads:
+            for load in loads[1:]:
                 load.start()
         elif i == 1:
             loop(0, n_seq, lambda hop: in_to_core(y, at.seq(hop)).start())
@@ -1432,9 +1448,11 @@
             out_to_core(1 - y).start()
             out_to_core(y).start()
             extra_to_core.start()
+        elif i == 3:
+            for load in loads[1:]:
+                load.wait()
         else:
-            for load in loads:
-                load.wait()
+            loads[0].wait()
 
     at.meet()
     for what, i in steps:
@@ -1490,7 +1508,8 @@
 
     for kind in range(2):
         for k in range(depth):
-            to_across(kind, k).wait_send()
+            if kind == 1:
+                to_across(kind, k).wait_send()
 
             @pl.when(z < k)
             def _():
@@ -1502,11 +1521,10 @@
 
 
 def reduce_all(
-    plan, n_dp, n_seq, late, first_act, keep, sent, d_proj, joined, hidden, g, w, o, normed, small
+    plan, n_dp, n_seq, late, first_act, keep, in_sent, d_proj, joined, hidden, g, w, o, normed, small
 ):
     depth = n_seq // 2
-    d_sent, in_sent = sent
-    block = d_sent.shape[1:]
+    block = (g.shape[2], g.shape[3])
     in_block = in_sent.shape[2:]
     width = block[1]
     main = joined.shape[-1] // n_dp
@@ -1518,7 +1536,7 @@
         functools.partial(
             reduce_kernel, n_seq=n_seq, late=late, first_act=first_act, keep=keep, plan=plan
         ),
-        in_specs=[rest] * 8 + [near, near],
+        in_specs=[rest] * 7 + [near, near],
         out_specs=[near, rest, near, rest, near],
         out_shape=[
             jax.ShapeDtypeStruct((2,) + block, f32),
@@ -1556,7 +1574,7 @@
             collective_id=1, has_side_effects=True, vmem_limit_bytes=60 * 2**20
         ),
         name="reduce_all",
-    )(*sent, d_proj, joined, hidden, g, w, o, normed, small)
+    )(in_sent, d_proj, joined, hidden, g, w, o, normed, small)
 
 def shares(n_seq, width, ffn, att, act):
     stretches, at = [], 0
@@ -1699,10 +1717,7 @@
     )
 
     blocks = lambda v: v.reshape(2, n_seq // 2, rows * own_tokens, v.shape[-1])
-    x, c = s % 2, p % 2
-    across = lambda v: lax.dynamic_index_in_dim(blocks(v), 1 - x, 0, keepdims=False)
-    d_sent = jnp.einsum("ztk,fk->ztf", across(d_proj), in_low, preferred_element_type=f32)
-
+    c = p % 2
     def to_core(v):
         some = v.shape[1] // n_dp
         firsts = [(2 * y_to + 1 - c) * some for y_to in range(2)]
@@ -1714,10 +1729,10 @@
     in_sent = over_tokens(jnp.concatenate(to_core(hidden), axis=1), d_proj).reshape(2, n_seq, in_rows, -1)
     normed, inv_std = normalise(tokens.reshape(rows * own_tokens, width))
     small_part = lax.dynamic_update_slice(jnp.zeros((8, width), f32), bias_part[:3], (2, s * att))
-    plan = ((1, 1), ((0, 0), (0, 1), (0, 2), (0, 3), (1, 0), (1, 1), (1, 3), (7, 2), (2, 0), (2, 1), (2, 2), (2, 3), (2, 4), (2, 5), (2, 6), (2, 7), (7, 4), (7, 6), (1, 2), (7, 0), (4, 0), (7, 3), (3, 0), (3, 1), (6, 0), (4, 1), (7, 5), (0, 4), (0, 5), (0, 6), (0, 7), (3, 2), (3, 3), (4, 2), (3, 4), (3, 5), (7, 1), (4, 3), (3, 6), (3, 7), (5, 0), (4, 4), (5, 1), (4, 5), (5, 2), (6, 1), (4, 6), (4, 7), (5, 3)))
+    plan = ((1, 1), ((1, 0), (1, 4), (7, 7), (0, 0), (0, 1), (0, 2), (0, 3), (1, 1), (1, 3), (7, 2), (2, 0), (2, 1), (2, 2), (2, 3), (2, 4), (2, 5), (2, 6), (2, 7), (7, 4), (7, 6), (1, 2), (7, 0), (4, 0), (7, 3), (3, 0), (3, 1), (6, 0), (4, 1), (3, 2), (3, 3), (4, 2), (7, 5), (0, 4), (0, 5), (0, 6), (0, 7), (3, 4), (3, 5), (7, 1), (4, 3), (3, 6), (3, 7), (5, 0), (4, 4), (5, 1), (4, 5), (5, 2), (6, 1), (4, 6), (4, 7), (5, 3)))
     sums, in_sum, out_sum, from_prev, small_sum = reduce_all(
         plan, n_dp, n_seq, late, act[0], keep,
-        (d_sent.astype(bf16), in_sent),
+        in_sent,
         blocks(d_proj), blocks(joined), blocks(hidden), blocks(g_full), in_low, out_mine,
         normed, small_part,
     )

time: 423 us -> 415 us (0.981)
  matrix products: 18.4 us -> 9.29 us
    dot_general x1 -> x0, matrix products: 9.29 us -> none  [split_heads(): jnp.einsum('ztk,fk->ztf', across(d_proj), in_low, preferred_element_type=...]
where the time goes in v7:
time: 415 us; the launch traced here: 407 us
  Pallas kernels  372 us (90%)
  other arithmetic  16.8 us (4%)
  matrix products  9.29 us (2%)
  local copies, waits for them, and re-layouts  8.49 us (2%)
    pallas_call x1, Pallas kernels, reduce_all(): pl.pallas_call(functools.partial(reduce_kernel, n_seq=n_seq, late=late, f...  185 us
    pallas_call x1, Pallas kernels, gather_all(): pl.pallas_call(functools.partial(gather_kernel, n_seq=n_seq, late=late, l...  144 us
    pallas_call x1, Pallas kernels, middle(): pl.pallas_call(functools.partial(middle_kernel, head_size=head_size, half...  24.9 us
    pallas_call x1, Pallas kernels, update_in(): pl.pallas_call(functools.partial(update_kernel, stretches=stretches, rate...  13.5 us
    dot_general x1, matrix products, split_heads(): lax.dot_general(a, b, (((0,), (0,)), ((), ())), preferred_element_type=f32)  9.29 us

profile of v7, /device:TPU:11, one launch (start us, length us, event | category | flops | bytes accessed | tf_op | source)
XLA Modules:
  0.0 407.5 jit_solution(14774299529142496227)
XLA Ops:
  0.7 0.7 convert_bitcast_fusion
  1.4 0.1 pad_select_fusion
  1.4 0.7 add_convert_fusion.1
  2.1 0.6 select_maximum_fusion.tile_ref
  2.7 0.0 copy-start.1
  2.7 4.7 %share_out.1.w_ref = bf16[8,64,2176]{2,1,0:T(8,128)(2,1)} custom-call(f32[64,17408]{1,0:T(8,128)} %w_ref.3), custom_call_target="tpu_custom_call" | custom-call | tf_op jit(solution)/shard_map/share_out/pallas_call | solution.py:1602
  7.5 0.0 copy-done.1
  7.5 1.1 convert_element_type.39.o_ref
  8.6 144.3 %gather_all.1 = (bf16[2,4,2,64,2048]{4,3,2,1,0:T(8,128)(2,1)}, bf16[2,4,2,64,2048]{4,3,2,1,0:T(8,128)(2,1)}, bf16[4,8,64,2176]{3,2,1,0:T(8,128)(2,1)}, bf16[4,36...) custom-call(bf16[2,64,2048]{2,1,0:T(8,128)(2,1)} %x_ref.1, ...), custom_call_target="tpu_custom_call" | custom-call | tf_op jit(solution)/shard_map/gather_all/pallas_call | solution.py:1041
  152.9 0.8 dynamic-slice_bitcast_fusion
  153.7 0.1 mul.181
  153.8 0.2 fusion.10
  154.0 0.2 fusion.9
  154.2 0.2 fusion.8
  154.5 0.2 fusion.11
  154.7 0.2 fusion.13
  155.0 0.0 copy-start.5
  155.0 1.3 pad_maximum_fusion.rope_ref
  156.3 1.3 broadcast_in_dim_reshape.9.seg_q_ref
  157.5 0.7 broadcast_in_dim_reshape.8.seg_k_ref
  158.2 0.0 copy-done.5
  158.3 0.6 copy.45
  158.9 24.9 %middle.1 = (bf16[2,4,2,64,1024]{4,3,2,1,0:T(8,128)(2,1)}, bf16[2,4,2,64,2176]{4,3,2,1,0:T(8,128)(2,1)}, f32[8,256]{1,0:T(8,128)}) custom-call(f32[2,4,2,64,2176]{4,3,2,1,0:T(8,128)} %bitcast.49, f32[2,4,2,64,2176]{4,3,2,1,0:T(8,128)} %bitcast.50, f32[2,4,2,64,2176]{4,3,2,1,0:T(8,128)} %bitcast.51, f32[1,768]{1,0:T(1,128)} %bitcast.72, f32[1,768]{1,0:T(1,128)} %bitcast.73, ...), custom_call_target="tpu_custom_call" | custom-call | tf_op jit(solution)/shard_map/middle/pallas_call | solution.py:514
  183.8 1.7 constant_dynamic-slice_fusion.2
  185.5 0.0 copy-start.11
  185.5 0.0 copy-start
  185.5 9.3 %convolution_convert_fusion = bf16[1024,2176]{1,0:T(8,128)(2,1)} fusion(bf16[1024,2176]{1,0:T(8,128)(2,1)} %bitcast.57, bf16[1024,512]{1,0:T(8,128)(2,1)S(1)} %get-tuple-element.63, bf16[1024,512]{1,0:T(8,128)(2,1)S(1)} %get-tuple-element.62), kind=kOutput, calls=%fused_computation | convolution fusion | flops 4569825280 | bytes 11010048 | tf_op jit(solution)/shard_map/dot_general | solution.py:1726
  194.8 0.0 copy-done.11
  194.8 0.4 dynamic_update_slice.3.small_ref
  195.2 0.0 copy-start.4
  195.2 0.0 copy-done
  195.3 0.2 convert_reduce_fusion
  195.4 0.3 multiply_reduce_fusion.1
  195.7 0.1 rsqrt.13
  195.8 0.1 div.56
  195.9 1.3 fusion.4.normed_ref
  197.2 0.0 copy-done.4
  197.2 184.6 %reduce_all.1 = (f32[2,128,2048]{2,1,0:T(8,128)}, bf16[8,64,2176]{2,1,0:T(8,128)(2,1)}, bf16[384,2048]{1,0:T(8,128)(2,1)}, bf16[128,2048]{1,0:T(8,128)(2,1)}, f32[8,128]{1,0:T(8,128)}) custom-call(bf16[2,8,64,2176]{3,2,1,0:T(8,128)(2,1)} %bitcast.59, bf16[2,4,128,2176]{3,2,1,0:T(8,128)(2,1)} %bitcast.58, bf16[2,4,128,1024]{3,2,1,0:T(8,128)(2,1)} %bitcast.63, ...), custom_call_target="tpu_custom_call" | custom-call | tf_op jit(solution)/shard_map/reduce_all/pallas_call | solution.py:1535
  381.8 1.3 slice.50
  383.0 6.9 %multiply_add_fusion = (f32[240,2048]{1,0:T(8,128)}, f32[240,2048]{1,0:T(8,128)}, f32[240,2048]{1,0:T(8,128)}, f32[240,2048]{1,0:T(8,128)}) fusion(f32[240,2048]{1,0:T(8,128)} %param.27, f32[240,2048]{1,0:T(8,128)S(1)} %copy-done.1, f32[240,2048]{1,0:T(8,128)} %param.25, f32[240,2048]{1,0:T(8,128)} %param.26, s32[]{:T(128)S(6)} %select_n.58, ...), kind=kLoop, calls=%fused_computation.6 | loop fusion | flops 11304960 | bytes 17235972 | tf_op jit(solution)/shard_map/add | solution.py:81
  390.0 0.0 copy-start.2
  390.0 13.5 %update_in.1 = (f32[64,17408]{1,0:T(8,128)}, f32[64,17408]{1,0:T(8,128)}, f32[64,17408]{1,0:T(8,128)}, f32[64,17408]{1,0:T(8,128)}) custom-call(bf16[8,64,2176]{2,1,0:T(8,128)(2,1)} %get-tuple-element.44.sum_ref, f32[64,17408]{1,0:T(8,128)} %w_ref.3, f32[64,17408]{1,0:T(8,128)} %m_ref.1, f32[64,17408]{1,0:T(8,128)} %v_ref.1, f32[64,17408]{1,0:T(8,128)} %a_ref.1), custom_call_target="tpu_custom_call" | custom-call | tf_op jit(solution)/shard_map/update_in/pallas_call | solution.py:1633
  403.5 0.0 copy-done.2
  403.5 0.4 fusion.5
  403.8 0.1 div.59
  403.9 0.1 div.61
  404.0 0.0 copy-start.3
  404.0 0.1 fusion.22
  404.2 0.9 copy-done.3
  405.1 0.0 copy-start.10
  405.1 0.0 copy-start.6
  405.1 0.0 copy-start.7
  405.1 0.0 copy-start.8
  405.1 0.0 copy-start.9
  405.1 1.7 multiply_add_fusion.1
  406.8 0.0 copy-done.10
  406.8 0.1 constant_dynamic-slice_fusion
  406.9 0.0 copy-done.6
  406.9 0.0 copy-done.7
  406.9 0.0 copy-done.8
  406.9 0.0 copy-done.9
  406.9 0.6 multiply_add_fusion.2
  (25 shorter events, 0.2 us)
Async XLA Ops:
  2.7 4.7 %copy-start.1 = (f32[240,2048]{1,0:T(8,128)S(1)}, f32[240,2048]{1,0:T(8,128)}, u32[]{:S(2)}) copy-start(f32[240,2048]{1,0:T(8,128)} %param.24) | copy-start | bytes 5898244
  155.0 3.2 copy-start.5
  185.5 9.3 %copy-start.11 = (f32[8,256]{1,0:T(8,128)S(1)}, f32[8,256]{1,0:T(8,128)}, u32[]{:S(2)}) copy-start(f32[8,256]{1,0:T(8,128)} %get-tuple-element.42) | copy-start | bytes 24580
  185.5 9.8 %copy-start = (bf16[2,64,2048]{2,1,0:T(8,128)(2,1)S(1)}, bf16[2,64,2048]{2,1,0:T(8,128)(2,1)}, u32[]{:S(2)}) copy-start(bf16[2,64,2048]{2,1,0:T(8,128)(2,1)} %x_ref.1) | copy-start | bytes 1572868
  195.2 1.9 copy-start.4
  390.0 13.5 %copy-start.2 = (f32[2,128,2048]{2,1,0:T(8,128)S(1)}, f32[2,128,2048]{2,1,0:T(8,128)}, u32[]{:S(2)}) copy-start(f32[2,128,2048]{2,1,0:T(8,128)} %get-tuple-element.43) | copy-start | bytes 6291460
  404.0 1.0 copy-start.3
  405.1 1.7 copy-start.10
  405.1 1.8 copy-start.6
  405.1 1.8 copy-start.7
  405.1 1.8 copy-start.8
  405.1 1.8 copy-start.9

commit v8 on v7

--- a/solution.py
+++ b/solution.py
@@ -1729,7 +1729,7 @@
     in_sent = over_tokens(jnp.concatenate(to_core(hidden), axis=1), d_proj).reshape(2, n_seq, in_rows, -1)
     normed, inv_std = normalise(tokens.reshape(rows * own_tokens, width))
     small_part = lax.dynamic_update_slice(jnp.zeros((8, width), f32), bias_part[:3], (2, s * att))
-    plan = ((1, 1), ((1, 0), (1, 4), (7, 7), (0, 0), (0, 1), (0, 2), (0, 3), (1, 1), (1, 3), (7, 2), (2, 0), (2, 1), (2, 2), (2, 3), (2, 4), (2, 5), (2, 6), (2, 7), (7, 4), (7, 6), (1, 2), (7, 0), (4, 0), (7, 3), (3, 0), (3, 1), (6, 0), (4, 1), (3, 2), (3, 3), (4, 2), (7, 5), (0, 4), (0, 5), (0, 6), (0, 7), (3, 4), (3, 5), (7, 1), (4, 3), (3, 6), (3, 7), (5, 0), (4, 4), (5, 1), (4, 5), (5, 2), (6, 1), (4, 6), (4, 7), (5, 3)))
+    plan = ((1, 1), ((1, 0), (1, 4), (7, 7), (0, 0), (0, 1), (0, 2), (0, 3), (1, 1), (1, 3), (7, 2), (2, 0), (2, 1), (2, 2), (2, 3), (2, 4), (2, 5), (2, 6), (2, 7), (7, 4), (7, 6), (1, 2), (7, 0), (4, 0), (7, 3), (3, 0), (3, 1), (3, 2), (6, 0), (4, 1), (3, 3), (3, 4), (4, 2), (7, 5), (0, 4), (0, 5), (0, 6), (0, 7), (3, 5), (3, 6), (7, 1), (4, 3), (3, 7), (5, 0), (4, 4), (5, 1), (4, 5), (5, 2), (6, 1), (4, 6), (4, 7), (5, 3)))
     sums, in_sum, out_sum, from_prev, small_sum = reduce_all(
         plan, n_dp, n_seq, late, act[0], keep,
         in_sent,

time: 415 us -> 411 us (level)
  no operation moved by 1% of the time
where the time goes in v8:
time: 411 us; the launch traced here: 407 us
  Pallas kernels  372 us (91%)
  other arithmetic  16.8 us (4%)
  matrix products  9.29 us (2%)
  local copies, waits for them, and re-layouts  8.49 us (2%)
    pallas_call x1, Pallas kernels, reduce_all(): pl.pallas_call(functools.partial(reduce_kernel, n_seq=n_seq, late=late, f...  184 us
    pallas_call x1, Pallas kernels, gather_all(): pl.pallas_call(functools.partial(gather_kernel, n_seq=n_seq, late=late, l...  144 us
    pallas_call x1, Pallas kernels, middle(): pl.pallas_call(functools.partial(middle_kernel, head_size=head_size, half...  24.9 us
    pallas_call x1, Pallas kernels, update_in(): pl.pallas_call(functools.partial(update_kernel, stretches=stretches, rate...  13.5 us
    dot_general x1, matrix products, split_heads(): lax.dot_general(a, b, (((0,), (0,)), ((), ())), preferred_element_type=f32)  9.29 us

profile of v8, /device:TPU:11, one launch (start us, length us, event | category | flops | bytes accessed | tf_op | source)
XLA Modules:
  0.0 407.3 jit_solution(2154299911141156059)
XLA Ops:
  0.7 0.7 convert_bitcast_fusion
  1.4 0.1 pad_select_fusion
  1.4 0.7 add_convert_fusion.1
  2.1 0.6 select_maximum_fusion.tile_ref
  2.7 0.0 copy-start.1
  2.7 4.7 %share_out.1.w_ref = bf16[8,64,2176]{2,1,0:T(8,128)(2,1)} custom-call(f32[64,17408]{1,0:T(8,128)} %w_ref.3), custom_call_target="tpu_custom_call" | custom-call | tf_op jit(solution)/shard_map/share_out/pallas_call | solution.py:1602
  7.5 0.0 copy-done.1
  7.5 1.1 convert_element_type.39.o_ref
  8.6 144.3 %gather_all.1 = (bf16[2,4,2,64,2048]{4,3,2,1,0:T(8,128)(2,1)}, bf16[2,4,2,64,2048]{4,3,2,1,0:T(8,128)(2,1)}, bf16[4,8,64,2176]{3,2,1,0:T(8,128)(2,1)}, bf16[4,36...) custom-call(bf16[2,64,2048]{2,1,0:T(8,128)(2,1)} %x_ref.1, ...), custom_call_target="tpu_custom_call" | custom-call | tf_op jit(solution)/shard_map/gather_all/pallas_call | solution.py:1041
  152.9 0.8 dynamic-slice_bitcast_fusion
  153.7 0.1 mul.181
  153.8 0.2 fusion.10
  154.0 0.2 fusion.9
  154.2 0.2 fusion.8
  154.5 0.2 fusion.11
  154.7 0.2 fusion.13
  155.0 0.0 copy-start.5
  155.0 1.3 pad_maximum_fusion.rope_ref
  156.3 1.3 broadcast_in_dim_reshape.9.seg_q_ref
  157.5 0.7 broadcast_in_dim_reshape.8.seg_k_ref
  158.2 0.0 copy-done.5
  158.3 0.6 copy.45
  158.9 24.9 %middle.1 = (bf16[2,4,2,64,1024]{4,3,2,1,0:T(8,128)(2,1)}, bf16[2,4,2,64,2176]{4,3,2,1,0:T(8,128)(2,1)}, f32[8,256]{1,0:T(8,128)}) custom-call(f32[2,4,2,64,2176]{4,3,2,1,0:T(8,128)} %bitcast.49, f32[2,4,2,64,2176]{4,3,2,1,0:T(8,128)} %bitcast.50, f32[2,4,2,64,2176]{4,3,2,1,0:T(8,128)} %bitcast.51, f32[1,768]{1,0:T(1,128)} %bitcast.72, f32[1,768]{1,0:T(1,128)} %bitcast.73, ...), custom_call_target="tpu_custom_call" | custom-call | tf_op jit(solution)/shard_map/middle/pallas_call | solution.py:514
  183.8 1.7 constant_dynamic-slice_fusion.2
  185.5 0.0 copy-start.11
  185.5 0.0 copy-start
  185.5 9.3 %convolution_convert_fusion = bf16[1024,2176]{1,0:T(8,128)(2,1)} fusion(bf16[1024,2176]{1,0:T(8,128)(2,1)} %bitcast.57, bf16[1024,512]{1,0:T(8,128)(2,1)S(1)} %get-tuple-element.63, bf16[1024,512]{1,0:T(8,128)(2,1)S(1)} %get-tuple-element.62), kind=kOutput, calls=%fused_computation | convolution fusion | flops 4569825280 | bytes 11010048 | tf_op jit(solution)/shard_map/dot_general | solution.py:1726
  194.8 0.0 copy-done.11
  194.8 0.4 dynamic_update_slice.3.small_ref
  195.2 0.0 copy-start.4
  195.2 0.0 copy-done
  195.3 0.2 convert_reduce_fusion
  195.4 0.3 multiply_reduce_fusion.1
  195.7 0.1 rsqrt.13
  195.8 0.1 div.56
  195.9 1.3 fusion.4.normed_ref
  197.2 0.0 copy-done.4
  197.2 184.4 %reduce_all.1 = (f32[2,128,2048]{2,1,0:T(8,128)}, bf16[8,64,2176]{2,1,0:T(8,128)(2,1)}, bf16[384,2048]{1,0:T(8,128)(2,1)}, bf16[128,2048]{1,0:T(8,128)(2,1)}, f32[8,128]{1,0:T(8,128)}) custom-call(bf16[2,8,64,2176]{3,2,1,0:T(8,128)(2,1)} %bitcast.59, bf16[2,4,128,2176]{3,2,1,0:T(8,128)(2,1)} %bitcast.58, bf16[2,4,128,1024]{3,2,1,0:T(8,128)(2,1)} %bitcast.63, ...), custom_call_target="tpu_custom_call" | custom-call | tf_op jit(solution)/shard_map/reduce_all/pallas_call | solution.py:1535
  381.5 1.3 slice.50
  382.8 6.9 %multiply_add_fusion = (f32[240,2048]{1,0:T(8,128)}, f32[240,2048]{1,0:T(8,128)}, f32[240,2048]{1,0:T(8,128)}, f32[240,2048]{1,0:T(8,128)}) fusion(f32[240,2048]{1,0:T(8,128)} %param.27, f32[240,2048]{1,0:T(8,128)S(1)} %copy-done.1, f32[240,2048]{1,0:T(8,128)} %param.25, f32[240,2048]{1,0:T(8,128)} %param.26, s32[]{:T(128)S(6)} %select_n.58, ...), kind=kLoop, calls=%fused_computation.6 | loop fusion | flops 11304960 | bytes 17235972 | tf_op jit(solution)/shard_map/add | solution.py:81
  389.8 0.0 copy-start.2
  389.8 13.5 %update_in.1 = (f32[64,17408]{1,0:T(8,128)}, f32[64,17408]{1,0:T(8,128)}, f32[64,17408]{1,0:T(8,128)}, f32[64,17408]{1,0:T(8,128)}) custom-call(bf16[8,64,2176]{2,1,0:T(8,128)(2,1)} %get-tuple-element.44.sum_ref, f32[64,17408]{1,0:T(8,128)} %w_ref.3, f32[64,17408]{1,0:T(8,128)} %m_ref.1, f32[64,17408]{1,0:T(8,128)} %v_ref.1, f32[64,17408]{1,0:T(8,128)} %a_ref.1), custom_call_target="tpu_custom_call" | custom-call | tf_op jit(solution)/shard_map/update_in/pallas_call | solution.py:1633
  403.3 0.0 copy-done.2
  403.3 0.4 fusion.5
  403.6 0.1 div.59
  403.7 0.1 div.61
  403.8 0.0 copy-start.3
  403.8 0.1 fusion.22
  404.0 0.9 copy-done.3
  404.9 0.0 copy-start.10
  404.9 0.0 copy-start.6
  404.9 0.0 copy-start.7
  404.9 0.0 copy-start.8
  404.9 0.0 copy-start.9
  404.9 1.7 multiply_add_fusion.1
  406.6 0.0 copy-done.10
  406.6 0.1 constant_dynamic-slice_fusion
  406.6 0.0 copy-done.6
  406.6 0.0 copy-done.7
  406.7 0.0 copy-done.8
  406.7 0.0 copy-done.9
  406.7 0.6 multiply_add_fusion.2
  (25 shorter events, 0.2 us)
Async XLA Ops:
  2.7 4.7 %copy-start.1 = (f32[240,2048]{1,0:T(8,128)S(1)}, f32[240,2048]{1,0:T(8,128)}, u32[]{:S(2)}) copy-start(f32[240,2048]{1,0:T(8,128)} %param.24) | copy-start | bytes 5898244
  155.0 3.2 copy-start.5
  185.5 9.3 %copy-start.11 = (f32[8,256]{1,0:T(8,128)S(1)}, f32[8,256]{1,0:T(8,128)}, u32[]{:S(2)}) copy-start(f32[8,256]{1,0:T(8,128)} %get-tuple-element.42) | copy-start | bytes 24580
  185.5 9.8 %copy-start = (bf16[2,64,2048]{2,1,0:T(8,128)(2,1)S(1)}, bf16[2,64,2048]{2,1,0:T(8,128)(2,1)}, u32[]{:S(2)}) copy-start(bf16[2,64,2048]{2,1,0:T(8,128)(2,1)} %x_ref.1) | copy-start | bytes 1572868
  195.2 1.9 copy-start.4
  389.8 13.5 %copy-start.2 = (f32[2,128,2048]{2,1,0:T(8,128)S(1)}, f32[2,128,2048]{2,1,0:T(8,128)}, u32[]{:S(2)}) copy-start(f32[2,128,2048]{2,1,0:T(8,128)} %get-tuple-element.43) | copy-start | bytes 6291460
  403.8 1.0 copy-start.3
  404.9 1.7 copy-start.10
  404.9 1.8 copy-start.6
  404.9 1.8 copy-start.7
  404.9 1.8 copy-start.8
  404.9 1.8 copy-start.9
